TPU v7x, 32 devices: a whole 2x2x4 slice. The times are simulated.
32 devices in a mesh: groups: 2 (over x), utt: 16 (over z, y, core).
Axes of the slice: x: 2, y: 2, z: 4, core: 2. Of those that a mesh axis runs over, the one named last changes fastest.
Arguments:
- cache_kv: bfloat16 [512, 8, 3072], P(('groups', 'utt')), parts along dimension 0, may hold values from -160 to 160
- new_rows: bfloat16 [512, 4608], P(('groups', 'utt')), parts along dimension 0, may hold values from -6 to 6
- cross_queries: bfloat16 [512, 1536], P(('groups', 'utt')), parts along dimension 0, may hold values from -6 to 6
- enc_kv: bfloat16 [32, 256, 3072], P(('groups', 'utt')), parts along dimension 0, may hold values from -160 to 160
- lengths: int32 [32], P(('groups', 'utt')), parts along dimension 0, may hold values from 64 to 256, as said below
- parents: int32 [32, 16], P(('groups', 'utt')), parts along dimension 0, may hold values from 0 to 15
Outputs:
- mixed: bfloat16 [512, 1536], P(('groups', 'utt')), parts along dimension 0
There are 2 independent parts, one for each index of `groups`. A program takes and returns all parts, laid end to end along the dimension named above; each array names one. Nothing has to cross between parts.
Inputs may be any that keep to these rules, and one draw needn't show every extreme that they name: `lengths`: some utterance of each part has all 256 frames.
All inputs are finite; a program needn't handle non-finite values.
Results may differ from a plain program's by a relative error of at most 0.009.
Values may be sent and summed in bfloat16 or wider, within the bound.
No kernel may reach another device: no remote copies, remote signals or barrier semaphores. Data moves between devices by JAX's collectives and lax.ppermute only.
A program may use at most 64 MiB of HBM per device.

v0:
```python
import jax
import jax.numpy as jnp
from jax import lax
from jax.sharding import PartitionSpec as P

HD = 128


def reorder(cache_rows, parents):
    utterances, beam_width = parents.shape
    grouped = cache_rows.reshape(utterances, beam_width, cache_rows.shape[1], cache_rows.shape[2])
    picked = jax.vmap(lambda block, picks: block[picks])(grouped, parents)
    return picked.reshape(cache_rows.shape)


def attend_self(query, old_keys, old_values, new_key, new_value):
    row_count = query.shape[0]
    history = old_keys.shape[1]
    head_count = query.shape[1] // HD
    scale = HD ** (-0.5)
    query_heads = query.reshape(row_count, head_count, HD)
    key_heads = old_keys.reshape(row_count, history, head_count, HD)
    value_heads = old_values.reshape(row_count, history, head_count, HD)
    old_scores = (
        jnp.einsum("rhd,rthd->rht", query_heads, key_heads, preferred_element_type=jnp.float32)
        * scale
    )
    own_score = (
        jnp.einsum(
            "rhd,rhd->rh",
            query_heads,
            new_key.reshape(row_count, head_count, HD),
            preferred_element_type=jnp.float32,
        )
        * scale
    )
    peak = jnp.maximum(jnp.max(old_scores, axis=2), own_score)
    old_exp = jnp.exp(old_scores - peak[:, :, None])
    own_exp = jnp.exp(own_score - peak)
    total = jnp.sum(old_exp, axis=2) + own_exp
    old_weight = (old_exp / total[:, :, None]).astype(jnp.bfloat16)
    own_weight = (own_exp / total).astype(jnp.bfloat16)
    context = jnp.einsum(
        "rht,rthd->rhd", old_weight, value_heads, preferred_element_type=jnp.float32
    )
    context = context + own_weight.astype(jnp.float32)[:, :, None] * new_value.reshape(
        row_count, head_count, HD
    ).astype(jnp.float32)
    return context.reshape(row_count, head_count * HD).astype(jnp.bfloat16)


def attend_frames(queries, frames_kv, frame_counts):
    utterances = frame_counts.shape[0]
    beam_width = queries.shape[0] // utterances
    feature = queries.shape[1]
    head_count = feature // HD
    frame_total = frames_kv.shape[1]
    scale = HD ** (-0.5)
    query_heads = queries.reshape(utterances, beam_width, head_count, HD)
    key_heads = frames_kv[:, :, :feature].reshape(utterances, frame_total, head_count, HD)
    value_heads = frames_kv[:, :, feature:].reshape(utterances, frame_total, head_count, HD)
    scores = (
        jnp.einsum("ubhd,ufhd->uhbf", query_heads, key_heads, preferred_element_type=jnp.float32)
        * scale
    )
    live = (
        lax.broadcasted_iota(jnp.int32, (utterances, 1, 1, frame_total), 3)
        < frame_counts[:, None, None, None]
    )
    scores = jnp.where(live, scores, -1e30)
    peak = jnp.max(scores, axis=3, keepdims=True)
    raised = jnp.where(live, jnp.exp(scores - peak), 0.0)
    weights = (raised / jnp.sum(raised, axis=3, keepdims=True)).astype(jnp.bfloat16)
    context = jnp.einsum(
        "uhbf,ufhd->ubhd", weights, value_heads, preferred_element_type=jnp.float32
    )
    return context.reshape(utterances * beam_width, feature)


def body(cache_kv, new_rows, cross_queries, enc_kv, lengths, parents):
    feature = cross_queries.shape[1]
    cross_context = attend_frames(cross_queries, enc_kv, lengths)
    arrived, new_here = (
        lax.all_to_all(cache_kv, "utt", split_axis=0, concat_axis=0, tiled=True),
        lax.all_to_all(new_rows, "utt", split_axis=0, concat_axis=0, tiled=True),
    )
    reordered = reorder(arrived, parents)
    self_context = attend_self(
        new_here[:, :feature],
        reordered[:, :, :feature],
        reordered[:, :, feature:],
        new_here[:, feature : 2 * feature],
        new_here[:, 2 * feature :],
    )
    mixed_here = (self_context.astype(jnp.float32) + cross_context).astype(jnp.bfloat16)
    mixed = lax.all_to_all(mixed_here, "utt", split_axis=0, concat_axis=0, tiled=True)
    return mixed


def solution(mesh):
    placed = (
        P(("groups", "utt"), None, None),
        P(("groups", "utt"), None),
        P(("groups", "utt"), None),
        P(("groups", "utt"), None, None),
        P(("groups", "utt")),
        P(("groups", "utt"), None),
    )
    return jax.shard_map(
        body, mesh=mesh, in_specs=placed, out_specs=P(("groups", "utt"), None), check_vma=False
    )
```

profile of v0, /device:TPU:0, one launch (start us, length us, event | category | flops | bytes accessed | tf_op | source)
XLA Modules:
  0.0 55.9 jit_solution(18194679548267514697)
XLA Ops:
  0.0 0.5 broadcast.47
  0.5 1.6 %reduce.6 = bf16[16,4608]{1,0:T(8,128)(2,1)S(1)} reduce(bf16[16,1,4608]{2,0,1:T(8,128)(2,1)} %bitcast.68, bf16[]{:T(256)} %broadcast.47), dimensions={1}, to_apply=%copy.29.reduce_sub_computation | reduce | bytes 294914 | tf_op jit(solution)/shard_map/all_to_all | solution.py:85
  2.1 0.7 %reshape.136 = bf16[16,2,2304]{2,1,0:T(2,128)(2,1)} reshape(bf16[16,4608]{1,0:T(8,128)(2,1)S(1)} %reduce.6) | data formatting | bytes 294912
  2.8 7.4 %all-to-all-start.1 = ((bf16[16,2,2304]{2,1,0:T(2,128)(2,1)}), bf16[16,2,2304]{2,1,0:T(2,128)(2,1)S(1)}, u32[]{:S(2)}, u32[]{:S(2)}) async-start(bf16[16,2,2304]{2,1,0:T(2,128)(2,1)} %reshape.136), calls=%async_computation.1 | async-start | bytes 294912 | tf_op jit(solution)/shard_map/all_to_all | solution.py:85
  10.2 1.5 %fusion.19 = (bf16[1,256,1536]{2,1,0:T(8,128)(2,1)S(1)}, bf16[1,256,1536]{2,1,0:T(8,128)(2,1)S(1)}) fusion(bf16[1,256,3072]{2,1,0:T(8,128)(2,1)} %param.9), kind=kLoop, calls=%fused_computation.41 | loop fusion | bytes 3145728 | tf_op jit(solution)/shard_map/slice | solution.py:60
  11.7 0.3 copy.51
  12.6 0.3 copy.52
  12.9 5.5 %all-to-all-done.1 = bf16[16,2,2304]{2,1,0:T(2,128)(2,1)S(1)} async-done(((bf16[16,2,2304]{2,1,0:T(2,128)(2,1)}), bf16[16,2,2304]{2,1,0:T(2,128)(2,1)S(1)}, u32[]{:S(2)}, u32[]{:S(2)}) %all-to-all-start.1) | async-done | bytes 147488 | tf_op jit(solution)/shard_map/all_to_all | solution.py:85
  18.4 3.6 %all-to-all-start = ((bf16[16,8,3072]{2,1,0:T(8,128)(2,1)}), bf16[16,8,3072]{2,1,0:T(8,128)(2,1)S(1)}, u32[]{:S(2)}, u32[]{:S(2)}) async-start(bf16[16,8,3072]{2,1,0:T(8,128)(2,1)} %param.6), calls=%async_computation | async-start | bytes 1572864 | tf_op jit(solution)/shard_map/all_to_all | solution.py:84
  22.0 0.4 fusion.21
  22.4 0.4 convolution_bitcast_fusion
  22.9 0.1 reshape.137
  23.2 0.1 fusion.8
  23.4 0.1 copy.43
  23.5 17.2 %all-to-all-done = bf16[16,8,3072]{2,1,0:T(8,128)(2,1)S(1)} async-done(((bf16[16,8,3072]{2,1,0:T(8,128)(2,1)}), bf16[16,8,3072]{2,1,0:T(8,128)(2,1)S(1)}, u32[]{:S(2)}, u32[]{:S(2)}) %all-to-all-start) | async-done | bytes 786464 | tf_op jit(solution)/shard_map/all_to_all | solution.py:84
  40.7 0.6 %gather_fusion = bf16[16,8,3072]{2,1,0:T(8,128)(2,1)S(1)} fusion(bf16[1,16,8,3072]{3,2,1,0:T(8,128)(2,1)S(1)} %bitcast.64, s32[16]{0:T(128)S(1)} %or_bitcast_fusion), kind=kCustom, calls=%fused_computation | custom fusion | bytes 1572992 | tf_op jit(solution)/shard_map/vmap()/gather | solution.py:12
  41.3 0.3 fusion.5
  41.6 0.1 copy.39
  41.9 0.1 copy.44
  42.0 0.3 fusion.6
  42.4 0.1 fusion.10
  42.6 0.7 %reduce.7 = bf16[16,1536]{1,0:T(8,128)(2,1)S(1)} reduce(bf16[16,1,1536]{2,0,1:T(8,128)(2,1)S(1)} %add_convert_fusion, bf16[]{:T(256)} %broadcast.47), dimensions={1}, to_apply=%copy.37.reduce_sub_computation | reduce | bytes 98306 | tf_op jit(solution)/shard_map/convert_element_type | solution.py:95
  43.3 12.0 %all_to_all.26 = bf16[16,2,768]{2,1,0:T(2,128)(2,1)S(1)} all-to-all(bf16[16,2,768]{2,1,0:T(2,128)(2,1)S(1)} %reshape.138), channel_id=1, replica_groups=mesh['groups'=2,'utt'=16] {'utt'}, dimensions={0} | all-to-all | bytes 98304 | tf_op jit(solution)/shard_map/all_to_all | solution.py:96
  55.3 0.6 %copy.66 = bf16[16,1,1536]{2,0,1:T(8,128)(2,1)} copy(bf16[16,1,1536]{2,1,0:T(2,128)(2,1)S(1)} %reshape.139) | data formatting | bytes 98304
  (26 shorter events, 0.6 us)
Async XLA Ops:
  0.0 22.0 %copy-start = (bf16[16,1536]{1,0:T(8,128)(2,1)S(1)}, bf16[16,1536]{1,0:T(8,128)(2,1)}, u32[]{:S(2)}) copy-start(bf16[16,1536]{1,0:T(8,128)(2,1)} %param.8) | copy-start | bytes 147460
  2.8 15.6 %all-to-all-start.1 = ((bf16[16,2,2304]{2,1,0:T(2,128)(2,1)}), bf16[16,2,2304]{2,1,0:T(2,128)(2,1)S(1)}, u32[]{:S(2)}, u32[]{:S(2)}) async-start(bf16[16,2,2304]{2,1,0:T(2,128)(2,1)} %reshape.136), calls=%async_computation.1 | async-start | bytes 294912 | tf_op jit(solution)/shard_map/all_to_all | solution.py:85
  18.4 22.3 %all-to-all-start = ((bf16[16,8,3072]{2,1,0:T(8,128)(2,1)}), bf16[16,8,3072]{2,1,0:T(8,128)(2,1)S(1)}, u32[]{:S(2)}, u32[]{:S(2)}) async-start(bf16[16,8,3072]{2,1,0:T(8,128)(2,1)} %param.6), calls=%async_computation | async-start | bytes 1572864 | tf_op jit(solution)/shard_map/all_to_all | solution.py:84
  22.0 0.8 %copy-start.1 = (s32[1,16]{1,0:T(1,128)S(1)}, s32[1,16]{1,0:T(1,128)}, u32[]{:S(2)}) copy-start(s32[1,16]{1,0:T(1,128)} %param.11) | copy-start | bytes 196
where the time goes:
time: 56.3 us; the launch traced here: 55.9 us
  waiting for transfers between devices  22.7 us (40%)
  blocking collectives  12 us (21%)
  starting transfers between devices  11 us (20%)
  local copies, waits for them, and re-layouts  5.25 us (9%)
  other arithmetic  2.63 us (5%)
  matrix products  1.41 us (3%)
  between operations  0.92 us (2%)
    all_to_all x1, waiting for transfers between devices, body(): lax.all_to_all(cache_kv, 'utt', split_axis=0, concat_axis=0, tiled=True)  17.2 us
    all_to_all x1, blocking collectives, body(): lax.all_to_all(mixed_here, 'utt', split_axis=0, concat_axis=0, tiled=True)  12 us
    all_to_all x1, starting transfers between devices, body(): lax.all_to_all(new_rows, 'utt', split_axis=0, concat_axis=0, tiled=True)  7.39 us
    all_to_all x1, waiting for transfers between devices, body(): lax.all_to_all(new_rows, 'utt', split_axis=0, concat_axis=0, tiled=True)  5.5 us
    all_to_all x1, starting transfers between devices, body(): lax.all_to_all(cache_kv, 'utt', split_axis=0, concat_axis=0, tiled=True)  3.62 us
    unnamed x12, local copies, waits for them, and re-layouts  2.06 us
    all_to_all x1, other arithmetic, body(): lax.all_to_all(new_rows, 'utt', split_axis=0, concat_axis=0, tiled=True)  1.6 us
    slice x1, local copies, waits for them, and re-layouts, attend_frames(): frames_kv[:, :, :feature].reshape(utterances, frame_total, head_count, HD)  1.47 us
  transfers between devices with their start and end apart: 2, of which 2 were waited for; matrix products, arithmetic and copies ran while one was open for 6% of the time, Pallas kernels for 0%

commit v1 on v0

--- a/solution.py
+++ b/solution.py
@@ -1,9 +1,16 @@
+import functools
+
 import jax
 import jax.numpy as jnp
 from jax import lax
+from jax.experimental import pallas as pl
+from jax.experimental.pallas import tpu as pltpu
 from jax.sharding import PartitionSpec as P
 
 HD = 128
+LANES = 128
+PARENT_LANE = 64
+MASKED = -1e30
 
 
 def reorder(cache_rows, parents):
@@ -77,7 +84,7 @@
     return context.reshape(utterances * beam_width, feature)
 
 
-def body(cache_kv, new_rows, cross_queries, enc_kv, lengths, parents):
+def body_by_utterance(cache_kv, new_rows, cross_queries, enc_kv, lengths, parents):
     feature = cross_queries.shape[1]
     cross_context = attend_frames(cross_queries, enc_kv, lengths)
     arrived, new_here = (
@@ -95,6 +102,229 @@
     mixed_here = (self_context.astype(jnp.float32) + cross_context).astype(jnp.bfloat16)
     mixed = lax.all_to_all(mixed_here, "utt", split_axis=0, concat_axis=0, tiled=True)
     return mixed
+
+
+def column(tile, lane_index, at):
+    return jnp.sum(jnp.where(lane_index == at, tile, 0.0), axis=1, keepdims=True)
+
+
+def pack_kernel(query_ref, key_ref, parents_ref, out_ref):
+    rows, feature = query_ref.shape
+    query = query_ref[...]
+    product = query.astype(jnp.float32) * key_ref[...].astype(jnp.float32)
+    lane = lax.broadcasted_iota(jnp.int32, (rows, LANES), 1)
+    heads = feature // HD
+    extra = jnp.zeros((rows, LANES), jnp.float32)
+    for head in range(heads):
+        own = jnp.sum(product[:, head * HD : (head + 1) * HD], axis=1, keepdims=True) * HD ** (-0.5)
+        for part in range(3):
+            term = own.astype(jnp.bfloat16).astype(jnp.float32)
+            extra = jnp.where(lane == part * heads + head, term, extra)
+            own = own - term
+    extra = extra + parents_ref[...].astype(jnp.float32)
+    out_ref[:, :feature] = query
+    out_ref[:, feature:] = extra.astype(jnp.bfloat16)
+
+
+def cross_kernel(lengths_ref, query_ref, frames_ref, out_ref):
+    rows, feature = query_ref.shape
+    frames = frames_ref.shape[0]
+    live = lax.broadcasted_iota(jnp.int32, (rows, frames), 1) < lengths_ref[0]
+    for head in range(feature // HD):
+        at = slice(head * HD, (head + 1) * HD)
+        value_at = slice(feature + head * HD, feature + (head + 1) * HD)
+        scores = lax.dot_general(
+            query_ref[:, at],
+            frames_ref[:, at],
+            (((1,), (1,)), ((), ())),
+            preferred_element_type=jnp.float32,
+        ) * HD ** (-0.5)
+        scores = jnp.where(live, scores, MASKED)
+        raised = jnp.where(live, jnp.exp(scores - jnp.max(scores, axis=1, keepdims=True)), 0.0)
+        weights = (raised / jnp.sum(raised, axis=1, keepdims=True)).astype(jnp.bfloat16)
+        context = jnp.dot(weights, frames_ref[:, value_at], preferred_element_type=jnp.float32)
+        out_ref[:, at] = context.astype(jnp.bfloat16)
+
+
+def self_kernel(masks, counts, me_ref, *refs):
+    query_refs, refs = refs[:counts], refs[counts:]
+    near_ref, far_ref, cross_near_ref, cross_far_ref, send_ref, keep_ref = refs
+    me = me_ref[0]
+    blocks = len(masks)
+    keys, feature = near_ref.shape[0], near_ref.shape[1] // 2
+    heads = feature // HD
+    queries = jnp.concatenate([ref[...] for ref in query_refs], axis=0)
+    rows = queries.shape[0]
+    beams = rows // blocks
+    history = keys // beams
+    extra = queries[:, feature:].astype(jnp.float32)
+
+    utt = lax.broadcasted_iota(jnp.int32, (beams, LANES), 0)
+    lane = lax.broadcasted_iota(jnp.int32, (beams, LANES), 1)
+    table = jnp.zeros((beams, LANES), jnp.float32)
+    for at, mask in enumerate(masks):
+        lists = extra[at * beams : (at + 1) * beams]
+        owner = me ^ mask
+        table = jnp.where(utt == owner, lists, table)
+        table = jnp.where(utt == (owner ^ 1), pltpu.roll(lists, LANES - beams, 1), table)
+    chosen = jnp.concatenate(
+        [column(table, lane, PARENT_LANE + (me ^ mask)) for mask in masks], axis=0
+    ).astype(jnp.int32)
+
+    row_utt = lax.broadcasted_iota(jnp.int32, (rows, 1), 0) % beams
+    row_mark = chosen * beams + row_utt
+    key_utt = lax.broadcasted_iota(jnp.int32, (rows, keys), 1) // history
+    near_live = row_mark == me * beams + key_utt
+    far_live = row_mark == (me ^ 1) * beams + key_utt
+    near_bias = jnp.where(near_live, 0.0, MASKED)
+    far_bias = jnp.where(far_live, 0.0, MASKED)
+    row_live = (chosen >> 1) == (me >> 1)
+
+    place = lax.broadcasted_iota(jnp.int32, (rows, beams), 1)
+    row_beam = me ^ jnp.concatenate(
+        [jnp.full((beams, beams), mask, jnp.int32) for mask in masks], axis=0
+    )
+    near_pick = ((place == row_beam) & (row_utt == me)).astype(jnp.bfloat16)
+    far_pick = ((place == row_beam) & (row_utt == (me ^ 1))).astype(jnp.bfloat16)
+
+    own_all = extra + pltpu.roll(extra, LANES - heads, 1) + pltpu.roll(extra, LANES - 2 * heads, 1)
+    row_lane = lax.broadcasted_iota(jnp.int32, (rows, LANES), 1)
+    shares = jnp.zeros((rows, LANES), jnp.float32)
+    half = rows // 2
+    scale = HD ** (-0.5)
+    over_last = (((1,), (1,)), ((), ()))
+    for head in range(heads):
+        at = slice(head * HD, (head + 1) * HD)
+        value_at = slice(feature + head * HD, feature + (head + 1) * HD)
+        query = queries[:, at]
+        near = lax.dot_general(query, near_ref[:, at], over_last, preferred_element_type=jnp.float32)
+        far = lax.dot_general(query, far_ref[:, at], over_last, preferred_element_type=jnp.float32)
+        near = near * scale + near_bias
+        far = far * scale + far_bias
+        own = own_all[:, head : head + 1]
+        peak = jnp.maximum(jnp.max(jnp.maximum(near, far), axis=1, keepdims=True), own)
+        near = jnp.exp(near - peak)
+        far = jnp.exp(far - peak)
+        own = jnp.exp(own - peak)
+        share = 1.0 / (jnp.sum(near + far, axis=1, keepdims=True) + own)
+        context = jnp.dot(
+            near.astype(jnp.bfloat16), near_ref[:, value_at], preferred_element_type=jnp.float32
+        ) + jnp.dot(far.astype(jnp.bfloat16), far_ref[:, value_at], preferred_element_type=jnp.float32)
+        cross = jnp.dot(
+            near_pick, cross_near_ref[:, at], preferred_element_type=jnp.float32
+        ) + jnp.dot(far_pick, cross_far_ref[:, at], preferred_element_type=jnp.float32)
+        out = (context * share + cross).astype(jnp.bfloat16)
+        keep_ref[:, at] = out[:half]
+        send_ref[:, at] = out[half:]
+        shares = jnp.where(row_lane == head, own * share, shares)
+    shares = jnp.where(row_live, shares, 0.0).astype(jnp.bfloat16)
+    keep_ref[:, feature:] = shares[:half]
+    send_ref[:, feature:] = shares[half:]
+
+
+def finish_kernel(kept_ref, came_ref, value_ref, out_ref):
+    feature = out_ref.shape[1]
+    shares = kept_ref[:, feature:].astype(jnp.float32) + came_ref[:, feature:].astype(jnp.float32)
+    for head in range(feature // HD):
+        at = slice(head * HD, (head + 1) * HD)
+        context = kept_ref[:, at].astype(jnp.float32) + came_ref[:, at].astype(jnp.float32)
+        out = context + shares[:, head : head + 1] * value_ref[:, at].astype(jnp.float32)
+        out_ref[:, at] = out.astype(jnp.bfloat16)
+
+
+def whole(shape):
+    return pl.BlockSpec(shape, lambda: (0,) * len(shape))
+
+
+def body_by_parent(devices, cache_kv, new_rows, cross_queries, enc_kv, lengths, parents):
+    beams = parents.shape[1]
+    rows, feature = cross_queries.shape
+    history = cache_kv.shape[1]
+    width = feature + LANES
+    keys = beams * history
+    me = lax.axis_index("utt").astype(jnp.int32).reshape(1)
+    smem = pl.BlockSpec(memory_space=pltpu.SMEM)
+    params = pltpu.CompilerParams(vmem_limit_bytes=32 * 1024 * 1024)
+
+    def swap(array, bit):
+        return lax.ppermute(array, "utt", [(i, i ^ bit) for i in range(devices)])
+
+    hops = [1 << k for k in range(devices.bit_length() - 2, 0, -1)]
+
+    lists = jnp.pad(parents, ((0, 0), (PARENT_LANE, LANES - PARENT_LANE - beams)))
+    lists = lists + jnp.pad(
+        swap(parents, 1), ((0, 0), (PARENT_LANE + beams, LANES - PARENT_LANE - 2 * beams))
+    )
+    near = cache_kv.reshape(keys, 2 * feature)
+    far = swap(near, 1)
+    own = pl.pallas_call(
+        pack_kernel,
+        out_shape=jax.ShapeDtypeStruct((rows, width), jnp.bfloat16),
+        grid=(1,),
+        in_specs=[
+            pl.BlockSpec((rows, feature), lambda i: (0, 0)),
+            pl.BlockSpec((rows, feature), lambda i: (0, 1)),
+            pl.BlockSpec((1, LANES), lambda i: (0, 0)),
+        ],
+        out_specs=pl.BlockSpec((rows, width), lambda i: (0, 0)),
+        compiler_params=params,
+    )(new_rows, new_rows, lists)
+
+    cross_near = pl.pallas_call(
+        cross_kernel,
+        out_shape=jax.ShapeDtypeStruct((rows, feature), jnp.bfloat16),
+        in_specs=[smem, whole((rows, feature)), whole((enc_kv.shape[1], 2 * feature))],
+        out_specs=whole((rows, feature)),
+        compiler_params=params,
+        cost_estimate=pl.CostEstimate(
+            flops=4 * rows * enc_kv.shape[1] * feature,
+            bytes_accessed=2 * enc_kv.size,
+            transcendentals=rows * enc_kv.shape[1] * feature // HD,
+        ),
+    )(lengths, cross_queries, enc_kv.reshape(enc_kv.shape[1], 2 * feature))
+    cross_far = swap(cross_near, 1)
+
+    gathered, masks, held, held_masks = [own], [0], own, [0]
+    for bit in hops:
+        came = swap(held, bit)
+        gathered.append(came)
+        masks = masks + [mask ^ bit for mask in held_masks]
+        held_masks = masks
+        if bit != hops[-1]:
+            held = jnp.concatenate([held, came], axis=0)
+
+    half = rows * len(masks) // 2
+    part = jax.ShapeDtypeStruct((half, width), jnp.bfloat16)
+    send, keep = pl.pallas_call(
+        functools.partial(self_kernel, tuple(masks), len(gathered)),
+        out_shape=(part, part),
+        in_specs=[smem]
+        + [whole(block.shape) for block in gathered]
+        + [whole((keys, 2 * feature))] * 2
+        + [whole((rows, feature))] * 2,
+        out_specs=(whole(part.shape), whole(part.shape)),
+        compiler_params=params,
+    )(me, *gathered, near, far, cross_near, cross_far)
+
+    for bit in hops[::-1]:
+        came = swap(send, bit)
+        if bit != hops[0]:
+            half = half // 2
+            send = keep[half:] + came[half:]
+            keep = keep[:half] + came[:half]
+
+    return pl.pallas_call(
+        finish_kernel,
+        out_shape=jax.ShapeDtypeStruct((rows, feature), jnp.bfloat16),
+        grid=(1,),
+        in_specs=[
+            pl.BlockSpec((rows, width), lambda i: (0, 0)),
+            pl.BlockSpec((rows, width), lambda i: (0, 0)),
+            pl.BlockSpec((rows, feature), lambda i: (0, 2)),
+        ],
+        out_specs=pl.BlockSpec((rows, feature), lambda i: (0, 0)),
+        compiler_params=params,
+    )(keep, came, new_rows)
 
 
 def solution(mesh):
@@ -106,6 +336,23 @@
         P(("groups", "utt")),
         P(("groups", "utt"), None),
     )
+    devices = mesh.shape["utt"]
+
+    def body(cache_kv, new_rows, cross_queries, enc_kv, lengths, parents):
+        beams = parents.shape[1]
+        heads = cross_queries.shape[1] // HD
+        fits = (
+            parents.shape[0] == 1
+            and devices == beams
+            and devices >= 4
+            and devices & (devices - 1) == 0
+            and beams % 16 == 0
+            and 3 * heads <= PARENT_LANE
+            and PARENT_LANE + 2 * beams <= LANES
+        )
+        plan = functools.partial(body_by_parent, devices) if fits else body_by_utterance
+        return plan(cache_kv, new_rows, cross_queries, enc_kv, lengths, parents)
+
     return jax.shard_map(
         body, mesh=mesh, in_specs=placed, out_specs=P(("groups", "utt"), None), check_vma=False
     )

time: 56.3 us -> 48.1 us (0.85)
  blocking collectives: 12 us -> 0 us
  Pallas kernels: 0 us -> 9.46 us
  local copies, waits for them, and re-layouts: 5.25 us -> 3.12 us
  other arithmetic: 2.63 us -> 0.81 us
  matrix products: 1.41 us -> 0 us
  starting transfers between devices: 11 us -> 12.1 us
  waiting for transfers between devices: 22.7 us -> 21.7 us
    all_to_all x2 -> x0, waiting for transfers between devices: 22.7 us -> none  [the longest x1 17.2 us: body(): lax.all_to_all(cache_kv, 'utt', split_axis=0, concat_axis=0, tiled=True)]
    ppermute x0 -> x9, waiting for transfers between devices: none -> 21.7 us  [swap(): return lax.ppermute(array, 'utt', [(i, i ^ bit) for i in range(devices)])]
    ppermute x0 -> x9, starting transfers between devices: none -> 12.1 us  [swap(): return lax.ppermute(array, 'utt', [(i, i ^ bit) for i in range(devices)])]
    all_to_all x1 -> x0, blocking collectives: 12 us -> none  [body(): lax.all_to_all(mixed_here, 'utt', split_axis=0, concat_axis=0, tiled=True)]
    all_to_all x2 -> x0, starting transfers between devices: 11 us -> none  [the longest x1 7.39 us: body(): lax.all_to_all(new_rows, 'utt', split_axis=0, concat_axis=0, tiled=True)]
    pallas_call x0 -> x4, Pallas kernels: none -> 9.46 us  [the longest x1 4.7 us: body_by_parent(): pl.pallas_call(functools.partial(self_kernel, tuple(masks), len(gathered)...]
    all_to_all x1 -> x0, other arithmetic: 1.6 us -> none  [body(): lax.all_to_all(new_rows, 'utt', split_axis=0, concat_axis=0, tiled=True)]
    slice x1 -> x0, local copies, waits for them, and re-layouts: 1.47 us -> none  [attend_frames(): frames_kv[:, :, :feature].reshape(utterances, frame_total, head_count, HD)]
  transfers between devices with their start and end apart: 2 -> 9, of which waited for: 2 -> 7; matrix products, arithmetic and copies ran while one was open for 6% -> 0% of each run, Pallas kernels for 0% -> 8%
where the time goes in v1:
time: 48.1 us; the launch traced here: 47.9 us
  waiting for transfers between devices  21.7 us (45%)
  starting transfers between devices  12.1 us (25%)
  Pallas kernels  9.46 us (20%)
  local copies, waits for them, and re-layouts  3.12 us (6%)
  other arithmetic  0.81 us (2%)
  between operations  0.71 us (1%)
    ppermute x9, waiting for transfers between devices, swap(): return lax.ppermute(array, 'utt', [(i, i ^ bit) for i in range(devices)])  21.7 us
    ppermute x9, starting transfers between devices, swap(): return lax.ppermute(array, 'utt', [(i, i ^ bit) for i in range(devices)])  12.1 us
    pallas_call x1, Pallas kernels, body_by_parent(): pl.pallas_call(functools.partial(self_kernel, tuple(masks), len(gathered)...  4.7 us
    pallas_call x1, Pallas kernels, body_by_parent(): pl.pallas_call(cross_kernel, out_shape=jax.ShapeDtypeStruct((rows, featur...  3.92 us
    unnamed x10, local copies, waits for them, and re-layouts  3.12 us
  transfers between devices with their start and end apart: 9, of which 7 were waited for; matrix products, arithmetic and copies ran while one was open for 0% of the time, Pallas kernels for 8%

profile of v1, /device:TPU:0, one launch (start us, length us, event | category | flops | bytes accessed | tf_op | source)
XLA Modules:
  0.0 47.9 jit_solution(7347773946520288639)
XLA Ops:
  0.0 0.5 collective-permute-start
  0.5 1.0 %collective-permute-done = s32[1,16]{1,0:T(1,128)S(1)} collective-permute-done((s32[1,16]{1,0:T(1,128)}, s32[1,16]{1,0:T(1,128)S(1)}, u32[]{:S(2)}, u32[]{:S(2)}) %collective-permute-start) | collective-permute-done | bytes 96 | tf_op jit(solution)/shard_map/ppermute | solution.py:250
  1.4 0.7 %pad_add_fusion.parents_ref = s32[1,128]{1,0:T(1,128)S(1)} fusion(s32[1,16]{1,0:T(1,128)S(1)} %collective-permute-done, s32[1,16]{1,0:T(1,128)} %param.11), kind=kLoop, calls=%fused_computation.6 | loop fusion | flops 128 | bytes 640 | tf_op jit(solution)/shard_map/add | solution.py:255
  2.1 0.9 %copy-done.1 = bf16[16,4608]{1,0:T(8,128)(2,1)S(1)} copy-done((bf16[16,4608]{1,0:T(8,128)(2,1)S(1)}, bf16[16,4608]{1,0:T(8,128)(2,1)}, u32[]{:S(2)}) %copy-start.1) | copy-done | bytes 147480
  3.1 0.1 shard_map.64.refs_0_
  3.2 4.0 %collective-permute-start.1 = (bf16[16,1664]{1,0:T(8,128)(2,1)S(1)}, bf16[16,1664]{1,0:T(8,128)(2,1)S(1)}, u32[]{:S(2)}, u32[]{:S(2)}) collective-permute-start(bf16[16,1664]{1,0:T(8,128)(2,1)S(1)} %shard_map.64.refs_0_), channel_id=1, source_target_pairs={{0,8},{1,9},{2,10},{3,11},{4,12},{5,13},{6,14},{7,15},{8,0},{9,1},... | collective-permute-start | bytes 159752 | tf_op jit(solution)/shard_map/ppermute | solution.py:250
  7.1 0.0 collective-permute-start.4
  7.1 2.2 %collective-permute-done.1.refs_1_ = bf16[16,1664]{1,0:T(8,128)(2,1)S(1)} collective-permute-done((bf16[16,1664]{1,0:T(8,128)(2,1)S(1)}, bf16[16,1664]{1,0:T(8,128)(2,1)S(1)}, u32[]{:S(2)}, u32[]{:S(2)}) %collective-permute-start.1) | collective-permute-done | bytes 53280 | tf_op jit(solution)/shard_map/ppermute | solution.py:250
  9.4 1.9 %collective-permute-start.2 = (bf16[32,1664]{1,0:T(8,128)(2,1)S(1)}, bf16[32,1664]{1,0:T(8,128)(2,1)S(1)}, u32[]{:S(2)}, u32[]{:S(2)}) collective-permute-start(bf16[32,1664]{1,0:T(8,128)(2,1)S(1)} %pad_maximum_fusion.1), channel_id=1, source_target_pairs={{0,4},{1,5},{2,6},{3,7},{4,0},{5,1},{6,2},{7,3},{8,12},{9,13},{10,... | collective-permute-start | bytes 319496 | tf_op jit(solution)/shard_map/ppermute | solution.py:250
  11.3 2.9 %collective-permute-done.2.refs_2_ = bf16[32,1664]{1,0:T(8,128)(2,1)S(1)} collective-permute-done((bf16[32,1664]{1,0:T(8,128)(2,1)S(1)}, bf16[32,1664]{1,0:T(8,128)(2,1)S(1)}, u32[]{:S(2)}, u32[]{:S(2)}) %collective-permute-start.2) | collective-permute-done | bytes 106528 | tf_op jit(solution)/shard_map/ppermute | solution.py:250
  14.2 2.9 %collective-permute-start.3 = (bf16[64,1664]{1,0:T(8,128)(2,1)S(1)}, bf16[64,1664]{1,0:T(8,128)(2,1)S(1)}, u32[]{:S(2)}, u32[]{:S(2)}) collective-permute-start(bf16[64,1664]{1,0:T(8,128)(2,1)S(1)} %pad_maximum_fusion), channel_id=1, source_target_pairs={{0,2},{1,3},{2,0},{3,1},{4,6},{5,7},{6,4},{7,5},{8,10},{9,11},{10,... | collective-permute-start | bytes 638984 | tf_op jit(solution)/shard_map/ppermute | solution.py:250
  17.8 0.0 copy-start
  17.8 1.4 %copy-done = bf16[1,256,3072]{2,1,0:T(8,128)(2,1)S(1)} copy-done((bf16[1,256,3072]{2,1,0:T(8,128)(2,1)S(1)}, bf16[1,256,3072]{2,1,0:T(8,128)(2,1)}, u32[]{:S(2)}) %copy-start) | copy-done | bytes 1572888
  19.2 0.8 %copy-done.4 = bf16[16,1536]{1,0:T(8,128)(2,1)S(1)} copy-done((bf16[16,1536]{1,0:T(8,128)(2,1)S(1)}, bf16[16,1536]{1,0:T(8,128)(2,1)}, u32[]{:S(2)}) %copy-start.4) | copy-done | bytes 49176
  20.0 3.9 %shard_map.65.refs_6_ = bf16[16,1536]{1,0:T(8,128)(2,1)S(1)} custom-call(s32[1]{0:T(128)S(6)} %copy.7.lengths_ref, bf16[16,1536]{1,0:T(8,128)(2,1)S(1)} %copy-done.4, bf16[256,3072]{1,0:T(8,128)(2,1)S(1)} %bitcast.3), custom_call_target="tpu_custom_call" | custom-call | flops 25165824 | bytes 1572864 | tf_op jit(solution)/shard_map/pallas_call | solution.py:273
  23.9 1.3 %collective-permute-done.5.refs_7_ = bf16[16,1536]{1,0:T(8,128)(2,1)S(1)} collective-permute-done((bf16[16,1536]{1,0:T(8,128)(2,1)S(1)}, bf16[16,1536]{1,0:T(8,128)(2,1)S(1)}, u32[]{:S(2)}, u32[]{:S(2)}) %collective-permute-start.5) | collective-permute-done | bytes 49184 | tf_op jit(solution)/shard_map/ppermute | solution.py:250
  25.2 4.7 %shard_map.66 = (bf16[64,1664]{1,0:T(8,128)(2,1)S(1)}, bf16[64,1664]{1,0:T(8,128)(2,1)S(1)}) custom-call(s32[1]{0:T(128)} %bitcast.me_ref, bf16[16,1664]{1,0:T(8,128)(2,1)S(1)} %shard_map.64.refs_0_, bf16[16,1664]{1,0:T(8,128)(2,1)S(1)} %collective-permute-done.1.refs_1_, bf16[32,1664]{1,0:T(8,128)(2,1)S(1)} %collective-permute-done.2.refs_2_, ...), custom_call_target="tpu_custom_call" | custom-call | tf_op jit(solution)/shard_map/pallas_call | solution.py:298
  29.9 0.1 collective-permute-start.6
  29.9 7.3 %collective-permute-done.6 = bf16[64,1664]{1,0:T(8,128)(2,1)S(1)} collective-permute-done((bf16[64,1664]{1,0:T(8,128)(2,1)S(1)}, bf16[64,1664]{1,0:T(8,128)(2,1)S(1)}, u32[]{:S(2)}, u32[]{:S(2)}) %collective-permute-start.6) | collective-permute-done | bytes 213024 | tf_op jit(solution)/shard_map/ppermute | solution.py:250
  37.3 0.5 %collective-permute-start.7 = (bf16[32,1664]{1,0:T(8,128)(2,1)S(1)}, bf16[32,1664]{1,0:T(8,128)(2,1)S(1)}, u32[]{:S(2)}, u32[]{:S(2)}) collective-permute-start(bf16[32,1664]{1,0:T(8,128)(2,1)S(1)} %get-tuple-element.10), channel_id=1, source_target_pairs={{0,4},{1,5},{2,6},{3,7},{4,0},{5,1},{6,2},{7,3},{8,12},{9,13},{10,... | collective-permute-start | bytes 319496 | tf_op jit(solution)/shard_map/ppermute | solution.py:250
  37.8 4.2 %collective-permute-done.7 = bf16[32,1664]{1,0:T(8,128)(2,1)S(1)} collective-permute-done((bf16[32,1664]{1,0:T(8,128)(2,1)S(1)}, bf16[32,1664]{1,0:T(8,128)(2,1)S(1)}, u32[]{:S(2)}, u32[]{:S(2)}) %collective-permute-start.7) | collective-permute-done | bytes 106528 | tf_op jit(solution)/shard_map/ppermute | solution.py:250
  42.1 2.3 %collective-permute-start.8 = (bf16[16,1664]{1,0:T(8,128)(2,1)S(1)}, bf16[16,1664]{1,0:T(8,128)(2,1)S(1)}, u32[]{:S(2)}, u32[]{:S(2)}) collective-permute-start(bf16[16,1664]{1,0:T(8,128)(2,1)S(1)} %get-tuple-element.11), channel_id=1, source_target_pairs={{0,8},{1,9},{2,10},{3,11},{4,12},{5,13},{6,14},{7,15},{8,0},{9,1},... | collective-permute-start | bytes 159752 | tf_op jit(solution)/shard_map/ppermute | solution.py:250
  44.4 2.8 %collective-permute-done.8.came_ref = bf16[16,1664]{1,0:T(8,128)(2,1)S(1)} collective-permute-done((bf16[16,1664]{1,0:T(8,128)(2,1)S(1)}, bf16[16,1664]{1,0:T(8,128)(2,1)S(1)}, u32[]{:S(2)}, u32[]{:S(2)}) %collective-permute-start.8) | collective-permute-done | bytes 53280 | tf_op jit(solution)/shard_map/ppermute | solution.py:250
  47.2 0.7 %shard_map.67 = bf16[16,1536]{1,0:T(8,128)(2,1)} custom-call(bf16[16,1664]{1,0:T(8,128)(2,1)S(1)} %get-tuple-element.12.kept_ref, bf16[16,1664]{1,0:T(8,128)(2,1)S(1)} %collective-permute-done.8.came_ref, bf16[16,4608]{1,0:T(8,128)(2,1)S(1)} %copy-done.2), custom_call_target="tpu_custom_call" | custom-call | tf_op jit(solution)/shard_map/pallas_call | solution.py:316
  (13 shorter events, 0.1 us)
Async XLA Ops:
  0.0 1.4 %collective-permute-start = (s32[1,16]{1,0:T(1,128)}, s32[1,16]{1,0:T(1,128)S(1)}, u32[]{:S(2)}, u32[]{:S(2)}) collective-permute-start(s32[1,16]{1,0:T(1,128)} %param.11), channel_id=1, source_target_pairs={{0,1},{1,0},{2,3},{3,2},{4,5},{5,4},{6,7},{7,6},{8,9},{9,8},{10,11... | collective-permute-start | bytes 200 | tf_op jit(solution)/shard_map/ppermute | solution.py:250
  2.1 0.9 %copy-start.1 = (bf16[16,4608]{1,0:T(8,128)(2,1)S(1)}, bf16[16,4608]{1,0:T(8,128)(2,1)}, u32[]{:S(2)}) copy-start(bf16[16,4608]{1,0:T(8,128)(2,1)} %value_ref.1) | copy-start | bytes 442372
  3.0 22.1 %copy-start.3 = (bf16[16,8,3072]{2,1,0:T(8,128)(2,1)S(1)}, bf16[16,8,3072]{2,1,0:T(8,128)(2,1)}, u32[]{:S(2)}) copy-start(bf16[16,8,3072]{2,1,0:T(8,128)(2,1)} %param.6) | copy-start | bytes 2359300
  3.2 6.2 %collective-permute-start.1 = (bf16[16,1664]{1,0:T(8,128)(2,1)S(1)}, bf16[16,1664]{1,0:T(8,128)(2,1)S(1)}, u32[]{:S(2)}, u32[]{:S(2)}) collective-permute-start(bf16[16,1664]{1,0:T(8,128)(2,1)S(1)} %shard_map.64.refs_0_), channel_id=1, source_target_pairs={{0,8},{1,9},{2,10},{3,11},{4,12},{5,13},{6,14},{7,15},{8,0},{9,1},... | collective-permute-start | bytes 159752 | tf_op jit(solution)/shard_map/ppermute | solution.py:250
  7.1 18.0 %collective-permute-start.4 = (bf16[128,3072]{1,0:T(8,128)(2,1)}, bf16[128,3072]{1,0:T(8,128)(2,1)S(1)}, u32[]{:S(2)}, u32[]{:S(2)}) collective-permute-start(bf16[128,3072]{1,0:T(8,128)(2,1)} %bitcast.4), channel_id=1, source_target_pairs={{0,1},{1,0},{2,3},{3,2},{4,5},{5,4},{6,7},{7,6},{8,9},{9,8},{10,11... | collective-permute-start | bytes 2359304 | tf_op jit(solution)/shard_map/ppermute | solution.py:250
  9.4 4.8 %collective-permute-start.2 = (bf16[32,1664]{1,0:T(8,128)(2,1)S(1)}, bf16[32,1664]{1,0:T(8,128)(2,1)S(1)}, u32[]{:S(2)}, u32[]{:S(2)}) collective-permute-start(bf16[32,1664]{1,0:T(8,128)(2,1)S(1)} %pad_maximum_fusion.1), channel_id=1, source_target_pairs={{0,4},{1,5},{2,6},{3,7},{4,0},{5,1},{6,2},{7,3},{8,12},{9,13},{10,... | collective-permute-start | bytes 319496 | tf_op jit(solution)/shard_map/ppermute | solution.py:250
  14.2 10.9 %collective-permute-start.3 = (bf16[64,1664]{1,0:T(8,128)(2,1)S(1)}, bf16[64,1664]{1,0:T(8,128)(2,1)S(1)}, u32[]{:S(2)}, u32[]{:S(2)}) collective-permute-start(bf16[64,1664]{1,0:T(8,128)(2,1)S(1)} %pad_maximum_fusion), channel_id=1, source_target_pairs={{0,2},{1,3},{2,0},{3,1},{4,6},{5,7},{6,4},{7,5},{8,10},{9,11},{10,... | collective-permute-start | bytes 638984 | tf_op jit(solution)/shard_map/ppermute | solution.py:250
  17.8 1.4 %copy-start = (bf16[1,256,3072]{2,1,0:T(8,128)(2,1)S(1)}, bf16[1,256,3072]{2,1,0:T(8,128)(2,1)}, u32[]{:S(2)}) copy-start(bf16[1,256,3072]{2,1,0:T(8,128)(2,1)} %param.9) | copy-start | bytes 4718596
  19.2 0.8 %copy-start.4 = (bf16[16,1536]{1,0:T(8,128)(2,1)S(1)}, bf16[16,1536]{1,0:T(8,128)(2,1)}, u32[]{:S(2)}) copy-start(bf16[16,1536]{1,0:T(8,128)(2,1)} %query_ref.3) | copy-start | bytes 147460
  23.9 23.3 %copy-start.2 = (bf16[16,4608]{1,0:T(8,128)(2,1)S(1)}, bf16[16,4608]{1,0:T(8,128)(2,1)}, u32[]{:S(2)}) copy-start(bf16[16,4608]{1,0:T(8,128)(2,1)} %value_ref.1) | copy-start | bytes 442372
  23.9 1.3 %collective-permute-start.5 = (bf16[16,1536]{1,0:T(8,128)(2,1)S(1)}, bf16[16,1536]{1,0:T(8,128)(2,1)S(1)}, u32[]{:S(2)}, u32[]{:S(2)}) collective-permute-start(bf16[16,1536]{1,0:T(8,128)(2,1)S(1)} %shard_map.65.refs_6_), channel_id=1, source_target_pairs={{0,1},{1,0},{2,3},{3,2},{4,5},{5,4},{6,7},{7,6},{8,9},{9,8},{10,11... | collective-permute-start | bytes 147464 | tf_op jit(solution)/shard_map/ppermute | solution.py:250
  29.9 7.4 %collective-permute-start.6 = (bf16[64,1664]{1,0:T(8,128)(2,1)S(1)}, bf16[64,1664]{1,0:T(8,128)(2,1)S(1)}, u32[]{:S(2)}, u32[]{:S(2)}) collective-permute-start(bf16[64,1664]{1,0:T(8,128)(2,1)S(1)} %get-tuple-element.8), channel_id=1, source_target_pairs={{0,2},{1,3},{2,0},{3,1},{4,6},{5,7},{6,4},{7,5},{8,10},{9,11},{10,... | collective-permute-start | bytes 638984 | tf_op jit(solution)/shard_map/ppermute | solution.py:250
  37.3 4.8 %collective-permute-start.7 = (bf16[32,1664]{1,0:T(8,128)(2,1)S(1)}, bf16[32,1664]{1,0:T(8,128)(2,1)S(1)}, u32[]{:S(2)}, u32[]{:S(2)}) collective-permute-start(bf16[32,1664]{1,0:T(8,128)(2,1)S(1)} %get-tuple-element.10), channel_id=1, source_target_pairs={{0,4},{1,5},{2,6},{3,7},{4,0},{5,1},{6,2},{7,3},{8,12},{9,13},{10,... | collective-permute-start | bytes 319496 | tf_op jit(solution)/shard_map/ppermute | solution.py:250
  42.1 5.1 %collective-permute-start.8 = (bf16[16,1664]{1,0:T(8,128)(2,1)S(1)}, bf16[16,1664]{1,0:T(8,128)(2,1)S(1)}, u32[]{:S(2)}, u32[]{:S(2)}) collective-permute-start(bf16[16,1664]{1,0:T(8,128)(2,1)S(1)} %get-tuple-element.11), channel_id=1, source_target_pairs={{0,8},{1,9},{2,10},{3,11},{4,12},{5,13},{6,14},{7,15},{8,0},{9,1},... | collective-permute-start | bytes 159752 | tf_op jit(solution)/shard_map/ppermute | solution.py:250

commit v2 on v0

--- a/solution.py
+++ b/solution.py
@@ -1,9 +1,16 @@
+import functools
+
 import jax
 import jax.numpy as jnp
 from jax import lax
+from jax.experimental import pallas as pl
+from jax.experimental.pallas import tpu as pltpu
 from jax.sharding import PartitionSpec as P
 
 HD = 128
+LANES = 128
+PARENT_LANE = 64
+MASKED = -1e30
 
 
 def reorder(cache_rows, parents):
@@ -77,7 +84,7 @@
     return context.reshape(utterances * beam_width, feature)
 
 
-def body(cache_kv, new_rows, cross_queries, enc_kv, lengths, parents):
+def body_by_utterance(cache_kv, new_rows, cross_queries, enc_kv, lengths, parents):
     feature = cross_queries.shape[1]
     cross_context = attend_frames(cross_queries, enc_kv, lengths)
     arrived, new_here = (
@@ -95,6 +102,356 @@
     mixed_here = (self_context.astype(jnp.float32) + cross_context).astype(jnp.bfloat16)
     mixed = lax.all_to_all(mixed_here, "utt", split_axis=0, concat_axis=0, tiled=True)
     return mixed
+
+
+CORE = 1
+CLASS = 2
+PAIR = CLASS | CORE
+OVER_LAST = (((1,), (1,)), ((), ()))
+
+
+def class_of(index):
+    return (index // CLASS) % 2
+
+
+def rank_in_class(utt):
+    return utt // (2 * CLASS) * CLASS + utt % CLASS
+
+
+def utt_of_rank(rank, device):
+    return rank // CLASS * (2 * CLASS) + class_of(device) * CLASS + rank % CLASS
+
+
+def class_order(beams, device):
+    row = lax.broadcasted_iota(jnp.int32, (beams, beams), 0)
+    col = lax.broadcasted_iota(jnp.int32, (beams, beams), 1)
+    half = beams // 2
+    place = rank_in_class(col) + jnp.where(class_of(col) == class_of(device), 0, half)
+    return (row == place).astype(jnp.bfloat16)
+
+
+def pack_kernel(query_ref, key_ref, parents_ref, keep_ref, send_ref):
+    rows, feature = query_ref.shape
+    half = rows // 2
+    beams = parents_ref.shape[1]
+    order = class_order(rows, lax.axis_index("utt"))
+    query = query_ref[...]
+    product = query.astype(jnp.float32) * key_ref[...].astype(jnp.float32)
+    lane = lax.broadcasted_iota(jnp.int32, (rows, LANES), 1)
+    heads = feature // HD
+    at_parent_lane = lax.broadcasted_iota(jnp.int32, (beams, LANES), 0) + PARENT_LANE
+    at_parent_lane = at_parent_lane == lax.broadcasted_iota(jnp.int32, (beams, LANES), 1)
+    extra = jnp.dot(
+        jnp.broadcast_to(parents_ref[...], (rows, beams)).astype(jnp.bfloat16),
+        at_parent_lane.astype(jnp.bfloat16),
+        preferred_element_type=jnp.float32,
+    )
+    for head in range(heads):
+        own = jnp.sum(product[:, head * HD : (head + 1) * HD], axis=1, keepdims=True) * HD ** (-0.5)
+        for part in range(3):
+            term = own.astype(jnp.bfloat16).astype(jnp.float32)
+            extra = jnp.where(lane == part * heads + head, term, extra)
+            own = own - term
+    extra = extra.astype(jnp.bfloat16)
+    for at in range(0, feature + LANES, LANES):
+        tile = query[:, at : at + LANES] if at < feature else extra
+        tile = jnp.dot(order, tile, preferred_element_type=jnp.float32)
+        keep_ref[:, at : at + LANES] = tile[:half].astype(jnp.bfloat16)
+        send_ref[:, at : at + LANES] = tile[half:].astype(jnp.bfloat16)
+
+
+def cross_weights_kernel(lengths_ref, query_ref, keys_ref, out_ref):
+    rows, feature = query_ref.shape
+    frames = keys_ref.shape[0]
+    heads = feature // HD
+    live = lax.broadcasted_iota(jnp.int32, (rows, frames), 1) < lengths_ref[...]
+    scores = []
+    for head in range(heads):
+        at = slice(head * HD, (head + 1) * HD)
+        scores.append(
+            lax.dot_general(
+                query_ref[:, at], keys_ref[:, at], OVER_LAST, preferred_element_type=jnp.float32
+            )
+        )
+    for head in range(heads):
+        masked = jnp.where(live, scores[head] * HD ** (-0.5), MASKED)
+        raised = jnp.where(live, jnp.exp(masked - jnp.max(masked, axis=1, keepdims=True)), 0.0)
+        weights = raised / jnp.sum(raised, axis=1, keepdims=True)
+        out_ref[head] = weights.astype(jnp.bfloat16)
+
+
+def cross_values_kernel(weights_ref, values_ref, out_ref):
+    for head in range(weights_ref.shape[0]):
+        at = slice(head * HD, (head + 1) * HD)
+        out_ref[:, at] = jnp.dot(
+            weights_ref[head], values_ref[:, at], preferred_element_type=jnp.float32
+        ).astype(jnp.bfloat16)
+
+
+def cached(near_ref, far_ref, pair_near_ref, pair_far_ref, mine, at):
+    pieces = [ref[part, mine, :, at] for ref in (near_ref, far_ref) for part in range(near_ref.shape[0])]
+    return jnp.concatenate(pieces + [pair_near_ref[:, at], pair_far_ref[:, at]], axis=0)
+
+
+def rows_of(masks, beams):
+    return [mask ^ pair for mask in masks for pair in (0, PAIR)]
+
+
+def self_weights_kernel(masks, counts, *refs):
+    query_refs, refs = refs[:counts], refs[counts:]
+    *cache_refs, weight_ref, share_ref = refs
+    me = lax.axis_index("utt").astype(jnp.int32)
+    mine = class_of(me)
+    pair_keys, feature = cache_refs[-1].shape
+    heads, rows, keys = weight_ref.shape
+    beams = query_refs[0].shape[0]
+    half_beams = beams // 2
+    history = pair_keys // half_beams
+    queries = jnp.concatenate([ref[...] for ref in query_refs], axis=0)
+    extra = queries[:, feature:].astype(jnp.float32)
+
+    scores = []
+    for head in range(heads):
+        at = slice(head * HD, (head + 1) * HD)
+        scores.append(
+            lax.dot_general(
+                queries[:, at],
+                cached(*cache_refs, mine, at),
+                OVER_LAST,
+                preferred_element_type=jnp.float32,
+            )
+        )
+
+    utt = utt_of_rank(lax.broadcasted_iota(jnp.int32, (half_beams, LANES), 0), me)
+    lane = lax.broadcasted_iota(jnp.int32, (half_beams, LANES), 1)
+    table = jnp.zeros((half_beams, LANES), jnp.float32)
+    for at, mask in enumerate(masks):
+        lists = extra[at * beams : at * beams + half_beams]
+        owner = me ^ mask
+        table = jnp.where(utt == owner, lists, table)
+        table = jnp.where(utt == (owner ^ CORE), pltpu.roll(lists, LANES - beams, 1), table)
+    chosen = jnp.concatenate(
+        [
+            jnp.sum(
+                jnp.where(lane == PARENT_LANE + (me ^ mask), table, 0.0), axis=1, keepdims=True
+            )
+            for mask in rows_of(masks, beams)
+        ],
+        axis=0,
+    ).astype(jnp.int32)
+
+    row_rank = lax.broadcasted_iota(jnp.int32, (rows, keys), 0) % half_beams
+    key = lax.broadcasted_iota(jnp.int32, (rows, keys), 1)
+    key_rank = key % pair_keys // history
+    run = key // pair_keys
+    owner = me ^ jnp.where(
+        run == 0, 0, jnp.where(run == 1, CORE, jnp.where(run == 2, PAIR, PAIR ^ CORE))
+    )
+    bias = jnp.where((key_rank == row_rank) & (chosen == owner), 0.0, MASKED)
+    group = CORE | PAIR
+    row_live = (chosen // (group + 1)) == (me // (group + 1))
+
+    own_all = extra + pltpu.roll(extra, LANES - heads, 1) + pltpu.roll(extra, LANES - 2 * heads, 1)
+    row_lane = lax.broadcasted_iota(jnp.int32, (rows, LANES), 1)
+    shares = jnp.zeros((rows, LANES), jnp.float32)
+    for head in range(heads):
+        masked = scores[head] * HD ** (-0.5) + bias
+        own = own_all[:, head : head + 1]
+        peak = jnp.maximum(jnp.max(masked, axis=1, keepdims=True), own)
+        raised = jnp.exp(masked - peak)
+        own = jnp.exp(own - peak)
+        share = 1.0 / (jnp.sum(raised, axis=1, keepdims=True) + own)
+        weight_ref[head] = (raised * share).astype(jnp.bfloat16)
+        shares = jnp.where(row_lane == head, own * share, shares)
+    share_ref[...] = jnp.where(row_live, shares, 0.0).astype(jnp.bfloat16)
+
+
+def self_values_kernel(masks, *refs):
+    weight_ref, share_ref, *cache_refs, cross_near_ref, cross_far_ref, send_ref, keep_ref = refs
+    me = lax.axis_index("utt").astype(jnp.int32)
+    mine = class_of(me)
+    heads, rows, _ = weight_ref.shape
+    feature = heads * HD
+    half = rows // 2
+    beams = cross_near_ref.shape[0]
+    half_beams = beams // 2
+    keep_ref[:, feature:] = share_ref[:half]
+    send_ref[:, feature:] = share_ref[half:]
+
+    place = lax.broadcasted_iota(jnp.int32, (rows, beams), 1)
+    pick_utt = utt_of_rank(lax.broadcasted_iota(jnp.int32, (rows, beams), 0) % half_beams, me)
+    row_beam = me ^ jnp.concatenate(
+        [jnp.full((half_beams, beams), mask, jnp.int32) for mask in rows_of(masks, beams)], axis=0
+    )
+    near_pick = ((place == row_beam) & (pick_utt == me)).astype(jnp.bfloat16)
+    far_pick = ((place == row_beam) & (pick_utt == (me ^ CORE))).astype(jnp.bfloat16)
+    pick = jnp.concatenate([near_pick, far_pick], axis=1)
+    for head in range(heads):
+        at = slice(head * HD, (head + 1) * HD)
+        out = jnp.dot(
+            weight_ref[head], cached(*cache_refs, mine, at), preferred_element_type=jnp.float32
+        )
+        cross = jnp.concatenate([cross_near_ref[:, at], cross_far_ref[:, at]], axis=0)
+        out = out + jnp.dot(pick, cross, preferred_element_type=jnp.float32)
+        out = out.astype(jnp.bfloat16)
+        keep_ref[:, at] = out[:half]
+        send_ref[:, at] = out[half:]
+
+
+def finish_kernel(mine_ref, came_ref, value_ref, out_ref):
+    rows, feature = out_ref.shape
+    order = class_order(rows, lax.axis_index("utt"))
+
+    def ordered(at):
+        tile = jnp.concatenate(
+            [mine_ref[:, at].astype(jnp.float32), came_ref[:, at].astype(jnp.float32)], axis=0
+        ).astype(jnp.bfloat16)
+        return lax.dot_general(
+            order, tile, (((0,), (0,)), ((), ())), preferred_element_type=jnp.float32
+        )
+
+    shares = ordered(slice(feature, feature + LANES))
+    for head in range(feature // HD):
+        at = slice(head * HD, (head + 1) * HD)
+        out = ordered(at) + shares[:, head : head + 1] * value_ref[:, at].astype(jnp.float32)
+        out_ref[:, at] = out.astype(jnp.bfloat16)
+
+
+def whole(shape):
+    return pl.BlockSpec(shape, lambda *_: (0,) * len(shape))
+
+
+def body_by_parent(devices, cache_kv, new_rows, cross_queries, enc_kv, lengths, parents):
+    beams = parents.shape[1]
+    rows, feature = cross_queries.shape
+    frames = enc_kv.shape[1]
+    history = cache_kv.shape[1]
+    heads = feature // HD
+    width = feature + LANES
+    keys = beams * history
+    me = lax.axis_index("utt").astype(jnp.int32)
+    params = pltpu.CompilerParams(vmem_limit_bytes=16 * 1024 * 1024)
+
+    def swap(array, bits):
+        return lax.ppermute(array, "utt", [(i, i ^ bits) for i in range(devices)])
+
+    def after(array, *others):
+        return lax.optimization_barrier((array,) + others)[0]
+
+    hops = [(1 << k) | CORE for k in range(devices.bit_length() - 2, 1, -1)]
+
+    half_rows = jax.ShapeDtypeStruct((rows // 2, width), jnp.bfloat16)
+    own, other = pl.pallas_call(
+        pack_kernel,
+        out_shape=(half_rows, half_rows),
+        grid=(1,),
+        in_specs=[
+            pl.BlockSpec((rows, feature), lambda i: (0, 0)),
+            pl.BlockSpec((rows, feature), lambda i: (0, 1)),
+            whole(parents.shape),
+        ],
+        out_specs=(whole(half_rows.shape), whole(half_rows.shape)),
+        compiler_params=params,
+    )(new_rows, new_rows, parents)
+    pair_rows = swap(other, PAIR)
+
+    near = cache_kv.reshape(beams // (2 * CLASS), 2, CLASS * history, 2 * feature)
+    far = swap(near, CORE)
+    other_class = lax.dynamic_index_in_dim(near, 1 - class_of(me), 1, keepdims=False)
+    pair_keys = swap(other_class[..., :feature], PAIR).reshape(keys // 2, feature)
+    pair_values = swap(after(other_class[..., feature:], pair_rows), PAIR)
+    pair_values = pair_values.reshape(keys // 2, feature)
+
+    lists = jnp.pad(
+        swap(parents, CORE).astype(jnp.bfloat16),
+        ((0, 0), (feature + PARENT_LANE + beams, LANES - PARENT_LANE - 2 * beams)),
+    )
+    held = jnp.concatenate([own + lists, pair_rows], axis=0)
+    gathered, masks, held_masks = [held], [0], [0]
+    for bits in hops:
+        came = swap(held, bits)
+        gathered.append(came)
+        masks = masks + [mask ^ bits for mask in held_masks]
+        held_masks = masks
+        if bits != hops[-1]:
+            held = jnp.concatenate([held, came], axis=0)
+
+    weights = pl.pallas_call(
+        cross_weights_kernel,
+        out_shape=jax.ShapeDtypeStruct((heads, rows, frames), jnp.bfloat16),
+        grid=(1,),
+        in_specs=[
+            whole((1, 1)),
+            whole((rows, feature)),
+            pl.BlockSpec((frames, feature), lambda i: (0, 0)),
+        ],
+        out_specs=whole((heads, rows, frames)),
+        compiler_params=params,
+    )(lengths.reshape(1, 1), cross_queries, enc_kv.reshape(frames, 2 * feature))
+    cross_near = pl.pallas_call(
+        cross_values_kernel,
+        out_shape=jax.ShapeDtypeStruct((rows, feature), jnp.bfloat16),
+        grid=(1,),
+        in_specs=[
+            whole((heads, rows, frames)),
+            pl.BlockSpec((frames, feature), lambda i: (0, 1)),
+        ],
+        out_specs=whole((rows, feature)),
+        compiler_params=params,
+    )(weights, enc_kv.reshape(frames, 2 * feature))
+    cross_far = swap(cross_near, CORE)
+
+    pair_far_keys = swap(after(pair_keys, held), CORE)
+    pair_far_values = swap(after(pair_values, gathered[-1]), CORE)
+
+    all_rows = rows * len(masks)
+    half = all_rows // 2
+    weight_shape = jax.ShapeDtypeStruct((heads, all_rows, 2 * keys), jnp.bfloat16)
+    share_shape = jax.ShapeDtypeStruct((all_rows, LANES), jnp.bfloat16)
+    part = jax.ShapeDtypeStruct((half, width), jnp.bfloat16)
+    near_shape = near.shape[:3] + (feature,)
+    in_keys = pl.BlockSpec(near_shape, lambda i: (0, 0, 0, 0))
+    in_values = pl.BlockSpec(near_shape, lambda i: (0, 0, 0, 1))
+    pair_spec = whole(pair_keys.shape)
+    weights, shares = pl.pallas_call(
+        functools.partial(self_weights_kernel, tuple(masks), len(gathered)),
+        out_shape=(weight_shape, share_shape),
+        grid=(1,),
+        in_specs=[whole(block.shape) for block in gathered]
+        + [in_keys, in_keys, pair_spec, pair_spec],
+        out_specs=(whole(weight_shape.shape), whole(share_shape.shape)),
+        compiler_params=params,
+    )(*gathered, near, far, pair_keys, pair_far_keys)
+    send, keep = pl.pallas_call(
+        functools.partial(self_values_kernel, tuple(masks)),
+        out_shape=(part, part),
+        grid=(1,),
+        in_specs=[whole(weights.shape), whole(shares.shape)]
+        + [in_values, in_values, pair_spec, pair_spec]
+        + [whole((rows, feature))] * 2,
+        out_specs=(whole(part.shape), whole(part.shape)),
+        compiler_params=params,
+    )(weights, shares, near, far, pair_values, pair_far_values, cross_near, cross_far)
+
+    for bits in hops[::-1]:
+        came = swap(send, bits)
+        half = half // 2
+        send = keep[half:] + came[half:]
+        keep = keep[:half] + came[:half]
+    came = swap(send, PAIR)
+
+    return pl.pallas_call(
+        finish_kernel,
+        out_shape=jax.ShapeDtypeStruct((rows, feature), jnp.bfloat16),
+        grid=(1,),
+        in_specs=[
+            whole(half_rows.shape),
+            whole(half_rows.shape),
+            pl.BlockSpec((rows, feature), lambda i: (0, 2)),
+        ],
+        out_specs=whole((rows, feature)),
+        compiler_params=params,
+    )(keep, came, new_rows)
 
 
 def solution(mesh):
@@ -106,6 +463,23 @@
         P(("groups", "utt")),
         P(("groups", "utt"), None),
     )
+    devices = mesh.shape["utt"]
+
+    def body(cache_kv, new_rows, cross_queries, enc_kv, lengths, parents):
+        beams = parents.shape[1]
+        heads = cross_queries.shape[1] // HD
+        fits = (
+            parents.shape[0] == 1
+            and devices == beams
+            and devices >= 8
+            and devices & (devices - 1) == 0
+            and beams % 16 == 0
+            and 3 * heads <= PARENT_LANE
+            and PARENT_LANE + 2 * beams <= LANES
+        )
+        plan = functools.partial(body_by_parent, devices) if fits else body_by_utterance
+        return plan(cache_kv, new_rows, cross_queries, enc_kv, lengths, parents)
+
     return jax.shard_map(
         body, mesh=mesh, in_specs=placed, out_specs=P(("groups", "utt"), None), check_vma=False
     )

time: 56.3 us -> 40.9 us (0.73)
  blocking collectives: 12 us -> 0 us
  waiting for transfers between devices: 22.7 us -> 16.3 us
  Pallas kernels: 0 us -> 5.29 us
  starting transfers between devices: 11 us -> 15.3 us
  other arithmetic: 2.63 us -> 0.06 us
  local copies, waits for them, and re-layouts: 5.25 us -> 2.75 us
  matrix products: 1.41 us -> 0 us
    all_to_all x2 -> x0, waiting for transfers between devices: 22.7 us -> none  [the longest x1 17.2 us: body(): lax.all_to_all(cache_kv, 'utt', split_axis=0, concat_axis=0, tiled=True)]
    ppermute x0 -> x13, waiting for transfers between devices: none -> 16.3 us  [swap(): return lax.ppermute(array, 'utt', [(i, i ^ bits) for i in range(devices)])]
    ppermute x0 -> x13, starting transfers between devices: none -> 15.3 us  [swap(): return lax.ppermute(array, 'utt', [(i, i ^ bits) for i in range(devices)])]
    all_to_all x1 -> x0, blocking collectives: 12 us -> none  [body(): lax.all_to_all(mixed_here, 'utt', split_axis=0, concat_axis=0, tiled=True)]
    all_to_all x2 -> x0, starting transfers between devices: 11 us -> none  [the longest x1 7.39 us: body(): lax.all_to_all(new_rows, 'utt', split_axis=0, concat_axis=0, tiled=True)]
    pallas_call x0 -> x6, Pallas kernels: none -> 5.29 us  [the longest x1 2.95 us: body_by_parent(): pl.pallas_call(functools.partial(self_weights_kernel, tuple(masks), len(g...]
    all_to_all x1 -> x0, other arithmetic: 1.6 us -> none  [body(): lax.all_to_all(new_rows, 'utt', split_axis=0, concat_axis=0, tiled=True)]
    slice x1, local copies, waits for them, and re-layouts: 1.47 us -> 0.03 us  [body_by_parent(): pair_values = swap(after(other_class[..., feature:], pair_rows), PAIR)]
  transfers between devices with their start and end apart: 2 -> 13, of which waited for: 2 -> 7; matrix products, arithmetic and copies ran while one was open for 6% -> 3% of each run, Pallas kernels for 0% -> 10%
where the time goes in v2:
time: 40.9 us; the launch traced here: 40.5 us
  waiting for transfers between devices  16.3 us (40%)
  starting transfers between devices  15.3 us (37%)
  Pallas kernels  5.29 us (13%)
  local copies, waits for them, and re-layouts  2.75 us (7%)
  between operations  0.77 us (2%)
    ppermute x13, waiting for transfers between devices, swap(): return lax.ppermute(array, 'utt', [(i, i ^ bits) for i in range(devices)])  16.3 us
    ppermute x13, starting transfers between devices, swap(): return lax.ppermute(array, 'utt', [(i, i ^ bits) for i in range(devices)])  15.3 us
    pallas_call x1, Pallas kernels, body_by_parent(): pl.pallas_call(functools.partial(self_weights_kernel, tuple(masks), len(g...  2.95 us
    unnamed x12, local copies, waits for them, and re-layouts  1.62 us
    squeeze x1, local copies, waits for them, and re-layouts, body_by_parent(): lax.dynamic_index_in_dim(near, 1 - class_of(me), 1, keepdims=False)  1.02 us
    pallas_call x1, Pallas kernels, body_by_parent(): pl.pallas_call(finish_kernel, out_shape=jax.ShapeDtypeStruct((rows, featu...  0.93 us
  transfers between devices with their start and end apart: 13, of which 7 were waited for; matrix products, arithmetic and copies ran while one was open for 3% of the time, Pallas kernels for 10%

profile of v2, /device:TPU:0, one launch (start us, length us, event | category | flops | bytes accessed | tf_op | source)
XLA Modules:
  0.0 40.5 jit_solution(8769915092099717466)
XLA Ops:
  0.0 0.5 %collective-permute-start = (s32[1,16]{1,0:T(1,128)}, s32[1,16]{1,0:T(1,128)S(1)}, u32[]{:S(2)}, u32[]{:S(2)}) collective-permute-start(s32[1,16]{1,0:T(1,128)} %parents_ref.1), channel_id=1, source_target_pairs={{0,1},{1,0},{2,3},{3,2},{4,5},{5,4},{6,7},{7,6},{8,9},{9,8},{10,11... | collective-permute-start | bytes 200 | tf_op jit(solution)/shard_map/ppermute | solution.py:336
  0.5 0.9 %copy-done.2 = bf16[16,4608]{1,0:T(8,128)(2,1)S(1)} copy-done((bf16[16,4608]{1,0:T(8,128)(2,1)S(1)}, bf16[16,4608]{1,0:T(8,128)(2,1)}, u32[]{:S(2)}) %copy-start.2) | copy-done | bytes 147480
  1.4 0.7 %copy-done.5 = s32[1,16]{1,0:T(1,128)S(1)} copy-done((s32[1,16]{1,0:T(1,128)S(1)}, s32[1,16]{1,0:T(1,128)}, u32[]{:S(2)}) %copy-start.5) | copy-done | bytes 88
  2.1 0.3 shard_map.64
  2.3 2.6 %collective-permute-start.1 = (bf16[8,1664]{1,0:T(8,128)(2,1)S(1)}, bf16[8,1664]{1,0:T(8,128)(2,1)S(1)}, u32[]{:S(2)}, u32[]{:S(2)}) collective-permute-start(bf16[8,1664]{1,0:T(8,128)(2,1)S(1)} %get-tuple-element.15), channel_id=1, source_target_pairs={{0,3},{1,2},{2,1},{3,0},{4,7},{5,6},{6,5},{7,4},{8,11},{9,10},{10,... | collective-permute-start | bytes 79880 | tf_op jit(solution)/shard_map/ppermute | solution.py:336
  5.1 1.0 %dynamic-slice_bitcast_fusion = bf16[4,16,3072]{2,1,0:T(8,128)(2,1)S(1)} fusion(bf16[4,2,16,3072]{3,2,1,0:T(8,128)(2,1)} %bitcast.11, s32[]{:T(128)S(6)} %select_n.17), kind=kLoop, calls=%fused_computation | loop fusion | bytes 786436 | tf_op jit(solution)/shard_map/jit(dynamic_index_in_dim)/squeeze | solution.py:360
  6.2 0.2 collective-permute-done.1
  6.5 2.8 %collective-permute-start.2 = (bf16[16,1664]{1,0:T(8,128)(2,1)S(1)}, bf16[16,1664]{1,0:T(8,128)(2,1)S(1)}, u32[]{:S(2)}, u32[]{:S(2)}) collective-permute-start(bf16[16,1664]{1,0:T(8,128)(2,1)S(1)} %pad_maximum_fusion.1.refs_0_), channel_id=1, source_target_pairs={{0,9},{1,8},{2,11},{3,10},{4,13},{5,12},{6,15},{7,14},{8,1},{9,0},... | collective-permute-start | bytes 159752 | tf_op jit(solution)/shard_map/ppermute | solution.py:336
  9.3 1.4 %collective-permute-start.5 = (bf16[4,16,1536]{2,1,0:T(8,128)(2,1)S(1)}, bf16[4,16,1536]{2,1,0:T(8,128)(2,1)S(1)}, u32[]{:S(2)}, u32[]{:S(2)}) collective-permute-start(bf16[4,16,1536]{2,1,0:T(8,128)(2,1)S(1)} %get-tuple-element.24), channel_id=1, source_target_pairs={{0,3},{1,2},{2,1},{3,0},{4,7},{5,6},{6,5},{7,4},{8,11},{9,10},{10,... | collective-permute-start | bytes 589832 | tf_op jit(solution)/shard_map/ppermute | solution.py:336
  10.7 0.5 %collective-permute-start.7 = (bf16[4,16,1536]{2,1,0:T(8,128)(2,1)S(1)}, bf16[4,16,1536]{2,1,0:T(8,128)(2,1)S(1)}, u32[]{:S(2)}, u32[]{:S(2)}) collective-permute-start(bf16[4,16,1536]{2,1,0:T(8,128)(2,1)S(1)} %get-tuple-element.19), channel_id=1, source_target_pairs={{0,3},{1,2},{2,1},{3,0},{4,7},{5,6},{6,5},{7,4},{8,11},{9,10},{10,... | collective-permute-start | bytes 589832 | tf_op jit(solution)/shard_map/ppermute | solution.py:336
  11.3 2.0 %collective-permute-start.3 = (bf16[32,1664]{1,0:T(8,128)(2,1)S(1)}, bf16[32,1664]{1,0:T(8,128)(2,1)S(1)}, u32[]{:S(2)}, u32[]{:S(2)}) collective-permute-start(bf16[32,1664]{1,0:T(8,128)(2,1)S(1)} %pad_maximum_fusion), channel_id=1, source_target_pairs={{0,5},{1,4},{2,7},{3,6},{4,1},{5,0},{6,3},{7,2},{8,13},{9,12},{10,... | collective-permute-start | bytes 319496 | tf_op jit(solution)/shard_map/ppermute | solution.py:336
  13.3 2.9 %collective-permute-done.5 = bf16[4,16,1536]{2,1,0:T(8,128)(2,1)S(1)} collective-permute-done((bf16[4,16,1536]{2,1,0:T(8,128)(2,1)S(1)}, bf16[4,16,1536]{2,1,0:T(8,128)(2,1)S(1)}, u32[]{:S(2)}, u32[]{:S(2)}) %collective-permute-start.5) | collective-permute-done | bytes 196640 | tf_op jit(solution)/shard_map/ppermute | solution.py:336
  16.2 0.8 %collective-permute-start.6 = (bf16[64,1536]{1,0:T(8,128)(2,1)S(1)}, bf16[64,1536]{1,0:T(8,128)(2,1)S(1)}, u32[]{:S(2)}, u32[]{:S(2)}) collective-permute-start(bf16[64,1536]{1,0:T(8,128)(2,1)S(1)} %bitcast.16), channel_id=1, source_target_pairs={{0,1},{1,0},{2,3},{3,2},{4,5},{5,4},{6,7},{7,6},{8,9},{9,8},{10,11... | collective-permute-start | bytes 589832 | tf_op jit(solution)/shard_map/ppermute | solution.py:336
  17.0 3.4 %collective-permute-done.7 = bf16[4,16,1536]{2,1,0:T(8,128)(2,1)S(1)} collective-permute-done((bf16[4,16,1536]{2,1,0:T(8,128)(2,1)S(1)}, bf16[4,16,1536]{2,1,0:T(8,128)(2,1)S(1)}, u32[]{:S(2)}, u32[]{:S(2)}) %collective-permute-start.7) | collective-permute-done | bytes 196640 | tf_op jit(solution)/shard_map/ppermute | solution.py:336
  21.3 0.5 %shard_map.66.weights_ref = bf16[12,16,256]{2,1,0:T(8,128)(2,1)S(1)} custom-call(s32[1,1]{1,0:T(1,128)} %bitcast.7.lengths_ref, bf16[16,1536]{1,0:T(8,128)(2,1)S(1)} %copy-done.4, bf16[256,3072]{1,0:T(8,128)(2,1)S(1)} %bitcast.8), custom_call_target="tpu_custom_call" | custom-call | tf_op jit(solution)/shard_map/pallas_call | solution.py:379
  22.0 0.4 collective-permute-start.9
  22.4 3.0 %shard_map.65 = (bf16[12,64,256]{2,1,0:T(8,128)(2,1)S(1)}, bf16[64,128]{1,0:T(8,128)(2,1)S(1)}) custom-call(bf16[16,1664]{1,0:T(8,128)(2,1)S(1)} %pad_maximum_fusion.1.refs_0_, bf16[16,1664]{1,0:T(8,128)(2,1)S(1)} %collective-permute-done.2.refs_1_, bf16[32,1664]{1,0:T(8,128)(2,1)S(1)} %collective-permute-done.3.refs_2_, ...), custom_call_target="tpu_custom_call" | custom-call | tf_op jit(solution)/shard_map/pallas_call | solution.py:416
  25.4 0.4 %shard_map.68 = (bf16[32,1664]{1,0:T(8,128)(2,1)S(1)}, bf16[32,1664]{1,0:T(8,128)(2,1)S(1)}) custom-call(bf16[12,64,256]{2,1,0:T(8,128)(2,1)S(1)} %get-tuple-element.17.refs_0_, bf16[64,128]{1,0:T(8,128)(2,1)S(1)} %get-tuple-element.18.refs_1_, bf16[4,2,16,3072]{3,2,1,0:T(8,128)(2,1)S(1)} %bitcast.13, ...), custom_call_target="tpu_custom_call" | custom-call | tf_op jit(solution)/shard_map/pallas_call | solution.py:425
  25.9 1.6 %collective-permute-start.10 = (bf16[32,1664]{1,0:T(8,128)(2,1)S(1)}, bf16[32,1664]{1,0:T(8,128)(2,1)S(1)}, u32[]{:S(2)}, u32[]{:S(2)}) collective-permute-start(bf16[32,1664]{1,0:T(8,128)(2,1)S(1)} %get-tuple-element.22), channel_id=1, source_target_pairs={{0,5},{1,4},{2,7},{3,6},{4,1},{5,0},{6,3},{7,2},{8,13},{9,12},{10,... | collective-permute-start | bytes 319496 | tf_op jit(solution)/shard_map/ppermute | solution.py:336
  27.4 3.4 %collective-permute-done.10 = bf16[32,1664]{1,0:T(8,128)(2,1)S(1)} collective-permute-done((bf16[32,1664]{1,0:T(8,128)(2,1)S(1)}, bf16[32,1664]{1,0:T(8,128)(2,1)S(1)}, u32[]{:S(2)}, u32[]{:S(2)}) %collective-permute-start.10) | collective-permute-done | bytes 106528 | tf_op jit(solution)/shard_map/ppermute | solution.py:336
  30.9 4.7 %collective-permute-done.11 = bf16[16,1664]{1,0:T(8,128)(2,1)S(1)} collective-permute-done((bf16[16,1664]{1,0:T(8,128)(2,1)S(1)}, bf16[16,1664]{1,0:T(8,128)(2,1)S(1)}, u32[]{:S(2)}, u32[]{:S(2)}) %collective-permute-start.11) | collective-permute-done | bytes 53280 | tf_op jit(solution)/shard_map/ppermute | solution.py:336
  35.5 2.5 %collective-permute-start.12 = (bf16[8,1664]{1,0:T(8,128)(2,1)S(1)}, bf16[8,1664]{1,0:T(8,128)(2,1)S(1)}, u32[]{:S(2)}, u32[]{:S(2)}) collective-permute-start(bf16[8,1664]{1,0:T(8,128)(2,1)S(1)} %get-tuple-element.27), channel_id=1, source_target_pairs={{0,3},{1,2},{2,1},{3,0},{4,7},{5,6},{6,5},{7,4},{8,11},{9,10},{10,... | collective-permute-start | bytes 79880 | tf_op jit(solution)/shard_map/ppermute | solution.py:336
  38.0 1.5 %collective-permute-done.12.came_ref = bf16[8,1664]{1,0:T(8,128)(2,1)S(1)} collective-permute-done((bf16[8,1664]{1,0:T(8,128)(2,1)S(1)}, bf16[8,1664]{1,0:T(8,128)(2,1)S(1)}, u32[]{:S(2)}, u32[]{:S(2)}) %collective-permute-start.12) | collective-permute-done | bytes 26656 | tf_op jit(solution)/shard_map/ppermute | solution.py:336
  39.6 0.9 %shard_map.69 = bf16[16,1536]{1,0:T(8,128)(2,1)} custom-call(bf16[8,1664]{1,0:T(8,128)(2,1)S(1)} %get-tuple-element.28.mine_ref, bf16[8,1664]{1,0:T(8,128)(2,1)S(1)} %collective-permute-done.12.came_ref, bf16[16,4608]{1,0:T(8,128)(2,1)S(1)} %copy-done.3), custom_call_target="tpu_custom_call" | custom-call | tf_op jit(solution)/shard_map/pallas_call | solution.py:443
  (29 shorter events, 1.0 us)
Async XLA Ops:
  0.0 21.3 %copy-start = (bf16[1,256,3072]{2,1,0:T(8,128)(2,1)S(1)}, bf16[1,256,3072]{2,1,0:T(8,128)(2,1)}, u32[]{:S(2)}) copy-start(bf16[1,256,3072]{2,1,0:T(8,128)(2,1)} %param.9) | copy-start | bytes 4718596
  0.0 6.1 %collective-permute-start = (s32[1,16]{1,0:T(1,128)}, s32[1,16]{1,0:T(1,128)S(1)}, u32[]{:S(2)}, u32[]{:S(2)}) collective-permute-start(s32[1,16]{1,0:T(1,128)} %parents_ref.1), channel_id=1, source_target_pairs={{0,1},{1,0},{2,3},{3,2},{4,5},{5,4},{6,7},{7,6},{8,9},{9,8},{10,11... | collective-permute-start | bytes 200 | tf_op jit(solution)/shard_map/ppermute | solution.py:336
  0.5 0.9 %copy-start.2 = (bf16[16,4608]{1,0:T(8,128)(2,1)S(1)}, bf16[16,4608]{1,0:T(8,128)(2,1)}, u32[]{:S(2)}) copy-start(bf16[16,4608]{1,0:T(8,128)(2,1)} %value_ref.1) | copy-start | bytes 442372
  1.4 0.7 %copy-start.5 = (s32[1,16]{1,0:T(1,128)S(1)}, s32[1,16]{1,0:T(1,128)}, u32[]{:S(2)}) copy-start(s32[1,16]{1,0:T(1,128)} %parents_ref.1) | copy-start | bytes 196
  2.1 19.2 %copy-start.4 = (bf16[16,1536]{1,0:T(8,128)(2,1)S(1)}, bf16[16,1536]{1,0:T(8,128)(2,1)}, u32[]{:S(2)}) copy-start(bf16[16,1536]{1,0:T(8,128)(2,1)} %query_ref.3) | copy-start | bytes 147460
  2.3 4.1 %collective-permute-start.1 = (bf16[8,1664]{1,0:T(8,128)(2,1)S(1)}, bf16[8,1664]{1,0:T(8,128)(2,1)S(1)}, u32[]{:S(2)}, u32[]{:S(2)}) collective-permute-start(bf16[8,1664]{1,0:T(8,128)(2,1)S(1)} %get-tuple-element.15), channel_id=1, source_target_pairs={{0,3},{1,2},{2,1},{3,0},{4,7},{5,6},{6,5},{7,4},{8,11},{9,10},{10,... | collective-permute-start | bytes 79880 | tf_op jit(solution)/shard_map/ppermute | solution.py:336
  4.9 17.5 %collective-permute-start.4 = (bf16[4,2,16,3072]{3,2,1,0:T(8,128)(2,1)}, bf16[4,2,16,3072]{3,2,1,0:T(8,128)(2,1)S(1)}, u32[]{:S(2)}, u32[]{:S(2)}) collective-permute-start(bf16[4,2,16,3072]{3,2,1,0:T(8,128)(2,1)} %bitcast.10), channel_id=1, source_target_pairs={{0,1},{1,0},{2,3},{3,2},{4,5},{5,4},{6,7},{7,6},{8,9},{9,8},{10,11... | collective-permute-start | bytes 2359304 | tf_op jit(solution)/shard_map/ppermute | solution.py:336
  6.5 4.9 %collective-permute-start.2 = (bf16[16,1664]{1,0:T(8,128)(2,1)S(1)}, bf16[16,1664]{1,0:T(8,128)(2,1)S(1)}, u32[]{:S(2)}, u32[]{:S(2)}) collective-permute-start(bf16[16,1664]{1,0:T(8,128)(2,1)S(1)} %pad_maximum_fusion.1.refs_0_), channel_id=1, source_target_pairs={{0,9},{1,8},{2,11},{3,10},{4,13},{5,12},{6,15},{7,14},{8,1},{9,0},... | collective-permute-start | bytes 159752 | tf_op jit(solution)/shard_map/ppermute | solution.py:336
  9.3 6.9 %collective-permute-start.5 = (bf16[4,16,1536]{2,1,0:T(8,128)(2,1)S(1)}, bf16[4,16,1536]{2,1,0:T(8,128)(2,1)S(1)}, u32[]{:S(2)}, u32[]{:S(2)}) collective-permute-start(bf16[4,16,1536]{2,1,0:T(8,128)(2,1)S(1)} %get-tuple-element.24), channel_id=1, source_target_pairs={{0,3},{1,2},{2,1},{3,0},{4,7},{5,6},{6,5},{7,4},{8,11},{9,10},{10,... | collective-permute-start | bytes 589832 | tf_op jit(solution)/shard_map/ppermute | solution.py:336
  10.7 9.8 %collective-permute-start.7 = (bf16[4,16,1536]{2,1,0:T(8,128)(2,1)S(1)}, bf16[4,16,1536]{2,1,0:T(8,128)(2,1)S(1)}, u32[]{:S(2)}, u32[]{:S(2)}) collective-permute-start(bf16[4,16,1536]{2,1,0:T(8,128)(2,1)S(1)} %get-tuple-element.19), channel_id=1, source_target_pairs={{0,3},{1,2},{2,1},{3,0},{4,7},{5,6},{6,5},{7,4},{8,11},{9,10},{10,... | collective-permute-start | bytes 589832 | tf_op jit(solution)/shard_map/ppermute | solution.py:336
  11.3 5.7 %collective-permute-start.3 = (bf16[32,1664]{1,0:T(8,128)(2,1)S(1)}, bf16[32,1664]{1,0:T(8,128)(2,1)S(1)}, u32[]{:S(2)}, u32[]{:S(2)}) collective-permute-start(bf16[32,1664]{1,0:T(8,128)(2,1)S(1)} %pad_maximum_fusion), channel_id=1, source_target_pairs={{0,5},{1,4},{2,7},{3,6},{4,1},{5,0},{6,3},{7,2},{8,13},{9,12},{10,... | collective-permute-start | bytes 319496 | tf_op jit(solution)/shard_map/ppermute | solution.py:336
  16.2 6.2 %collective-permute-start.6 = (bf16[64,1536]{1,0:T(8,128)(2,1)S(1)}, bf16[64,1536]{1,0:T(8,128)(2,1)S(1)}, u32[]{:S(2)}, u32[]{:S(2)}) collective-permute-start(bf16[64,1536]{1,0:T(8,128)(2,1)S(1)} %bitcast.16), channel_id=1, source_target_pairs={{0,1},{1,0},{2,3},{3,2},{4,5},{5,4},{6,7},{7,6},{8,9},{9,8},{10,11... | collective-permute-start | bytes 589832 | tf_op jit(solution)/shard_map/ppermute | solution.py:336
  20.4 5.0 %collective-permute-start.8 = (bf16[64,1536]{1,0:T(8,128)(2,1)S(1)}, bf16[64,1536]{1,0:T(8,128)(2,1)S(1)}, u32[]{:S(2)}, u32[]{:S(2)}) collective-permute-start(bf16[64,1536]{1,0:T(8,128)(2,1)S(1)} %bitcast.14), channel_id=1, source_target_pairs={{0,1},{1,0},{2,3},{3,2},{4,5},{5,4},{6,7},{7,6},{8,9},{9,8},{10,11... | collective-permute-start | bytes 589832 | tf_op jit(solution)/shard_map/ppermute | solution.py:336
  21.3 1.2 %copy-start.1 = (bf16[16,8,3072]{2,1,0:T(8,128)(2,1)S(1)}, bf16[16,8,3072]{2,1,0:T(8,128)(2,1)}, u32[]{:S(2)}) copy-start(bf16[16,8,3072]{2,1,0:T(8,128)(2,1)} %param.6) | copy-start | bytes 2359300
  22.0 3.4 %collective-permute-start.9 = (bf16[16,1536]{1,0:T(8,128)(2,1)S(1)}, bf16[16,1536]{1,0:T(8,128)(2,1)S(1)}, u32[]{:S(2)}, u32[]{:S(2)}) collective-permute-start(bf16[16,1536]{1,0:T(8,128)(2,1)S(1)} %shard_map.67.refs_6_), channel_id=1, source_target_pairs={{0,1},{1,0},{2,3},{3,2},{4,5},{5,4},{6,7},{7,6},{8,9},{9,8},{10,11... | collective-permute-start | bytes 147464 | tf_op jit(solution)/shard_map/ppermute | solution.py:336
  25.4 14.2 %copy-start.3 = (bf16[16,4608]{1,0:T(8,128)(2,1)S(1)}, bf16[16,4608]{1,0:T(8,128)(2,1)}, u32[]{:S(2)}) copy-start(bf16[16,4608]{1,0:T(8,128)(2,1)} %value_ref.1) | copy-start | bytes 442372
  25.9 4.9 %collective-permute-start.10 = (bf16[32,1664]{1,0:T(8,128)(2,1)S(1)}, bf16[32,1664]{1,0:T(8,128)(2,1)S(1)}, u32[]{:S(2)}, u32[]{:S(2)}) collective-permute-start(bf16[32,1664]{1,0:T(8,128)(2,1)S(1)} %get-tuple-element.22), channel_id=1, source_target_pairs={{0,5},{1,4},{2,7},{3,6},{4,1},{5,0},{6,3},{7,2},{8,13},{9,12},{10,... | collective-permute-start | bytes 319496 | tf_op jit(solution)/shard_map/ppermute | solution.py:336
  30.8 4.7 %collective-permute-start.11 = (bf16[16,1664]{1,0:T(8,128)(2,1)S(1)}, bf16[16,1664]{1,0:T(8,128)(2,1)S(1)}, u32[]{:S(2)}, u32[]{:S(2)}) collective-permute-start(bf16[16,1664]{1,0:T(8,128)(2,1)S(1)} %get-tuple-element.26), channel_id=1, source_target_pairs={{0,9},{1,8},{2,11},{3,10},{4,13},{5,12},{6,15},{7,14},{8,1},{9,0},... | collective-permute-start | bytes 159752 | tf_op jit(solution)/shard_map/ppermute | solution.py:336
  35.5 4.0 %collective-permute-start.12 = (bf16[8,1664]{1,0:T(8,128)(2,1)S(1)}, bf16[8,1664]{1,0:T(8,128)(2,1)S(1)}, u32[]{:S(2)}, u32[]{:S(2)}) collective-permute-start(bf16[8,1664]{1,0:T(8,128)(2,1)S(1)} %get-tuple-element.27), channel_id=1, source_target_pairs={{0,3},{1,2},{2,1},{3,0},{4,7},{5,6},{6,5},{7,4},{8,11},{9,10},{10,... | collective-permute-start | bytes 79880 | tf_op jit(solution)/shard_map/ppermute | solution.py:336

commit v3 on v2

--- a/solution.py
+++ b/solution.py
@@ -130,11 +130,25 @@
     return (row == place).astype(jnp.bfloat16)
 
 
-def pack_kernel(query_ref, key_ref, parents_ref, keep_ref, send_ref):
+def pack_kernel(
+    new_ref, parents_hbm_ref, cache_ref, keep_ref, send_ref, other_ref, query_ref, key_ref, parents_ref, sems
+):
     rows, feature = query_ref.shape
+    other = 1 - class_of(lax.axis_index("utt").astype(jnp.int32))
+    slicing = pltpu.make_async_copy(cache_ref.at[:, other], other_ref, sems.at[3])
+    copies = [
+        pltpu.make_async_copy(new_ref.at[:, :feature], query_ref, sems.at[0]),
+        pltpu.make_async_copy(new_ref.at[:, feature : 2 * feature], key_ref, sems.at[1]),
+        pltpu.make_async_copy(parents_hbm_ref, parents_ref, sems.at[2]),
+    ]
+    for copy in copies:
+        copy.start()
+    slicing.start()
     half = rows // 2
     beams = parents_ref.shape[1]
     order = class_order(rows, lax.axis_index("utt"))
+    for copy in copies:
+        copy.wait()
     query = query_ref[...]
     product = query.astype(jnp.float32) * key_ref[...].astype(jnp.float32)
     lane = lax.broadcasted_iota(jnp.int32, (rows, LANES), 1)
@@ -158,10 +172,14 @@
         tile = jnp.dot(order, tile, preferred_element_type=jnp.float32)
         keep_ref[:, at : at + LANES] = tile[:half].astype(jnp.bfloat16)
         send_ref[:, at : at + LANES] = tile[half:].astype(jnp.bfloat16)
-
-
-def cross_weights_kernel(lengths_ref, query_ref, keys_ref, out_ref):
+    slicing.wait()
+
+
+def cross_weights_kernel(lengths_ref, query_ref, frames_ref, out_ref, keys_ref, sem):
     rows, feature = query_ref.shape
+    copy = pltpu.make_async_copy(frames_ref.at[:, :feature], keys_ref, sem)
+    copy.start()
+    copy.wait()
     frames = keys_ref.shape[0]
     heads = feature // HD
     live = lax.broadcasted_iota(jnp.int32, (rows, frames), 1) < lengths_ref[...]
@@ -180,7 +198,11 @@
         out_ref[head] = weights.astype(jnp.bfloat16)
 
 
-def cross_values_kernel(weights_ref, values_ref, out_ref):
+def cross_values_kernel(weights_ref, frames_ref, out_ref, values_ref, sem):
+    feature = values_ref.shape[1]
+    copy = pltpu.make_async_copy(frames_ref.at[:, feature:], values_ref, sem)
+    copy.start()
+    copy.wait()
     for head in range(weights_ref.shape[0]):
         at = slice(head * HD, (head + 1) * HD)
         out_ref[:, at] = jnp.dot(
@@ -199,7 +221,7 @@
 
 def self_weights_kernel(masks, counts, *refs):
     query_refs, refs = refs[:counts], refs[counts:]
-    *cache_refs, weight_ref, share_ref = refs
+    *cache_refs, weight_ref, share_ref, terms_ref, spread_ref = refs
     me = lax.axis_index("utt").astype(jnp.int32)
     mine = class_of(me)
     pair_keys, feature = cache_refs[-1].shape
@@ -209,18 +231,6 @@
     history = pair_keys // half_beams
     queries = jnp.concatenate([ref[...] for ref in query_refs], axis=0)
     extra = queries[:, feature:].astype(jnp.float32)
-
-    scores = []
-    for head in range(heads):
-        at = slice(head * HD, (head + 1) * HD)
-        scores.append(
-            lax.dot_general(
-                queries[:, at],
-                cached(*cache_refs, mine, at),
-                OVER_LAST,
-                preferred_element_type=jnp.float32,
-            )
-        )
 
     utt = utt_of_rank(lax.broadcasted_iota(jnp.int32, (half_beams, LANES), 0), me)
     lane = lax.broadcasted_iota(jnp.int32, (half_beams, LANES), 1)
@@ -247,23 +257,65 @@
     owner = me ^ jnp.where(
         run == 0, 0, jnp.where(run == 1, CORE, jnp.where(run == 2, PAIR, PAIR ^ CORE))
     )
-    bias = jnp.where((key_rank == row_rank) & (chosen == owner), 0.0, MASKED)
+    live = (key_rank == row_rank) & (chosen == owner)
     group = CORE | PAIR
     row_live = (chosen // (group + 1)) == (me // (group + 1))
 
-    own_all = extra + pltpu.roll(extra, LANES - heads, 1) + pltpu.roll(extra, LANES - 2 * heads, 1)
+    tiles = [slice(at, at + LANES) for at in range(0, keys, LANES)]
+    for head in range(heads):
+        at = slice(head * HD, (head + 1) * HD)
+        scores = lax.dot_general(
+            queries[:, at], cached(*cache_refs, mine, at), OVER_LAST, preferred_element_type=jnp.float32
+        )
+        scores = jnp.where(live, scores, 0.0)
+        rest = sum(scores[:, tile] for tile in tiles)
+        for term_at in range(3):
+            term = rest.astype(jnp.bfloat16)
+            rest = rest - term.astype(jnp.float32)
+            terms_ref[head * rows : (head + 1) * rows, term_at * LANES : (term_at + 1) * LANES] = term
     row_lane = lax.broadcasted_iota(jnp.int32, (rows, LANES), 1)
-    shares = jnp.zeros((rows, LANES), jnp.float32)
-    for head in range(heads):
-        masked = scores[head] * HD ** (-0.5) + bias
-        own = own_all[:, head : head + 1]
-        peak = jnp.maximum(jnp.max(masked, axis=1, keepdims=True), own)
-        raised = jnp.exp(masked - peak)
-        own = jnp.exp(own - peak)
-        share = 1.0 / (jnp.sum(raised, axis=1, keepdims=True) + own)
-        weight_ref[head] = (raised * share).astype(jnp.bfloat16)
-        shares = jnp.where(row_lane == head, own * share, shares)
-    share_ref[...] = jnp.where(row_live, shares, 0.0).astype(jnp.bfloat16)
+    fold = lax.broadcasted_iota(jnp.int32, (3 * LANES, LANES), 0) % history
+    fold = fold == lax.broadcasted_iota(jnp.int32, (3 * LANES, LANES), 1) % history
+    fold = fold.astype(jnp.bfloat16)
+    folded = jnp.dot(terms_ref[...], fold, preferred_element_type=jnp.float32)
+    packed = jnp.zeros((rows, LANES), jnp.float32)
+    for head in range(heads):
+        packed = jnp.where(
+            row_lane // history == head, folded[head * rows : (head + 1) * rows], packed
+        )
+    packed = packed * HD ** (-0.5)
+    part = lax.broadcasted_iota(jnp.int32, (LANES, LANES), 0)
+    spread = lax.broadcasted_iota(jnp.int32, (LANES, LANES), 1) // history
+    spread = (part < 3 * heads) & (part % heads == spread)
+    own = jnp.dot(
+        queries[:, feature:], spread.astype(jnp.bfloat16), preferred_element_type=jnp.float32
+    )
+
+    def over_tokens(tile, combine):
+        step = 1
+        while step < history:
+            left = pltpu.roll(tile, step, 1)
+            right = pltpu.roll(tile, LANES - step, 1)
+            tile = combine(tile, jnp.where(row_lane // step % 2 == 0, right, left))
+            step = 2 * step
+        return tile
+
+    peak = jnp.maximum(over_tokens(packed, jnp.maximum), own)
+    raised = jnp.exp(packed - peak)
+    own = jnp.exp(own - peak)
+    share = 1.0 / (over_tokens(raised, jnp.add) + own)
+    share_ref[...] = jnp.where(row_live, own * share, 0.0).astype(jnp.bfloat16)
+    packed = (raised * share).astype(jnp.bfloat16)
+    for head in range(heads):
+        spread_ref[head * rows : (head + 1) * rows] = jnp.where(
+            row_lane // history == head, packed, jnp.zeros_like(packed)
+        )
+    weights = jnp.dot(spread_ref[...], fold[:LANES], preferred_element_type=jnp.float32)
+    for head in range(heads):
+        for tile in tiles:
+            weight_ref[head, :, tile] = jnp.where(
+                live[:, tile], weights[head * rows : (head + 1) * rows], 0.0
+            ).astype(jnp.bfloat16)
 
 
 def self_values_kernel(masks, *refs):
@@ -298,7 +350,7 @@
         send_ref[:, at] = out[half:]
 
 
-def finish_kernel(mine_ref, came_ref, value_ref, out_ref):
+def finish_kernel(history, mine_ref, came_ref, value_ref, out_ref):
     rows, feature = out_ref.shape
     order = class_order(rows, lax.axis_index("utt"))
 
@@ -313,7 +365,7 @@
     shares = ordered(slice(feature, feature + LANES))
     for head in range(feature // HD):
         at = slice(head * HD, (head + 1) * HD)
-        out = ordered(at) + shares[:, head : head + 1] * value_ref[:, at].astype(jnp.float32)
+        out = ordered(at) + shares[:, head * history : head * history + 1] * value_ref[:, at].astype(jnp.float32)
         out_ref[:, at] = out.astype(jnp.bfloat16)
 
 
@@ -340,69 +392,74 @@
 
     hops = [(1 << k) | CORE for k in range(devices.bit_length() - 2, 1, -1)]
 
+    near = cache_kv.reshape(beams // (2 * CLASS), 2, CLASS * history, 2 * feature)
     half_rows = jax.ShapeDtypeStruct((rows // 2, width), jnp.bfloat16)
-    own, other = pl.pallas_call(
+    half_cache = jax.ShapeDtypeStruct(near.shape[:1] + near.shape[2:], jnp.bfloat16)
+    own, other, other_cache = pl.pallas_call(
         pack_kernel,
-        out_shape=(half_rows, half_rows),
+        out_shape=(half_rows, half_rows, half_cache),
+        in_specs=[pl.BlockSpec(memory_space=pltpu.HBM)] * 3,
+        out_specs=(whole(half_rows.shape), whole(half_rows.shape), whole(half_cache.shape)),
+        scratch_shapes=[
+            pltpu.VMEM((rows, feature), jnp.bfloat16),
+            pltpu.VMEM((rows, feature), jnp.bfloat16),
+            pltpu.VMEM(parents.shape, jnp.int32),
+            pltpu.SemaphoreType.DMA((4,)),
+        ],
+        compiler_params=params,
+    )(
+        pltpu.with_memory_space_constraint(new_rows, pltpu.HBM),
+        pltpu.with_memory_space_constraint(parents, pltpu.HBM),
+        pltpu.with_memory_space_constraint(near, pltpu.HBM),
+    )
+    pair_rows = swap(other, PAIR)
+    far = swap(near, CORE)
+    pair_near = swap(other_cache, PAIR).reshape(keys // 2, 2 * feature)
+
+    lists = jnp.pad(
+        swap(after(parents, other), CORE).astype(jnp.bfloat16),
+        ((0, 0), (feature + PARENT_LANE + beams, LANES - PARENT_LANE - 2 * beams)),
+    )
+    held = jnp.concatenate([own + lists, pair_rows], axis=0)
+    gathered, masks, held_masks = [held], [0], [0]
+
+    frames_kv = pltpu.with_memory_space_constraint(enc_kv.reshape(frames, 2 * feature), pltpu.HBM)
+    frames_scratch = [pltpu.VMEM((frames, feature), jnp.bfloat16), pltpu.SemaphoreType.DMA(())]
+    cross_weights = pl.pallas_call(
+        cross_weights_kernel,
+        out_shape=jax.ShapeDtypeStruct((heads, rows, frames), jnp.bfloat16),
         grid=(1,),
         in_specs=[
-            pl.BlockSpec((rows, feature), lambda i: (0, 0)),
-            pl.BlockSpec((rows, feature), lambda i: (0, 1)),
-            whole(parents.shape),
+            whole((1, 1)),
+            whole((rows, feature)),
+            pl.BlockSpec(memory_space=pltpu.HBM),
         ],
-        out_specs=(whole(half_rows.shape), whole(half_rows.shape)),
+        out_specs=whole((heads, rows, frames)),
+        scratch_shapes=frames_scratch,
         compiler_params=params,
-    )(new_rows, new_rows, parents)
-    pair_rows = swap(other, PAIR)
-
-    near = cache_kv.reshape(beams // (2 * CLASS), 2, CLASS * history, 2 * feature)
-    far = swap(near, CORE)
-    other_class = lax.dynamic_index_in_dim(near, 1 - class_of(me), 1, keepdims=False)
-    pair_keys = swap(other_class[..., :feature], PAIR).reshape(keys // 2, feature)
-    pair_values = swap(after(other_class[..., feature:], pair_rows), PAIR)
-    pair_values = pair_values.reshape(keys // 2, feature)
-
-    lists = jnp.pad(
-        swap(parents, CORE).astype(jnp.bfloat16),
-        ((0, 0), (feature + PARENT_LANE + beams, LANES - PARENT_LANE - 2 * beams)),
-    )
-    held = jnp.concatenate([own + lists, pair_rows], axis=0)
-    gathered, masks, held_masks = [held], [0], [0]
+    )(lengths.reshape(1, 1), after(cross_queries, held), frames_kv)
     for bits in hops:
         came = swap(held, bits)
         gathered.append(came)
         masks = masks + [mask ^ bits for mask in held_masks]
         held_masks = masks
         if bits != hops[-1]:
-            held = jnp.concatenate([held, came], axis=0)
-
-    weights = pl.pallas_call(
-        cross_weights_kernel,
-        out_shape=jax.ShapeDtypeStruct((heads, rows, frames), jnp.bfloat16),
-        grid=(1,),
-        in_specs=[
-            whole((1, 1)),
-            whole((rows, feature)),
-            pl.BlockSpec((frames, feature), lambda i: (0, 0)),
-        ],
-        out_specs=whole((heads, rows, frames)),
-        compiler_params=params,
-    )(lengths.reshape(1, 1), cross_queries, enc_kv.reshape(frames, 2 * feature))
+            held = after(jnp.concatenate([held, came], axis=0), cross_weights)
+
     cross_near = pl.pallas_call(
         cross_values_kernel,
         out_shape=jax.ShapeDtypeStruct((rows, feature), jnp.bfloat16),
         grid=(1,),
-        in_specs=[
-            whole((heads, rows, frames)),
-            pl.BlockSpec((frames, feature), lambda i: (0, 1)),
-        ],
+        in_specs=[whole((heads, rows, frames)), pl.BlockSpec(memory_space=pltpu.HBM)],
         out_specs=whole((rows, feature)),
+        scratch_shapes=frames_scratch,
         compiler_params=params,
-    )(weights, enc_kv.reshape(frames, 2 * feature))
+    )(after(cross_weights, held), frames_kv)
     cross_far = swap(cross_near, CORE)
 
+    pair_keys, pair_values = pair_near[:, :feature], pair_near[:, feature:]
     pair_far_keys = swap(after(pair_keys, held), CORE)
-    pair_far_values = swap(after(pair_values, gathered[-1]), CORE)
+    pair_far_values = swap(after(pair_values, gathered[-1], cross_near), CORE)
 
     all_rows = rows * len(masks)
     half = all_rows // 2
@@ -420,6 +477,10 @@
         in_specs=[whole(block.shape) for block in gathered]
         + [in_keys, in_keys, pair_spec, pair_spec],
         out_specs=(whole(weight_shape.shape), whole(share_shape.shape)),
+        scratch_shapes=[
+            pltpu.VMEM((heads * all_rows, 3 * LANES), jnp.bfloat16),
+            pltpu.VMEM((heads * all_rows, LANES), jnp.bfloat16),
+        ],
         compiler_params=params,
     )(*gathered, near, far, pair_keys, pair_far_keys)
     send, keep = pl.pallas_call(
@@ -441,7 +502,7 @@
     came = swap(send, PAIR)
 
     return pl.pallas_call(
-        finish_kernel,
+        functools.partial(finish_kernel, history),
         out_shape=jax.ShapeDtypeStruct((rows, feature), jnp.bfloat16),
         grid=(1,),
         in_specs=[
@@ -468,12 +529,15 @@
     def body(cache_kv, new_rows, cross_queries, enc_kv, lengths, parents):
         beams = parents.shape[1]
         heads = cross_queries.shape[1] // HD
+        history = cache_kv.shape[1]
         fits = (
             parents.shape[0] == 1
             and devices == beams
             and devices >= 8
             and devices & (devices - 1) == 0
             and beams % 16 == 0
+            and history & (history - 1) == 0
+            and heads * history <= LANES
             and 3 * heads <= PARENT_LANE
             and PARENT_LANE + 2 * beams <= LANES
         )

time: 40.9 us -> 34.6 us (0.85)
  waiting for transfers between devices: 16.3 us -> 10.6 us
  local copies, waits for them, and re-layouts: 2.75 us -> 0.93 us
  Pallas kernels: 5.29 us -> 6.86 us
    ppermute x13 -> x12, waiting for transfers between devices: 16.3 us -> 10.6 us  [swap(): return lax.ppermute(array, 'utt', [(i, i ^ bits) for i in range(devices)])]
    pallas_call x1, Pallas kernels: 2.95 us -> 1.39 us  [body_by_parent(): pl.pallas_call(functools.partial(self_weights_kernel, tuple(masks), len(g...]
    pallas_call x1, Pallas kernels: 0.23 us -> 1.36 us  [body_by_parent(): pl.pallas_call(cross_values_kernel, out_shape=jax.ShapeDtypeStruct((rows,...]
    pallas_call x1, Pallas kernels: 0.51 us -> 1.63 us  [body_by_parent(): pl.pallas_call(cross_weights_kernel, out_shape=jax.ShapeDtypeStruct((head...]
    squeeze x1 -> x0, local copies, waits for them, and re-layouts: 1.02 us -> none  [body_by_parent(): lax.dynamic_index_in_dim(near, 1 - class_of(me), 1, keepdims=False)]
    pallas_call x2, Pallas kernels: 1.18 us -> 2.05 us  [the longest x1 1.13 us: body_by_parent(): pl.pallas_call(pack_kernel, out_shape=(half_rows, half_rows, half_cache),...]
    unnamed x12 -> x6, local copies, waits for them, and re-layouts: 1.62 us -> 0.81 us
    ppermute x13 -> x12, starting transfers between devices: 15.3 us -> 15 us  [swap(): return lax.ppermute(array, 'utt', [(i, i ^ bits) for i in range(devices)])]
  transfers between devices with their start and end apart: 13 -> 12, of which waited for: 7 -> 6; matrix products, arithmetic and copies ran while one was open for 3% -> 0% of each run, Pallas kernels for 10% -> 13%
where the time goes in v3:
time: 34.6 us; the launch traced here: 34.2 us
  starting transfers between devices  15 us (43%)
  waiting for transfers between devices  10.6 us (31%)
  Pallas kernels  6.86 us (20%)
  local copies, waits for them, and re-layouts  0.93 us (3%)
  between operations  0.77 us (2%)
    ppermute x12, starting transfers between devices, swap(): return lax.ppermute(array, 'utt', [(i, i ^ bits) for i in range(devices)])  15 us
    ppermute x12, waiting for transfers between devices, swap(): return lax.ppermute(array, 'utt', [(i, i ^ bits) for i in range(devices)])  10.6 us
    pallas_call x1, Pallas kernels, body_by_parent(): pl.pallas_call(cross_weights_kernel, out_shape=jax.ShapeDtypeStruct((head...  1.63 us
    pallas_call x1, Pallas kernels, body_by_parent(): pl.pallas_call(functools.partial(self_weights_kernel, tuple(masks), len(g...  1.39 us
    pallas_call x1, Pallas kernels, body_by_parent(): pl.pallas_call(cross_values_kernel, out_shape=jax.ShapeDtypeStruct((rows,...  1.36 us
    pallas_call x1, Pallas kernels, body_by_parent(): pl.pallas_call(pack_kernel, out_shape=(half_rows, half_rows, half_cache),...  1.13 us
    pallas_call x1, Pallas kernels, body_by_parent(): pl.pallas_call(functools.partial(finish_kernel, history), out_shape=jax.S...  0.93 us
    unnamed x6, local copies, waits for them, and re-layouts  0.81 us
  transfers between devices with their start and end apart: 12, of which 6 were waited for; matrix products, arithmetic and copies ran while one was open for 0% of the time, Pallas kernels for 13%

profile of v3, /device:TPU:0, one launch (start us, length us, event | category | flops | bytes accessed | tf_op | source)
XLA Modules:
  0.0 34.2 jit_solution(5252038848175820566)
XLA Ops:
  0.0 1.1 %shard_map.64 = (bf16[8,1664]{1,0:T(8,128)(2,1)S(1)}, bf16[8,1664]{1,0:T(8,128)(2,1)S(1)}, bf16[4,16,3072]{2,1,0:T(8,128)(2,1)S(1)}) custom-call(bf16[16,4608]{1,0:T(8,128)(2,1)} %value_ref.1, s32[1,16]{1,0:T(1,128)} %parents_hbm_ref.1, bf16[4,2,16,3072]{3,2,1,0:T(8,128)(2,1)} %bitcast.5), custom_call_target="tpu_custom_call" | custom-call | tf_op jit(solution)/shard_map/pallas_call | solution.py:398
  1.1 2.5 %collective-permute-start.1 = (bf16[8,1664]{1,0:T(8,128)(2,1)S(1)}, bf16[8,1664]{1,0:T(8,128)(2,1)S(1)}, u32[]{:S(2)}, u32[]{:S(2)}) collective-permute-start(bf16[8,1664]{1,0:T(8,128)(2,1)S(1)} %get-tuple-element.19), channel_id=1, source_target_pairs={{0,3},{1,2},{2,1},{3,0},{4,7},{5,6},{6,5},{7,4},{8,11},{9,10},{10,... | collective-permute-start | bytes 79880 | tf_op jit(solution)/shard_map/ppermute | solution.py:388
  3.6 0.7 %collective-permute-start = (s32[1,16]{1,0:T(1,128)}, s32[1,16]{1,0:T(1,128)S(1)}, u32[]{:S(2)}, u32[]{:S(2)}) collective-permute-start(s32[1,16]{1,0:T(1,128)} %parents_hbm_ref.1), channel_id=1, source_target_pairs={{0,1},{1,0},{2,3},{3,2},{4,5},{5,4},{6,7},{7,6},{8,9},{9,8},{10,11... | collective-permute-start | bytes 200 | tf_op jit(solution)/shard_map/ppermute | solution.py:388
  4.4 0.9 %collective-permute-done = s32[1,16]{1,0:T(1,128)S(1)} collective-permute-done((s32[1,16]{1,0:T(1,128)}, s32[1,16]{1,0:T(1,128)S(1)}, u32[]{:S(2)}, u32[]{:S(2)}) %collective-permute-start) | collective-permute-done | bytes 96 | tf_op jit(solution)/shard_map/ppermute | solution.py:388
  5.4 3.1 %collective-permute-start.2 = (bf16[16,1664]{1,0:T(8,128)(2,1)S(1)}, bf16[16,1664]{1,0:T(8,128)(2,1)S(1)}, u32[]{:S(2)}, u32[]{:S(2)}) collective-permute-start(bf16[16,1664]{1,0:T(8,128)(2,1)S(1)} %pad_maximum_fusion.1.refs_0_), channel_id=1, source_target_pairs={{0,9},{1,8},{2,11},{3,10},{4,13},{5,12},{6,15},{7,14},{8,1},{9,0},... | collective-permute-start | bytes 159752 | tf_op jit(solution)/shard_map/ppermute | solution.py:388
  8.4 0.4 %collective-permute-start.4 = (bf16[4,2,16,3072]{3,2,1,0:T(8,128)(2,1)}, bf16[4,2,16,3072]{3,2,1,0:T(8,128)(2,1)S(1)}, u32[]{:S(2)}, u32[]{:S(2)}) collective-permute-start(bf16[4,2,16,3072]{3,2,1,0:T(8,128)(2,1)} %bitcast.6), channel_id=1, source_target_pairs={{0,1},{1,0},{2,3},{3,2},{4,5},{5,4},{6,7},{7,6},{8,9},{9,8},{10,11... | collective-permute-start | bytes 2359304 | tf_op jit(solution)/shard_map/ppermute | solution.py:388
  9.5 0.8 %copy-done.2 = bf16[16,1536]{1,0:T(8,128)(2,1)S(1)} copy-done((bf16[16,1536]{1,0:T(8,128)(2,1)S(1)}, bf16[16,1536]{1,0:T(8,128)(2,1)}, u32[]{:S(2)}) %copy-start.2) | copy-done | bytes 49176
  10.3 1.6 %shard_map.65.weights_ref = bf16[12,16,256]{2,1,0:T(8,128)(2,1)S(1)} custom-call(s32[1,1]{1,0:T(1,128)} %bitcast.4.lengths_ref, bf16[16,1536]{1,0:T(8,128)(2,1)S(1)} %copy-done.2, bf16[256,3072]{1,0:T(8,128)(2,1)} %bitcast.9), custom_call_target="tpu_custom_call" | custom-call | tf_op jit(solution)/shard_map/pallas_call | solution.py:428
  12.0 1.4 %collective-permute-start.3 = (bf16[32,1664]{1,0:T(8,128)(2,1)S(1)}, bf16[32,1664]{1,0:T(8,128)(2,1)S(1)}, u32[]{:S(2)}, u32[]{:S(2)}) collective-permute-start(bf16[32,1664]{1,0:T(8,128)(2,1)S(1)} %pad_maximum_fusion), channel_id=1, source_target_pairs={{0,5},{1,4},{2,7},{3,6},{4,1},{5,0},{6,3},{7,2},{8,13},{9,12},{10,... | collective-permute-start | bytes 319496 | tf_op jit(solution)/shard_map/ppermute | solution.py:388
  13.3 1.4 %shard_map.67.refs_6_ = bf16[16,1536]{1,0:T(8,128)(2,1)S(1)} custom-call(bf16[12,16,256]{2,1,0:T(8,128)(2,1)S(1)} %shard_map.65.weights_ref, bf16[256,3072]{1,0:T(8,128)(2,1)} %bitcast.10), custom_call_target="tpu_custom_call" | custom-call | tf_op jit(solution)/shard_map/pallas_call | solution.py:449
  14.7 0.8 %collective-permute-done.5 = bf16[4,16,3072]{2,1,0:T(8,128)(2,1)S(1)} collective-permute-done((bf16[4,16,3072]{2,1,0:T(8,128)(2,1)S(1)}, bf16[4,16,3072]{2,1,0:T(8,128)(2,1)S(1)}, u32[]{:S(2)}, u32[]{:S(2)}) %collective-permute-start.5) | collective-permute-done | bytes 393248 | tf_op jit(solution)/shard_map/ppermute | solution.py:388
  15.5 0.4 %collective-permute-start.6 = (bf16[64,1536]{1,0:T(8,128)(2,1)S(1)}, bf16[64,1536]{1,0:T(8,128)(2,1)S(1)}, u32[]{:S(2)}, u32[]{:S(2)}) collective-permute-start(bf16[64,1536]{1,0:T(8,128)(2,1)S(1)} %get-tuple-element.24.refs_5_), channel_id=1, source_target_pairs={{0,1},{1,0},{2,3},{3,2},{4,5},{5,4},{6,7},{7,6},{8,9},{9,8},{10,11... | collective-permute-start | bytes 589832 | tf_op jit(solution)/shard_map/ppermute | solution.py:388
  15.9 1.1 %collective-permute-done.3.refs_2_ = bf16[32,1664]{1,0:T(8,128)(2,1)S(1)} collective-permute-done((bf16[32,1664]{1,0:T(8,128)(2,1)S(1)}, bf16[32,1664]{1,0:T(8,128)(2,1)S(1)}, u32[]{:S(2)}, u32[]{:S(2)}) %collective-permute-start.3) | collective-permute-done | bytes 106528 | tf_op jit(solution)/shard_map/ppermute | solution.py:388
  17.0 0.1 collective-permute-start.7
  17.1 0.4 %collective-permute-start.8 = (bf16[16,1536]{1,0:T(8,128)(2,1)S(1)}, bf16[16,1536]{1,0:T(8,128)(2,1)S(1)}, u32[]{:S(2)}, u32[]{:S(2)}) collective-permute-start(bf16[16,1536]{1,0:T(8,128)(2,1)S(1)} %shard_map.67.refs_6_), channel_id=1, source_target_pairs={{0,1},{1,0},{2,3},{3,2},{4,5},{5,4},{6,7},{7,6},{8,9},{9,8},{10,11... | collective-permute-start | bytes 147464 | tf_op jit(solution)/shard_map/ppermute | solution.py:388
  17.5 1.4 %shard_map.66 = (bf16[12,64,256]{2,1,0:T(8,128)(2,1)S(1)}, bf16[64,128]{1,0:T(8,128)(2,1)S(1)}) custom-call(bf16[16,1664]{1,0:T(8,128)(2,1)S(1)} %pad_maximum_fusion.1.refs_0_, bf16[16,1664]{1,0:T(8,128)(2,1)S(1)} %collective-permute-done.2.refs_1_, bf16[32,1664]{1,0:T(8,128)(2,1)S(1)} %collective-permute-done.3.refs_2_, ...), custom_call_target="tpu_custom_call" | custom-call | tf_op jit(solution)/shard_map/pallas_call | solution.py:473
  19.0 0.4 %shard_map.68 = (bf16[32,1664]{1,0:T(8,128)(2,1)S(1)}, bf16[32,1664]{1,0:T(8,128)(2,1)S(1)}) custom-call(bf16[12,64,256]{2,1,0:T(8,128)(2,1)S(1)} %get-tuple-element.25.refs_0_, bf16[64,128]{1,0:T(8,128)(2,1)S(1)} %get-tuple-element.26.refs_1_, bf16[4,2,16,3072]{3,2,1,0:T(8,128)(2,1)S(1)} %bitcast.8, ...), custom_call_target="tpu_custom_call" | custom-call | tf_op jit(solution)/shard_map/pallas_call | solution.py:486
  19.4 1.4 %collective-permute-start.9 = (bf16[32,1664]{1,0:T(8,128)(2,1)S(1)}, bf16[32,1664]{1,0:T(8,128)(2,1)S(1)}, u32[]{:S(2)}, u32[]{:S(2)}) collective-permute-start(bf16[32,1664]{1,0:T(8,128)(2,1)S(1)} %get-tuple-element.30), channel_id=1, source_target_pairs={{0,5},{1,4},{2,7},{3,6},{4,1},{5,0},{6,3},{7,2},{8,13},{9,12},{10,... | collective-permute-start | bytes 319496 | tf_op jit(solution)/shard_map/ppermute | solution.py:388
  20.8 3.7 %collective-permute-done.9 = bf16[32,1664]{1,0:T(8,128)(2,1)S(1)} collective-permute-done((bf16[32,1664]{1,0:T(8,128)(2,1)S(1)}, bf16[32,1664]{1,0:T(8,128)(2,1)S(1)}, u32[]{:S(2)}, u32[]{:S(2)}) %collective-permute-start.9) | collective-permute-done | bytes 106528 | tf_op jit(solution)/shard_map/ppermute | solution.py:388
  24.5 2.1 %collective-permute-start.10 = (bf16[16,1664]{1,0:T(8,128)(2,1)S(1)}, bf16[16,1664]{1,0:T(8,128)(2,1)S(1)}, u32[]{:S(2)}, u32[]{:S(2)}) collective-permute-start(bf16[16,1664]{1,0:T(8,128)(2,1)S(1)} %get-tuple-element.34), channel_id=1, source_target_pairs={{0,9},{1,8},{2,11},{3,10},{4,13},{5,12},{6,15},{7,14},{8,1},{9,0},... | collective-permute-start | bytes 159752 | tf_op jit(solution)/shard_map/ppermute | solution.py:388
  26.6 2.6 %collective-permute-done.10 = bf16[16,1664]{1,0:T(8,128)(2,1)S(1)} collective-permute-done((bf16[16,1664]{1,0:T(8,128)(2,1)S(1)}, bf16[16,1664]{1,0:T(8,128)(2,1)S(1)}, u32[]{:S(2)}, u32[]{:S(2)}) %collective-permute-start.10) | collective-permute-done | bytes 53280 | tf_op jit(solution)/shard_map/ppermute | solution.py:388
  29.3 2.5 %collective-permute-start.11 = (bf16[8,1664]{1,0:T(8,128)(2,1)S(1)}, bf16[8,1664]{1,0:T(8,128)(2,1)S(1)}, u32[]{:S(2)}, u32[]{:S(2)}) collective-permute-start(bf16[8,1664]{1,0:T(8,128)(2,1)S(1)} %get-tuple-element.35), channel_id=1, source_target_pairs={{0,3},{1,2},{2,1},{3,0},{4,7},{5,6},{6,5},{7,4},{8,11},{9,10},{10,... | collective-permute-start | bytes 79880 | tf_op jit(solution)/shard_map/ppermute | solution.py:388
  31.8 1.5 %collective-permute-done.11.came_ref = bf16[8,1664]{1,0:T(8,128)(2,1)S(1)} collective-permute-done((bf16[8,1664]{1,0:T(8,128)(2,1)S(1)}, bf16[8,1664]{1,0:T(8,128)(2,1)S(1)}, u32[]{:S(2)}, u32[]{:S(2)}) %collective-permute-start.11) | collective-permute-done | bytes 26656 | tf_op jit(solution)/shard_map/ppermute | solution.py:388
  33.3 0.9 %shard_map.69 = bf16[16,1536]{1,0:T(8,128)(2,1)} custom-call(bf16[8,1664]{1,0:T(8,128)(2,1)S(1)} %get-tuple-element.36.mine_ref, bf16[8,1664]{1,0:T(8,128)(2,1)S(1)} %collective-permute-done.11.came_ref, bf16[16,4608]{1,0:T(8,128)(2,1)S(1)} %copy-done.1), custom_call_target="tpu_custom_call" | custom-call | tf_op jit(solution)/shard_map/pallas_call | solution.py:504
  (20 shorter events, 0.3 us)
Async XLA Ops:
  1.1 4.2 %collective-permute-start.1 = (bf16[8,1664]{1,0:T(8,128)(2,1)S(1)}, bf16[8,1664]{1,0:T(8,128)(2,1)S(1)}, u32[]{:S(2)}, u32[]{:S(2)}) collective-permute-start(bf16[8,1664]{1,0:T(8,128)(2,1)S(1)} %get-tuple-element.19), channel_id=1, source_target_pairs={{0,3},{1,2},{2,1},{3,0},{4,7},{5,6},{6,5},{7,4},{8,11},{9,10},{10,... | collective-permute-start | bytes 79880 | tf_op jit(solution)/shard_map/ppermute | solution.py:388
  3.6 1.6 %collective-permute-start = (s32[1,16]{1,0:T(1,128)}, s32[1,16]{1,0:T(1,128)S(1)}, u32[]{:S(2)}, u32[]{:S(2)}) collective-permute-start(s32[1,16]{1,0:T(1,128)} %parents_hbm_ref.1), channel_id=1, source_target_pairs={{0,1},{1,0},{2,3},{3,2},{4,5},{5,4},{6,7},{7,6},{8,9},{9,8},{10,11... | collective-permute-start | bytes 200 | tf_op jit(solution)/shard_map/ppermute | solution.py:388
  4.3 11.2 %collective-permute-start.5 = (bf16[4,16,3072]{2,1,0:T(8,128)(2,1)S(1)}, bf16[4,16,3072]{2,1,0:T(8,128)(2,1)S(1)}, u32[]{:S(2)}, u32[]{:S(2)}) collective-permute-start(bf16[4,16,3072]{2,1,0:T(8,128)(2,1)S(1)} %get-tuple-element.23), channel_id=1, source_target_pairs={{0,3},{1,2},{2,1},{3,0},{4,7},{5,6},{6,5},{7,4},{8,11},{9,10},{10,... | collective-permute-start | bytes 1179656 | tf_op jit(solution)/shard_map/ppermute | solution.py:388
  5.4 6.6 %collective-permute-start.2 = (bf16[16,1664]{1,0:T(8,128)(2,1)S(1)}, bf16[16,1664]{1,0:T(8,128)(2,1)S(1)}, u32[]{:S(2)}, u32[]{:S(2)}) collective-permute-start(bf16[16,1664]{1,0:T(8,128)(2,1)S(1)} %pad_maximum_fusion.1.refs_0_), channel_id=1, source_target_pairs={{0,9},{1,8},{2,11},{3,10},{4,13},{5,12},{6,15},{7,14},{8,1},{9,0},... | collective-permute-start | bytes 159752 | tf_op jit(solution)/shard_map/ppermute | solution.py:388
  8.4 9.1 %collective-permute-start.4 = (bf16[4,2,16,3072]{3,2,1,0:T(8,128)(2,1)}, bf16[4,2,16,3072]{3,2,1,0:T(8,128)(2,1)S(1)}, u32[]{:S(2)}, u32[]{:S(2)}) collective-permute-start(bf16[4,2,16,3072]{3,2,1,0:T(8,128)(2,1)} %bitcast.6), channel_id=1, source_target_pairs={{0,1},{1,0},{2,3},{3,2},{4,5},{5,4},{6,7},{7,6},{8,9},{9,8},{10,11... | collective-permute-start | bytes 2359304 | tf_op jit(solution)/shard_map/ppermute | solution.py:388
  9.5 0.8 %copy-start.2 = (bf16[16,1536]{1,0:T(8,128)(2,1)S(1)}, bf16[16,1536]{1,0:T(8,128)(2,1)}, u32[]{:S(2)}) copy-start(bf16[16,1536]{1,0:T(8,128)(2,1)} %query_ref) | copy-start | bytes 147460
  11.9 5.6 %copy-start = (bf16[16,8,3072]{2,1,0:T(8,128)(2,1)S(1)}, bf16[16,8,3072]{2,1,0:T(8,128)(2,1)}, u32[]{:S(2)}) copy-start(bf16[16,8,3072]{2,1,0:T(8,128)(2,1)} %param.6) | copy-start | bytes 2359300
  12.0 5.0 %collective-permute-start.3 = (bf16[32,1664]{1,0:T(8,128)(2,1)S(1)}, bf16[32,1664]{1,0:T(8,128)(2,1)S(1)}, u32[]{:S(2)}, u32[]{:S(2)}) collective-permute-start(bf16[32,1664]{1,0:T(8,128)(2,1)S(1)} %pad_maximum_fusion), channel_id=1, source_target_pairs={{0,5},{1,4},{2,7},{3,6},{4,1},{5,0},{6,3},{7,2},{8,13},{9,12},{10,... | collective-permute-start | bytes 319496 | tf_op jit(solution)/shard_map/ppermute | solution.py:388
  15.5 2.0 %collective-permute-start.6 = (bf16[64,1536]{1,0:T(8,128)(2,1)S(1)}, bf16[64,1536]{1,0:T(8,128)(2,1)S(1)}, u32[]{:S(2)}, u32[]{:S(2)}) collective-permute-start(bf16[64,1536]{1,0:T(8,128)(2,1)S(1)} %get-tuple-element.24.refs_5_), channel_id=1, source_target_pairs={{0,1},{1,0},{2,3},{3,2},{4,5},{5,4},{6,7},{7,6},{8,9},{9,8},{10,11... | collective-permute-start | bytes 589832 | tf_op jit(solution)/shard_map/ppermute | solution.py:388
  17.0 1.9 %collective-permute-start.7 = (bf16[64,1536]{1,0:T(8,128)(2,1)S(1)}, bf16[64,1536]{1,0:T(8,128)(2,1)S(1)}, u32[]{:S(2)}, u32[]{:S(2)}) collective-permute-start(bf16[64,1536]{1,0:T(8,128)(2,1)S(1)} %get-tuple-element.28.refs_4_), channel_id=1, source_target_pairs={{0,1},{1,0},{2,3},{3,2},{4,5},{5,4},{6,7},{7,6},{8,9},{9,8},{10,11... | collective-permute-start | bytes 589832 | tf_op jit(solution)/shard_map/ppermute | solution.py:388
  17.1 1.8 %collective-permute-start.8 = (bf16[16,1536]{1,0:T(8,128)(2,1)S(1)}, bf16[16,1536]{1,0:T(8,128)(2,1)S(1)}, u32[]{:S(2)}, u32[]{:S(2)}) collective-permute-start(bf16[16,1536]{1,0:T(8,128)(2,1)S(1)} %shard_map.67.refs_6_), channel_id=1, source_target_pairs={{0,1},{1,0},{2,3},{3,2},{4,5},{5,4},{6,7},{7,6},{8,9},{9,8},{10,11... | collective-permute-start | bytes 147464 | tf_op jit(solution)/shard_map/ppermute | solution.py:388
  18.9 14.4 %copy-start.1 = (bf16[16,4608]{1,0:T(8,128)(2,1)S(1)}, bf16[16,4608]{1,0:T(8,128)(2,1)}, u32[]{:S(2)}) copy-start(bf16[16,4608]{1,0:T(8,128)(2,1)} %value_ref.1) | copy-start | bytes 442372
  19.4 5.0 %collective-permute-start.9 = (bf16[32,1664]{1,0:T(8,128)(2,1)S(1)}, bf16[32,1664]{1,0:T(8,128)(2,1)S(1)}, u32[]{:S(2)}, u32[]{:S(2)}) collective-permute-start(bf16[32,1664]{1,0:T(8,128)(2,1)S(1)} %get-tuple-element.30), channel_id=1, source_target_pairs={{0,5},{1,4},{2,7},{3,6},{4,1},{5,0},{6,3},{7,2},{8,13},{9,12},{10,... | collective-permute-start | bytes 319496 | tf_op jit(solution)/shard_map/ppermute | solution.py:388
  24.5 4.8 %collective-permute-start.10 = (bf16[16,1664]{1,0:T(8,128)(2,1)S(1)}, bf16[16,1664]{1,0:T(8,128)(2,1)S(1)}, u32[]{:S(2)}, u32[]{:S(2)}) collective-permute-start(bf16[16,1664]{1,0:T(8,128)(2,1)S(1)} %get-tuple-element.34), channel_id=1, source_target_pairs={{0,9},{1,8},{2,11},{3,10},{4,13},{5,12},{6,15},{7,14},{8,1},{9,0},... | collective-permute-start | bytes 159752 | tf_op jit(solution)/shard_map/ppermute | solution.py:388
  29.3 4.1 %collective-permute-start.11 = (bf16[8,1664]{1,0:T(8,128)(2,1)S(1)}, bf16[8,1664]{1,0:T(8,128)(2,1)S(1)}, u32[]{:S(2)}, u32[]{:S(2)}) collective-permute-start(bf16[8,1664]{1,0:T(8,128)(2,1)S(1)} %get-tuple-element.35), channel_id=1, source_target_pairs={{0,3},{1,2},{2,1},{3,0},{4,7},{5,6},{6,5},{7,4},{8,11},{9,10},{10,... | collective-permute-start | bytes 79880 | tf_op jit(solution)/shard_map/ppermute | solution.py:388

commit v4 on v3

--- a/solution.py
+++ b/solution.py
@@ -175,14 +175,21 @@
     slicing.wait()
 
 
-def cross_weights_kernel(lengths_ref, query_ref, frames_ref, out_ref, keys_ref, sem):
+def cross_weights_kernel(
+    lengths_ref, query_hbm_ref, frames_ref, out_ref, query_ref, keys_ref, sems
+):
     rows, feature = query_ref.shape
-    copy = pltpu.make_async_copy(frames_ref.at[:, :feature], keys_ref, sem)
-    copy.start()
-    copy.wait()
+    copies = [
+        pltpu.make_async_copy(frames_ref.at[:, :feature], keys_ref, sems.at[0]),
+        pltpu.make_async_copy(query_hbm_ref, query_ref, sems.at[1]),
+    ]
+    for copy in copies:
+        copy.start()
+    for copy in copies:
+        copy.wait()
     frames = keys_ref.shape[0]
     heads = feature // HD
-    live = lax.broadcasted_iota(jnp.int32, (rows, frames), 1) < lengths_ref[...]
+    live = lax.broadcasted_iota(jnp.int32, (rows, frames), 1) < lengths_ref[:, :1]
     scores = []
     for head in range(heads):
         at = slice(head * HD, (head + 1) * HD)
@@ -390,6 +397,9 @@
     def after(array, *others):
         return lax.optimization_barrier((array,) + others)[0]
 
+    def in_hbm(array):
+        return pltpu.with_memory_space_constraint(array, pltpu.HBM)
+
     hops = [(1 << k) | CORE for k in range(devices.bit_length() - 2, 1, -1)]
 
     near = cache_kv.reshape(beams // (2 * CLASS), 2, CLASS * history, 2 * feature)
@@ -408,9 +418,9 @@
         ],
         compiler_params=params,
     )(
-        pltpu.with_memory_space_constraint(new_rows, pltpu.HBM),
-        pltpu.with_memory_space_constraint(parents, pltpu.HBM),
-        pltpu.with_memory_space_constraint(near, pltpu.HBM),
+        in_hbm(new_rows),
+        in_hbm(parents),
+        in_hbm(near),
     )
     pair_rows = swap(other, PAIR)
     far = swap(near, CORE)
@@ -420,24 +430,23 @@
         swap(after(parents, other), CORE).astype(jnp.bfloat16),
         ((0, 0), (feature + PARENT_LANE + beams, LANES - PARENT_LANE - 2 * beams)),
     )
-    held = jnp.concatenate([own + lists, pair_rows], axis=0)
+    frame_count = jnp.broadcast_to(lengths.reshape(1, 1), (1, LANES))
+    held = after(jnp.concatenate([own + lists, pair_rows], axis=0), frame_count)
     gathered, masks, held_masks = [held], [0], [0]
 
-    frames_kv = pltpu.with_memory_space_constraint(enc_kv.reshape(frames, 2 * feature), pltpu.HBM)
-    frames_scratch = [pltpu.VMEM((frames, feature), jnp.bfloat16), pltpu.SemaphoreType.DMA(())]
+    frames_kv = in_hbm(enc_kv.reshape(frames, 2 * feature))
     cross_weights = pl.pallas_call(
         cross_weights_kernel,
         out_shape=jax.ShapeDtypeStruct((heads, rows, frames), jnp.bfloat16),
-        grid=(1,),
-        in_specs=[
-            whole((1, 1)),
-            whole((rows, feature)),
-            pl.BlockSpec(memory_space=pltpu.HBM),
+        in_specs=[whole((1, LANES))] + [pl.BlockSpec(memory_space=pltpu.HBM)] * 2,
+        out_specs=whole((heads, rows, frames)),
+        scratch_shapes=[
+            pltpu.VMEM((rows, feature), jnp.bfloat16),
+            pltpu.VMEM((frames, feature), jnp.bfloat16),
+            pltpu.SemaphoreType.DMA((2,)),
         ],
-        out_specs=whole((heads, rows, frames)),
-        scratch_shapes=frames_scratch,
         compiler_params=params,
-    )(lengths.reshape(1, 1), after(cross_queries, held), frames_kv)
+    )(frame_count, in_hbm(after(cross_queries, held)), frames_kv)
     for bits in hops:
         came = swap(held, bits)
         gathered.append(came)
@@ -452,7 +461,10 @@
         grid=(1,),
         in_specs=[whole((heads, rows, frames)), pl.BlockSpec(memory_space=pltpu.HBM)],
         out_specs=whole((rows, feature)),
-        scratch_shapes=frames_scratch,
+        scratch_shapes=[
+            pltpu.VMEM((frames, feature), jnp.bfloat16),
+            pltpu.SemaphoreType.DMA(()),
+        ],
         compiler_params=params,
     )(after(cross_weights, held), frames_kv)
     cross_far = swap(cross_near, CORE)

time: 34.6 us -> 33.6 us (0.971)
  waiting for transfers between devices: 10.6 us -> 9.56 us
  local copies, waits for them, and re-layouts: 0.93 us -> 0.13 us
  starting transfers between devices: 15 us -> 15.6 us
    ppermute x12, waiting for transfers between devices: 10.6 us -> 9.56 us  [swap(): return lax.ppermute(array, 'utt', [(i, i ^ bits) for i in range(devices)])]
    unnamed x6 -> x4, local copies, waits for them, and re-layouts: 0.81 us -> 0.01 us
    ppermute x12, starting transfers between devices: 15 us -> 15.6 us  [swap(): return lax.ppermute(array, 'utt', [(i, i ^ bits) for i in range(devices)])]
where the time goes in v4:
time: 33.6 us; the launch traced here: 33 us
  starting transfers between devices  15.6 us (46%)
  waiting for transfers between devices  9.56 us (28%)
  Pallas kernels  6.87 us (20%)
  between operations  0.78 us (2%)
    ppermute x12, starting transfers between devices, swap(): return lax.ppermute(array, 'utt', [(i, i ^ bits) for i in range(devices)])  15.6 us
    ppermute x12, waiting for transfers between devices, swap(): return lax.ppermute(array, 'utt', [(i, i ^ bits) for i in range(devices)])  9.56 us
    pallas_call x1, Pallas kernels, body_by_parent(): pl.pallas_call(cross_weights_kernel, out_shape=jax.ShapeDtypeStruct((head...  1.64 us
    pallas_call x1, Pallas kernels, body_by_parent(): pl.pallas_call(functools.partial(self_weights_kernel, tuple(masks), len(g...  1.39 us
    pallas_call x1, Pallas kernels, body_by_parent(): pl.pallas_call(cross_values_kernel, out_shape=jax.ShapeDtypeStruct((rows,...  1.36 us
    pallas_call x1, Pallas kernels, body_by_parent(): pl.pallas_call(pack_kernel, out_shape=(half_rows, half_rows, half_cache),...  1.13 us
    pallas_call x1, Pallas kernels, body_by_parent(): pl.pallas_call(functools.partial(finish_kernel, history), out_shape=jax.S...  0.92 us
  transfers between devices with their start and end apart: 12, of which 6 were waited for; matrix products, arithmetic and copies ran while one was open for 0% of the time, Pallas kernels for 13%

profile of v4, /device:TPU:0, one launch (start us, length us, event | category | flops | bytes accessed | tf_op | source)
XLA Modules:
  0.0 33.0 jit_solution(16510537615961987606)
XLA Ops:
  0.0 1.1 %shard_map.64 = (bf16[8,1664]{1,0:T(8,128)(2,1)S(1)}, bf16[8,1664]{1,0:T(8,128)(2,1)S(1)}, bf16[4,16,3072]{2,1,0:T(8,128)(2,1)S(1)}) custom-call(bf16[16,4608]{1,0:T(8,128)(2,1)} %value_ref.1, s32[1,16]{1,0:T(1,128)} %parents_hbm_ref.1, bf16[4,2,16,3072]{3,2,1,0:T(8,128)(2,1)} %bitcast.5), custom_call_target="tpu_custom_call" | custom-call | tf_op jit(solution)/shard_map/pallas_call | solution.py:408
  1.1 2.5 %collective-permute-start.1 = (bf16[8,1664]{1,0:T(8,128)(2,1)S(1)}, bf16[8,1664]{1,0:T(8,128)(2,1)S(1)}, u32[]{:S(2)}, u32[]{:S(2)}) collective-permute-start(bf16[8,1664]{1,0:T(8,128)(2,1)S(1)} %get-tuple-element.20), channel_id=1, source_target_pairs={{0,3},{1,2},{2,1},{3,0},{4,7},{5,6},{6,5},{7,4},{8,11},{9,10},{10,... | collective-permute-start | bytes 79880 | tf_op jit(solution)/shard_map/ppermute | solution.py:395
  3.6 0.7 %collective-permute-start = (s32[1,16]{1,0:T(1,128)}, s32[1,16]{1,0:T(1,128)S(1)}, u32[]{:S(2)}, u32[]{:S(2)}) collective-permute-start(s32[1,16]{1,0:T(1,128)} %parents_hbm_ref.1), channel_id=1, source_target_pairs={{0,1},{1,0},{2,3},{3,2},{4,5},{5,4},{6,7},{7,6},{8,9},{9,8},{10,11... | collective-permute-start | bytes 200 | tf_op jit(solution)/shard_map/ppermute | solution.py:395
  5.0 0.2 collective-permute-done
  5.2 0.1 pad_reduce_fusion
  5.4 3.1 %collective-permute-start.2 = (bf16[16,1664]{1,0:T(8,128)(2,1)S(1)}, bf16[16,1664]{1,0:T(8,128)(2,1)S(1)}, u32[]{:S(2)}, u32[]{:S(2)}) collective-permute-start(bf16[16,1664]{1,0:T(8,128)(2,1)S(1)} %pad_maximum_fusion.1.refs_0_), channel_id=1, source_target_pairs={{0,9},{1,8},{2,11},{3,10},{4,13},{5,12},{6,15},{7,14},{8,1},{9,0},... | collective-permute-start | bytes 159752 | tf_op jit(solution)/shard_map/ppermute | solution.py:395
  8.5 0.4 %collective-permute-start.4 = (bf16[4,2,16,3072]{3,2,1,0:T(8,128)(2,1)}, bf16[4,2,16,3072]{3,2,1,0:T(8,128)(2,1)S(1)}, u32[]{:S(2)}, u32[]{:S(2)}) collective-permute-start(bf16[4,2,16,3072]{3,2,1,0:T(8,128)(2,1)} %bitcast.6), channel_id=1, source_target_pairs={{0,1},{1,0},{2,3},{3,2},{4,5},{5,4},{6,7},{7,6},{8,9},{9,8},{10,11... | collective-permute-start | bytes 2359304 | tf_op jit(solution)/shard_map/ppermute | solution.py:395
  8.9 1.6 %shard_map.65.weights_ref = bf16[12,16,256]{2,1,0:T(8,128)(2,1)S(1)} custom-call(s32[1,128]{1,0:T(1,128)S(1)} %broadcast_in_dim.8.lengths_ref, bf16[16,1536]{1,0:T(8,128)(2,1)} %query_hbm_ref, bf16[256,3072]{1,0:T(8,128)(2,1)} %bitcast.9), custom_call_target="tpu_custom_call" | custom-call | tf_op jit(solution)/shard_map/pallas_call | solution.py:438
  10.6 2.2 %collective-permute-start.3 = (bf16[32,1664]{1,0:T(8,128)(2,1)S(1)}, bf16[32,1664]{1,0:T(8,128)(2,1)S(1)}, u32[]{:S(2)}, u32[]{:S(2)}) collective-permute-start(bf16[32,1664]{1,0:T(8,128)(2,1)S(1)} %pad_maximum_fusion), channel_id=1, source_target_pairs={{0,5},{1,4},{2,7},{3,6},{4,1},{5,0},{6,3},{7,2},{8,13},{9,12},{10,... | collective-permute-start | bytes 319496 | tf_op jit(solution)/shard_map/ppermute | solution.py:395
  12.8 1.4 %shard_map.67.refs_6_ = bf16[16,1536]{1,0:T(8,128)(2,1)S(1)} custom-call(bf16[12,16,256]{2,1,0:T(8,128)(2,1)S(1)} %shard_map.65.weights_ref, bf16[256,3072]{1,0:T(8,128)(2,1)} %bitcast.10), custom_call_target="tpu_custom_call" | custom-call | tf_op jit(solution)/shard_map/pallas_call | solution.py:458
  14.2 1.3 %collective-permute-done.5 = bf16[4,16,3072]{2,1,0:T(8,128)(2,1)S(1)} collective-permute-done((bf16[4,16,3072]{2,1,0:T(8,128)(2,1)S(1)}, bf16[4,16,3072]{2,1,0:T(8,128)(2,1)S(1)}, u32[]{:S(2)}, u32[]{:S(2)}) %collective-permute-start.5) | collective-permute-done | bytes 393248 | tf_op jit(solution)/shard_map/ppermute | solution.py:395
  15.5 0.4 %collective-permute-start.6 = (bf16[64,1536]{1,0:T(8,128)(2,1)S(1)}, bf16[64,1536]{1,0:T(8,128)(2,1)S(1)}, u32[]{:S(2)}, u32[]{:S(2)}) collective-permute-start(bf16[64,1536]{1,0:T(8,128)(2,1)S(1)} %get-tuple-element.26.refs_5_), channel_id=1, source_target_pairs={{0,1},{1,0},{2,3},{3,2},{4,5},{5,4},{6,7},{7,6},{8,9},{9,8},{10,11... | collective-permute-start | bytes 589832 | tf_op jit(solution)/shard_map/ppermute | solution.py:395
  15.9 0.2 collective-permute-start.7
  16.2 0.3 collective-permute-start.8
  16.4 0.6 %collective-permute-done.6.refs_6_ = bf16[64,1536]{1,0:T(8,128)(2,1)S(1)} collective-permute-done((bf16[64,1536]{1,0:T(8,128)(2,1)S(1)}, bf16[64,1536]{1,0:T(8,128)(2,1)S(1)}, u32[]{:S(2)}, u32[]{:S(2)}) %collective-permute-start.6) | collective-permute-done | bytes 196640 | tf_op jit(solution)/shard_map/ppermute | solution.py:395
  17.1 1.4 %shard_map.66 = (bf16[12,64,256]{2,1,0:T(8,128)(2,1)S(1)}, bf16[64,128]{1,0:T(8,128)(2,1)S(1)}) custom-call(bf16[16,1664]{1,0:T(8,128)(2,1)S(1)} %pad_maximum_fusion.1.refs_0_, bf16[16,1664]{1,0:T(8,128)(2,1)S(1)} %collective-permute-done.2.refs_1_, bf16[32,1664]{1,0:T(8,128)(2,1)S(1)} %collective-permute-done.3.refs_2_, ...), custom_call_target="tpu_custom_call" | custom-call | tf_op jit(solution)/shard_map/pallas_call | solution.py:485
  18.5 0.4 %shard_map.68 = (bf16[32,1664]{1,0:T(8,128)(2,1)S(1)}, bf16[32,1664]{1,0:T(8,128)(2,1)S(1)}) custom-call(bf16[12,64,256]{2,1,0:T(8,128)(2,1)S(1)} %get-tuple-element.27.refs_0_, bf16[64,128]{1,0:T(8,128)(2,1)S(1)} %get-tuple-element.28.refs_1_, bf16[4,2,16,3072]{3,2,1,0:T(8,128)(2,1)S(1)} %bitcast.8, ...), custom_call_target="tpu_custom_call" | custom-call | tf_op jit(solution)/shard_map/pallas_call | solution.py:498
  18.9 1.5 %collective-permute-start.9 = (bf16[32,1664]{1,0:T(8,128)(2,1)S(1)}, bf16[32,1664]{1,0:T(8,128)(2,1)S(1)}, u32[]{:S(2)}, u32[]{:S(2)}) collective-permute-start(bf16[32,1664]{1,0:T(8,128)(2,1)S(1)} %get-tuple-element.32), channel_id=1, source_target_pairs={{0,5},{1,4},{2,7},{3,6},{4,1},{5,0},{6,3},{7,2},{8,13},{9,12},{10,... | collective-permute-start | bytes 319496 | tf_op jit(solution)/shard_map/ppermute | solution.py:395
  20.5 3.4 %collective-permute-done.9 = bf16[32,1664]{1,0:T(8,128)(2,1)S(1)} collective-permute-done((bf16[32,1664]{1,0:T(8,128)(2,1)S(1)}, bf16[32,1664]{1,0:T(8,128)(2,1)S(1)}, u32[]{:S(2)}, u32[]{:S(2)}) %collective-permute-start.9) | collective-permute-done | bytes 106528 | tf_op jit(solution)/shard_map/ppermute | solution.py:395
  23.9 2.8 %collective-permute-start.10 = (bf16[16,1664]{1,0:T(8,128)(2,1)S(1)}, bf16[16,1664]{1,0:T(8,128)(2,1)S(1)}, u32[]{:S(2)}, u32[]{:S(2)}) collective-permute-start(bf16[16,1664]{1,0:T(8,128)(2,1)S(1)} %get-tuple-element.36), channel_id=1, source_target_pairs={{0,9},{1,8},{2,11},{3,10},{4,13},{5,12},{6,15},{7,14},{8,1},{9,0},... | collective-permute-start | bytes 159752 | tf_op jit(solution)/shard_map/ppermute | solution.py:395
  26.7 2.1 %collective-permute-done.10 = bf16[16,1664]{1,0:T(8,128)(2,1)S(1)} collective-permute-done((bf16[16,1664]{1,0:T(8,128)(2,1)S(1)}, bf16[16,1664]{1,0:T(8,128)(2,1)S(1)}, u32[]{:S(2)}, u32[]{:S(2)}) %collective-permute-start.10) | collective-permute-done | bytes 53280 | tf_op jit(solution)/shard_map/ppermute | solution.py:395
  28.7 1.4 %collective-permute-start.11 = (bf16[8,1664]{1,0:T(8,128)(2,1)S(1)}, bf16[8,1664]{1,0:T(8,128)(2,1)S(1)}, u32[]{:S(2)}, u32[]{:S(2)}) collective-permute-start(bf16[8,1664]{1,0:T(8,128)(2,1)S(1)} %get-tuple-element.37), channel_id=1, source_target_pairs={{0,3},{1,2},{2,1},{3,0},{4,7},{5,6},{6,5},{7,4},{8,11},{9,10},{10,... | collective-permute-start | bytes 79880 | tf_op jit(solution)/shard_map/ppermute | solution.py:395
  30.1 1.9 %collective-permute-done.11.came_ref = bf16[8,1664]{1,0:T(8,128)(2,1)S(1)} collective-permute-done((bf16[8,1664]{1,0:T(8,128)(2,1)S(1)}, bf16[8,1664]{1,0:T(8,128)(2,1)S(1)}, u32[]{:S(2)}, u32[]{:S(2)}) %collective-permute-start.11) | collective-permute-done | bytes 26656 | tf_op jit(solution)/shard_map/ppermute | solution.py:395
  32.1 0.9 %shard_map.69 = bf16[16,1536]{1,0:T(8,128)(2,1)} custom-call(bf16[8,1664]{1,0:T(8,128)(2,1)S(1)} %get-tuple-element.38.mine_ref, bf16[8,1664]{1,0:T(8,128)(2,1)S(1)} %collective-permute-done.11.came_ref, bf16[16,4608]{1,0:T(8,128)(2,1)S(1)} %copy-done.1), custom_call_target="tpu_custom_call" | custom-call | tf_op jit(solution)/shard_map/pallas_call | solution.py:516
  (19 shorter events, 0.2 us)
Async XLA Ops:
  1.1 4.2 %collective-permute-start.1 = (bf16[8,1664]{1,0:T(8,128)(2,1)S(1)}, bf16[8,1664]{1,0:T(8,128)(2,1)S(1)}, u32[]{:S(2)}, u32[]{:S(2)}) collective-permute-start(bf16[8,1664]{1,0:T(8,128)(2,1)S(1)} %get-tuple-element.20), channel_id=1, source_target_pairs={{0,3},{1,2},{2,1},{3,0},{4,7},{5,6},{6,5},{7,4},{8,11},{9,10},{10,... | collective-permute-start | bytes 79880 | tf_op jit(solution)/shard_map/ppermute | solution.py:395
  3.6 1.6 %collective-permute-start = (s32[1,16]{1,0:T(1,128)}, s32[1,16]{1,0:T(1,128)S(1)}, u32[]{:S(2)}, u32[]{:S(2)}) collective-permute-start(s32[1,16]{1,0:T(1,128)} %parents_hbm_ref.1), channel_id=1, source_target_pairs={{0,1},{1,0},{2,3},{3,2},{4,5},{5,4},{6,7},{7,6},{8,9},{9,8},{10,11... | collective-permute-start | bytes 200 | tf_op jit(solution)/shard_map/ppermute | solution.py:395
  4.3 11.2 %collective-permute-start.5 = (bf16[4,16,3072]{2,1,0:T(8,128)(2,1)S(1)}, bf16[4,16,3072]{2,1,0:T(8,128)(2,1)S(1)}, u32[]{:S(2)}, u32[]{:S(2)}) collective-permute-start(bf16[4,16,3072]{2,1,0:T(8,128)(2,1)S(1)} %get-tuple-element.25), channel_id=1, source_target_pairs={{0,3},{1,2},{2,1},{3,0},{4,7},{5,6},{6,5},{7,4},{8,11},{9,10},{10,... | collective-permute-start | bytes 1179656 | tf_op jit(solution)/shard_map/ppermute | solution.py:395
  5.4 5.2 %collective-permute-start.2 = (bf16[16,1664]{1,0:T(8,128)(2,1)S(1)}, bf16[16,1664]{1,0:T(8,128)(2,1)S(1)}, u32[]{:S(2)}, u32[]{:S(2)}) collective-permute-start(bf16[16,1664]{1,0:T(8,128)(2,1)S(1)} %pad_maximum_fusion.1.refs_0_), channel_id=1, source_target_pairs={{0,9},{1,8},{2,11},{3,10},{4,13},{5,12},{6,15},{7,14},{8,1},{9,0},... | collective-permute-start | bytes 159752 | tf_op jit(solution)/shard_map/ppermute | solution.py:395
  8.5 8.5 %collective-permute-start.4 = (bf16[4,2,16,3072]{3,2,1,0:T(8,128)(2,1)}, bf16[4,2,16,3072]{3,2,1,0:T(8,128)(2,1)S(1)}, u32[]{:S(2)}, u32[]{:S(2)}) collective-permute-start(bf16[4,2,16,3072]{3,2,1,0:T(8,128)(2,1)} %bitcast.6), channel_id=1, source_target_pairs={{0,1},{1,0},{2,3},{3,2},{4,5},{5,4},{6,7},{7,6},{8,9},{9,8},{10,11... | collective-permute-start | bytes 2359304 | tf_op jit(solution)/shard_map/ppermute | solution.py:395
  10.6 6.5 %copy-start = (bf16[16,8,3072]{2,1,0:T(8,128)(2,1)S(1)}, bf16[16,8,3072]{2,1,0:T(8,128)(2,1)}, u32[]{:S(2)}) copy-start(bf16[16,8,3072]{2,1,0:T(8,128)(2,1)} %param.6) | copy-start | bytes 2359300
  10.6 5.3 %collective-permute-start.3 = (bf16[32,1664]{1,0:T(8,128)(2,1)S(1)}, bf16[32,1664]{1,0:T(8,128)(2,1)S(1)}, u32[]{:S(2)}, u32[]{:S(2)}) collective-permute-start(bf16[32,1664]{1,0:T(8,128)(2,1)S(1)} %pad_maximum_fusion), channel_id=1, source_target_pairs={{0,5},{1,4},{2,7},{3,6},{4,1},{5,0},{6,3},{7,2},{8,13},{9,12},{10,... | collective-permute-start | bytes 319496 | tf_op jit(solution)/shard_map/ppermute | solution.py:395
  15.5 1.5 %collective-permute-start.6 = (bf16[64,1536]{1,0:T(8,128)(2,1)S(1)}, bf16[64,1536]{1,0:T(8,128)(2,1)S(1)}, u32[]{:S(2)}, u32[]{:S(2)}) collective-permute-start(bf16[64,1536]{1,0:T(8,128)(2,1)S(1)} %get-tuple-element.26.refs_5_), channel_id=1, source_target_pairs={{0,1},{1,0},{2,3},{3,2},{4,5},{5,4},{6,7},{7,6},{8,9},{9,8},{10,11... | collective-permute-start | bytes 589832 | tf_op jit(solution)/shard_map/ppermute | solution.py:395
  15.9 2.6 %collective-permute-start.7 = (bf16[64,1536]{1,0:T(8,128)(2,1)S(1)}, bf16[64,1536]{1,0:T(8,128)(2,1)S(1)}, u32[]{:S(2)}, u32[]{:S(2)}) collective-permute-start(bf16[64,1536]{1,0:T(8,128)(2,1)S(1)} %get-tuple-element.30.refs_4_), channel_id=1, source_target_pairs={{0,1},{1,0},{2,3},{3,2},{4,5},{5,4},{6,7},{7,6},{8,9},{9,8},{10,11... | collective-permute-start | bytes 589832 | tf_op jit(solution)/shard_map/ppermute | solution.py:395
  16.2 2.3 %collective-permute-start.8 = (bf16[16,1536]{1,0:T(8,128)(2,1)S(1)}, bf16[16,1536]{1,0:T(8,128)(2,1)S(1)}, u32[]{:S(2)}, u32[]{:S(2)}) collective-permute-start(bf16[16,1536]{1,0:T(8,128)(2,1)S(1)} %shard_map.67.refs_6_), channel_id=1, source_target_pairs={{0,1},{1,0},{2,3},{3,2},{4,5},{5,4},{6,7},{7,6},{8,9},{9,8},{10,11... | collective-permute-start | bytes 147464 | tf_op jit(solution)/shard_map/ppermute | solution.py:395
  18.5 13.6 %copy-start.1 = (bf16[16,4608]{1,0:T(8,128)(2,1)S(1)}, bf16[16,4608]{1,0:T(8,128)(2,1)}, u32[]{:S(2)}) copy-start(bf16[16,4608]{1,0:T(8,128)(2,1)} %value_ref.1) | copy-start | bytes 442372
  18.9 4.9 %collective-permute-start.9 = (bf16[32,1664]{1,0:T(8,128)(2,1)S(1)}, bf16[32,1664]{1,0:T(8,128)(2,1)S(1)}, u32[]{:S(2)}, u32[]{:S(2)}) collective-permute-start(bf16[32,1664]{1,0:T(8,128)(2,1)S(1)} %get-tuple-element.32), channel_id=1, source_target_pairs={{0,5},{1,4},{2,7},{3,6},{4,1},{5,0},{6,3},{7,2},{8,13},{9,12},{10,... | collective-permute-start | bytes 319496 | tf_op jit(solution)/shard_map/ppermute | solution.py:395
  23.9 4.9 %collective-permute-start.10 = (bf16[16,1664]{1,0:T(8,128)(2,1)S(1)}, bf16[16,1664]{1,0:T(8,128)(2,1)S(1)}, u32[]{:S(2)}, u32[]{:S(2)}) collective-permute-start(bf16[16,1664]{1,0:T(8,128)(2,1)S(1)} %get-tuple-element.36), channel_id=1, source_target_pairs={{0,9},{1,8},{2,11},{3,10},{4,13},{5,12},{6,15},{7,14},{8,1},{9,0},... | collective-permute-start | bytes 159752 | tf_op jit(solution)/shard_map/ppermute | solution.py:395
  28.7 3.3 %collective-permute-start.11 = (bf16[8,1664]{1,0:T(8,128)(2,1)S(1)}, bf16[8,1664]{1,0:T(8,128)(2,1)S(1)}, u32[]{:S(2)}, u32[]{:S(2)}) collective-permute-start(bf16[8,1664]{1,0:T(8,128)(2,1)S(1)} %get-tuple-element.37), channel_id=1, source_target_pairs={{0,3},{1,2},{2,1},{3,0},{4,7},{5,6},{6,5},{7,4},{8,11},{9,10},{10,... | collective-permute-start | bytes 79880 | tf_op jit(solution)/shard_map/ppermute | solution.py:395

commit v5 on v4

--- a/solution.py
+++ b/solution.py
@@ -326,16 +326,17 @@
 
 
 def self_values_kernel(masks, *refs):
-    weight_ref, share_ref, *cache_refs, cross_near_ref, cross_far_ref, send_ref, keep_ref = refs
+    out_refs = refs[-len(masks) :]
+    weight_ref, share_ref, *cache_refs, cross_near_ref, cross_far_ref = refs[: -len(masks)]
     me = lax.axis_index("utt").astype(jnp.int32)
     mine = class_of(me)
     heads, rows, _ = weight_ref.shape
     feature = heads * HD
-    half = rows // 2
     beams = cross_near_ref.shape[0]
+    blocks = [slice(at * beams, (at + 1) * beams) for at in (masks.index(m) for m in sorted(masks))]
     half_beams = beams // 2
-    keep_ref[:, feature:] = share_ref[:half]
-    send_ref[:, feature:] = share_ref[half:]
+    for out_ref, block in zip(out_refs, blocks):
+        out_ref[:, feature:] = share_ref[block]
 
     place = lax.broadcasted_iota(jnp.int32, (rows, beams), 1)
     pick_utt = utt_of_rank(lax.broadcasted_iota(jnp.int32, (rows, beams), 0) % half_beams, me)
@@ -353,8 +354,8 @@
         cross = jnp.concatenate([cross_near_ref[:, at], cross_far_ref[:, at]], axis=0)
         out = out + jnp.dot(pick, cross, preferred_element_type=jnp.float32)
         out = out.astype(jnp.bfloat16)
-        keep_ref[:, at] = out[:half]
-        send_ref[:, at] = out[half:]
+        for out_ref, block in zip(out_refs, blocks):
+            out_ref[:, at] = out[block]
 
 
 def finish_kernel(history, mine_ref, came_ref, value_ref, out_ref):
@@ -474,10 +475,9 @@
     pair_far_values = swap(after(pair_values, gathered[-1], cross_near), CORE)
 
     all_rows = rows * len(masks)
-    half = all_rows // 2
     weight_shape = jax.ShapeDtypeStruct((heads, all_rows, 2 * keys), jnp.bfloat16)
     share_shape = jax.ShapeDtypeStruct((all_rows, LANES), jnp.bfloat16)
-    part = jax.ShapeDtypeStruct((half, width), jnp.bfloat16)
+    part = jax.ShapeDtypeStruct((rows, width), jnp.bfloat16)
     near_shape = near.shape[:3] + (feature,)
     in_keys = pl.BlockSpec(near_shape, lambda i: (0, 0, 0, 0))
     in_values = pl.BlockSpec(near_shape, lambda i: (0, 0, 0, 1))
@@ -495,23 +495,22 @@
         ],
         compiler_params=params,
     )(*gathered, near, far, pair_keys, pair_far_keys)
-    send, keep = pl.pallas_call(
+    parts = pl.pallas_call(
         functools.partial(self_values_kernel, tuple(masks)),
-        out_shape=(part, part),
+        out_shape=(part,) * len(masks),
         grid=(1,),
         in_specs=[whole(weights.shape), whole(shares.shape)]
         + [in_values, in_values, pair_spec, pair_spec]
         + [whole((rows, feature))] * 2,
-        out_specs=(whole(part.shape), whole(part.shape)),
+        out_specs=(whole(part.shape),) * len(masks),
         compiler_params=params,
     )(weights, shares, near, far, pair_values, pair_far_values, cross_near, cross_far)
 
-    for bits in hops[::-1]:
-        came = swap(send, bits)
-        half = half // 2
-        send = keep[half:] + came[half:]
-        keep = keep[:half] + came[:half]
-    came = swap(send, PAIR)
+    mixed = parts[0]
+    for mask, part in zip(sorted(masks)[1:], parts[1:]):
+        mixed = mixed + swap(part, mask)
+    keep = mixed[: rows // 2]
+    came = swap(mixed[rows // 2 :], PAIR)
 
     return pl.pallas_call(
         functools.partial(finish_kernel, history),

time: 33.6 us -> 33.1 us (0.985); the launches traced: 33 us -> 32.9 us
  waiting for transfers between devices: 9.56 us -> 9.03 us
  starting transfers between devices: 15.6 us -> 16 us
    ppermute x12 -> x13, waiting for transfers between devices: 9.56 us -> 9.03 us  [swap(): return lax.ppermute(array, 'utt', [(i, i ^ bits) for i in range(devices)])]
    ppermute x12 -> x13, starting transfers between devices: 15.6 us -> 16 us  [swap(): return lax.ppermute(array, 'utt', [(i, i ^ bits) for i in range(devices)])]
  transfers between devices with their start and end apart: 12 -> 13, of which waited for: 6 -> 7; matrix products, arithmetic and copies ran while one was open for 0% -> 0% of each run, Pallas kernels for 13% -> 13%
where the time goes in v5:
time: 33.1 us; the launch traced here: 32.9 us
  starting transfers between devices  16 us (48%)
  waiting for transfers between devices  9.03 us (27%)
  Pallas kernels  6.87 us (21%)
  between operations  0.78 us (2%)
    ppermute x13, starting transfers between devices, swap(): return lax.ppermute(array, 'utt', [(i, i ^ bits) for i in range(devices)])  16 us
    ppermute x13, waiting for transfers between devices, swap(): return lax.ppermute(array, 'utt', [(i, i ^ bits) for i in range(devices)])  9.03 us
    pallas_call x1, Pallas kernels, body_by_parent(): pl.pallas_call(cross_weights_kernel, out_shape=jax.ShapeDtypeStruct((head...  1.64 us
    pallas_call x1, Pallas kernels, body_by_parent(): pl.pallas_call(functools.partial(self_weights_kernel, tuple(masks), len(g...  1.39 us
    pallas_call x1, Pallas kernels, body_by_parent(): pl.pallas_call(cross_values_kernel, out_shape=jax.ShapeDtypeStruct((rows,...  1.36 us
    pallas_call x1, Pallas kernels, body_by_parent(): pl.pallas_call(pack_kernel, out_shape=(half_rows, half_rows, half_cache),...  1.13 us
    pallas_call x1, Pallas kernels, body_by_parent(): pl.pallas_call(functools.partial(finish_kernel, history), out_shape=jax.S...  0.93 us
  transfers between devices with their start and end apart: 13, of which 7 were waited for; matrix products, arithmetic and copies ran while one was open for 0% of the time, Pallas kernels for 13%

profile of v5, /device:TPU:0, one launch (start us, length us, event | category | flops | bytes accessed | tf_op | source)
XLA Modules:
  0.0 32.9 jit_solution(2483600290752603137)
XLA Ops:
  0.0 1.1 %shard_map.64 = (bf16[8,1664]{1,0:T(8,128)(2,1)S(1)}, bf16[8,1664]{1,0:T(8,128)(2,1)S(1)}, bf16[4,16,3072]{2,1,0:T(8,128)(2,1)S(1)}) custom-call(bf16[16,4608]{1,0:T(8,128)(2,1)} %value_ref.1, s32[1,16]{1,0:T(1,128)} %parents_hbm_ref.1, bf16[4,2,16,3072]{3,2,1,0:T(8,128)(2,1)} %bitcast.5), custom_call_target="tpu_custom_call" | custom-call | tf_op jit(solution)/shard_map/pallas_call | solution.py:409
  1.1 2.5 %collective-permute-start.1 = (bf16[8,1664]{1,0:T(8,128)(2,1)S(1)}, bf16[8,1664]{1,0:T(8,128)(2,1)S(1)}, u32[]{:S(2)}, u32[]{:S(2)}) collective-permute-start(bf16[8,1664]{1,0:T(8,128)(2,1)S(1)} %get-tuple-element.22), channel_id=1, source_target_pairs={{0,3},{1,2},{2,1},{3,0},{4,7},{5,6},{6,5},{7,4},{8,11},{9,10},{10,... | collective-permute-start | bytes 79880 | tf_op jit(solution)/shard_map/ppermute | solution.py:396
  3.6 0.7 %collective-permute-start = (s32[1,16]{1,0:T(1,128)}, s32[1,16]{1,0:T(1,128)S(1)}, u32[]{:S(2)}, u32[]{:S(2)}) collective-permute-start(s32[1,16]{1,0:T(1,128)} %parents_hbm_ref.1), channel_id=1, source_target_pairs={{0,1},{1,0},{2,3},{3,2},{4,5},{5,4},{6,7},{7,6},{8,9},{9,8},{10,11... | collective-permute-start | bytes 200 | tf_op jit(solution)/shard_map/ppermute | solution.py:396
  5.0 0.2 collective-permute-done
  5.4 3.1 %collective-permute-start.2 = (bf16[16,1664]{1,0:T(8,128)(2,1)S(1)}, bf16[16,1664]{1,0:T(8,128)(2,1)S(1)}, u32[]{:S(2)}, u32[]{:S(2)}) collective-permute-start(bf16[16,1664]{1,0:T(8,128)(2,1)S(1)} %pad_maximum_fusion.1.refs_0_), channel_id=1, source_target_pairs={{0,9},{1,8},{2,11},{3,10},{4,13},{5,12},{6,15},{7,14},{8,1},{9,0},... | collective-permute-start | bytes 159752 | tf_op jit(solution)/shard_map/ppermute | solution.py:396
  8.5 0.4 %collective-permute-start.4 = (bf16[4,2,16,3072]{3,2,1,0:T(8,128)(2,1)}, bf16[4,2,16,3072]{3,2,1,0:T(8,128)(2,1)S(1)}, u32[]{:S(2)}, u32[]{:S(2)}) collective-permute-start(bf16[4,2,16,3072]{3,2,1,0:T(8,128)(2,1)} %bitcast.6), channel_id=1, source_target_pairs={{0,1},{1,0},{2,3},{3,2},{4,5},{5,4},{6,7},{7,6},{8,9},{9,8},{10,11... | collective-permute-start | bytes 2359304 | tf_op jit(solution)/shard_map/ppermute | solution.py:396
  8.9 1.6 %shard_map.65.weights_ref = bf16[12,16,256]{2,1,0:T(8,128)(2,1)S(1)} custom-call(s32[1,128]{1,0:T(1,128)S(1)} %broadcast_in_dim.8.lengths_ref, bf16[16,1536]{1,0:T(8,128)(2,1)} %query_hbm_ref, bf16[256,3072]{1,0:T(8,128)(2,1)} %bitcast.9), custom_call_target="tpu_custom_call" | custom-call | tf_op jit(solution)/shard_map/pallas_call | solution.py:439
  10.6 2.2 %collective-permute-start.3 = (bf16[32,1664]{1,0:T(8,128)(2,1)S(1)}, bf16[32,1664]{1,0:T(8,128)(2,1)S(1)}, u32[]{:S(2)}, u32[]{:S(2)}) collective-permute-start(bf16[32,1664]{1,0:T(8,128)(2,1)S(1)} %pad_maximum_fusion), channel_id=1, source_target_pairs={{0,5},{1,4},{2,7},{3,6},{4,1},{5,0},{6,3},{7,2},{8,13},{9,12},{10,... | collective-permute-start | bytes 319496 | tf_op jit(solution)/shard_map/ppermute | solution.py:396
  12.8 1.4 %shard_map.67.refs_6_ = bf16[16,1536]{1,0:T(8,128)(2,1)S(1)} custom-call(bf16[12,16,256]{2,1,0:T(8,128)(2,1)S(1)} %shard_map.65.weights_ref, bf16[256,3072]{1,0:T(8,128)(2,1)} %bitcast.10), custom_call_target="tpu_custom_call" | custom-call | tf_op jit(solution)/shard_map/pallas_call | solution.py:459
  14.2 1.3 %collective-permute-done.5 = bf16[4,16,3072]{2,1,0:T(8,128)(2,1)S(1)} collective-permute-done((bf16[4,16,3072]{2,1,0:T(8,128)(2,1)S(1)}, bf16[4,16,3072]{2,1,0:T(8,128)(2,1)S(1)}, u32[]{:S(2)}, u32[]{:S(2)}) %collective-permute-start.5) | collective-permute-done | bytes 393248 | tf_op jit(solution)/shard_map/ppermute | solution.py:396
  15.5 0.4 %collective-permute-start.6 = (bf16[64,1536]{1,0:T(8,128)(2,1)S(1)}, bf16[64,1536]{1,0:T(8,128)(2,1)S(1)}, u32[]{:S(2)}, u32[]{:S(2)}) collective-permute-start(bf16[64,1536]{1,0:T(8,128)(2,1)S(1)} %get-tuple-element.28.refs_5_), channel_id=1, source_target_pairs={{0,1},{1,0},{2,3},{3,2},{4,5},{5,4},{6,7},{7,6},{8,9},{9,8},{10,11... | collective-permute-start | bytes 589832 | tf_op jit(solution)/shard_map/ppermute | solution.py:396
  15.9 0.2 collective-permute-start.7
  16.2 0.3 collective-permute-start.8
  16.4 0.6 %collective-permute-done.6.refs_6_ = bf16[64,1536]{1,0:T(8,128)(2,1)S(1)} collective-permute-done((bf16[64,1536]{1,0:T(8,128)(2,1)S(1)}, bf16[64,1536]{1,0:T(8,128)(2,1)S(1)}, u32[]{:S(2)}, u32[]{:S(2)}) %collective-permute-start.6) | collective-permute-done | bytes 196640 | tf_op jit(solution)/shard_map/ppermute | solution.py:396
  17.1 1.4 %shard_map.66 = (bf16[12,64,256]{2,1,0:T(8,128)(2,1)S(1)}, bf16[64,128]{1,0:T(8,128)(2,1)S(1)}) custom-call(bf16[16,1664]{1,0:T(8,128)(2,1)S(1)} %pad_maximum_fusion.1.refs_0_, bf16[16,1664]{1,0:T(8,128)(2,1)S(1)} %collective-permute-done.2.refs_1_, bf16[32,1664]{1,0:T(8,128)(2,1)S(1)} %collective-permute-done.3.refs_2_, ...), custom_call_target="tpu_custom_call" | custom-call | tf_op jit(solution)/shard_map/pallas_call | solution.py:485
  18.5 0.4 %shard_map.68 = (bf16[16,1664]{1,0:T(8,128)(2,1)S(1)}, bf16[16,1664]{1,0:T(8,128)(2,1)S(1)}, bf16[16,1664]{1,0:T(8,128)(2,1)S(1)}, bf16[16,1664]{1,0:T(8,128)(2,1)S(1)}) custom-call(bf16[12,64,256]{2,1,0:T(8,128)(2,1)S(1)} %get-tuple-element.29.refs_0_, bf16[64,128]{1,0:T(8,128)(2,1)S(1)} %get-tuple-element.30.refs_1_, bf16[4,2,16,3072]{3,2,1,0:T(8,128)(2,1)S(1)} %bitcast.8, ...), custom_call_target="tpu_custom_call" | custom-call | tf_op jit(solution)/shard_map/pallas_call | solution.py:498
  18.9 4.4 %collective-permute-start.11 = (bf16[16,1664]{1,0:T(8,128)(2,1)S(1)}, bf16[16,1664]{1,0:T(8,128)(2,1)S(1)}, u32[]{:S(2)}, u32[]{:S(2)}) collective-permute-start(bf16[16,1664]{1,0:T(8,128)(2,1)S(1)} %get-tuple-element.36), channel_id=1, source_target_pairs={{0,12},{1,13},{2,14},{3,15},{4,8},{5,9},{6,10},{7,11},{8,4},{9,5},... | collective-permute-start | bytes 159752 | tf_op jit(solution)/shard_map/ppermute | solution.py:396
  23.3 0.4 %collective-permute-start.9 = (bf16[16,1664]{1,0:T(8,128)(2,1)S(1)}, bf16[16,1664]{1,0:T(8,128)(2,1)S(1)}, u32[]{:S(2)}, u32[]{:S(2)}) collective-permute-start(bf16[16,1664]{1,0:T(8,128)(2,1)S(1)} %get-tuple-element.34), channel_id=1, source_target_pairs={{0,5},{1,4},{2,7},{3,6},{4,1},{5,0},{6,3},{7,2},{8,13},{9,12},{10,... | collective-permute-start | bytes 159752 | tf_op jit(solution)/shard_map/ppermute | solution.py:396
  23.7 1.9 %collective-permute-done.11 = bf16[16,1664]{1,0:T(8,128)(2,1)S(1)} collective-permute-done((bf16[16,1664]{1,0:T(8,128)(2,1)S(1)}, bf16[16,1664]{1,0:T(8,128)(2,1)S(1)}, u32[]{:S(2)}, u32[]{:S(2)}) %collective-permute-start.11) | collective-permute-done | bytes 53280 | tf_op jit(solution)/shard_map/ppermute | solution.py:396
  25.6 2.9 %collective-permute-done.10 = bf16[16,1664]{1,0:T(8,128)(2,1)S(1)} collective-permute-done((bf16[16,1664]{1,0:T(8,128)(2,1)S(1)}, bf16[16,1664]{1,0:T(8,128)(2,1)S(1)}, u32[]{:S(2)}, u32[]{:S(2)}) %collective-permute-start.10) | collective-permute-done | bytes 53280 | tf_op jit(solution)/shard_map/ppermute | solution.py:396
  28.4 0.1 collective-permute-done.9
  28.6 1.4 %collective-permute-start.12 = (bf16[8,1664]{1,0:T(8,128)(2,1)S(1)}, bf16[8,1664]{1,0:T(8,128)(2,1)S(1)}, u32[]{:S(2)}, u32[]{:S(2)}) collective-permute-start(bf16[8,1664]{1,0:T(8,128)(2,1)S(1)} %get-tuple-element.39), channel_id=1, source_target_pairs={{0,3},{1,2},{2,1},{3,0},{4,7},{5,6},{6,5},{7,4},{8,11},{9,10},{10,... | collective-permute-start | bytes 79880 | tf_op jit(solution)/shard_map/ppermute | solution.py:396
  30.0 2.0 %collective-permute-done.12.came_ref = bf16[8,1664]{1,0:T(8,128)(2,1)S(1)} collective-permute-done((bf16[8,1664]{1,0:T(8,128)(2,1)S(1)}, bf16[8,1664]{1,0:T(8,128)(2,1)S(1)}, u32[]{:S(2)}, u32[]{:S(2)}) %collective-permute-start.12) | collective-permute-done | bytes 26656 | tf_op jit(solution)/shard_map/ppermute | solution.py:396
  32.0 0.9 %shard_map.69 = bf16[16,1536]{1,0:T(8,128)(2,1)} custom-call(bf16[8,1664]{1,0:T(8,128)(2,1)S(1)} %get-tuple-element.40.mine_ref, bf16[8,1664]{1,0:T(8,128)(2,1)S(1)} %collective-permute-done.12.came_ref, bf16[16,4608]{1,0:T(8,128)(2,1)S(1)} %copy-done.1), custom_call_target="tpu_custom_call" | custom-call | tf_op jit(solution)/shard_map/pallas_call | solution.py:515
  (21 shorter events, 0.3 us)
Async XLA Ops:
  1.1 4.2 %collective-permute-start.1 = (bf16[8,1664]{1,0:T(8,128)(2,1)S(1)}, bf16[8,1664]{1,0:T(8,128)(2,1)S(1)}, u32[]{:S(2)}, u32[]{:S(2)}) collective-permute-start(bf16[8,1664]{1,0:T(8,128)(2,1)S(1)} %get-tuple-element.22), channel_id=1, source_target_pairs={{0,3},{1,2},{2,1},{3,0},{4,7},{5,6},{6,5},{7,4},{8,11},{9,10},{10,... | collective-permute-start | bytes 79880 | tf_op jit(solution)/shard_map/ppermute | solution.py:396
  3.6 1.6 %collective-permute-start = (s32[1,16]{1,0:T(1,128)}, s32[1,16]{1,0:T(1,128)S(1)}, u32[]{:S(2)}, u32[]{:S(2)}) collective-permute-start(s32[1,16]{1,0:T(1,128)} %parents_hbm_ref.1), channel_id=1, source_target_pairs={{0,1},{1,0},{2,3},{3,2},{4,5},{5,4},{6,7},{7,6},{8,9},{9,8},{10,11... | collective-permute-start | bytes 200 | tf_op jit(solution)/shard_map/ppermute | solution.py:396
  4.3 11.2 %collective-permute-start.5 = (bf16[4,16,3072]{2,1,0:T(8,128)(2,1)S(1)}, bf16[4,16,3072]{2,1,0:T(8,128)(2,1)S(1)}, u32[]{:S(2)}, u32[]{:S(2)}) collective-permute-start(bf16[4,16,3072]{2,1,0:T(8,128)(2,1)S(1)} %get-tuple-element.27), channel_id=1, source_target_pairs={{0,3},{1,2},{2,1},{3,0},{4,7},{5,6},{6,5},{7,4},{8,11},{9,10},{10,... | collective-permute-start | bytes 1179656 | tf_op jit(solution)/shard_map/ppermute | solution.py:396
  5.4 5.2 %collective-permute-start.2 = (bf16[16,1664]{1,0:T(8,128)(2,1)S(1)}, bf16[16,1664]{1,0:T(8,128)(2,1)S(1)}, u32[]{:S(2)}, u32[]{:S(2)}) collective-permute-start(bf16[16,1664]{1,0:T(8,128)(2,1)S(1)} %pad_maximum_fusion.1.refs_0_), channel_id=1, source_target_pairs={{0,9},{1,8},{2,11},{3,10},{4,13},{5,12},{6,15},{7,14},{8,1},{9,0},... | collective-permute-start | bytes 159752 | tf_op jit(solution)/shard_map/ppermute | solution.py:396
  8.5 8.5 %collective-permute-start.4 = (bf16[4,2,16,3072]{3,2,1,0:T(8,128)(2,1)}, bf16[4,2,16,3072]{3,2,1,0:T(8,128)(2,1)S(1)}, u32[]{:S(2)}, u32[]{:S(2)}) collective-permute-start(bf16[4,2,16,3072]{3,2,1,0:T(8,128)(2,1)} %bitcast.6), channel_id=1, source_target_pairs={{0,1},{1,0},{2,3},{3,2},{4,5},{5,4},{6,7},{7,6},{8,9},{9,8},{10,11... | collective-permute-start | bytes 2359304 | tf_op jit(solution)/shard_map/ppermute | solution.py:396
  10.6 6.5 %copy-start = (bf16[16,8,3072]{2,1,0:T(8,128)(2,1)S(1)}, bf16[16,8,3072]{2,1,0:T(8,128)(2,1)}, u32[]{:S(2)}) copy-start(bf16[16,8,3072]{2,1,0:T(8,128)(2,1)} %param.6) | copy-start | bytes 2359300
  10.6 5.3 %collective-permute-start.3 = (bf16[32,1664]{1,0:T(8,128)(2,1)S(1)}, bf16[32,1664]{1,0:T(8,128)(2,1)S(1)}, u32[]{:S(2)}, u32[]{:S(2)}) collective-permute-start(bf16[32,1664]{1,0:T(8,128)(2,1)S(1)} %pad_maximum_fusion), channel_id=1, source_target_pairs={{0,5},{1,4},{2,7},{3,6},{4,1},{5,0},{6,3},{7,2},{8,13},{9,12},{10,... | collective-permute-start | bytes 319496 | tf_op jit(solution)/shard_map/ppermute | solution.py:396
  15.5 1.5 %collective-permute-start.6 = (bf16[64,1536]{1,0:T(8,128)(2,1)S(1)}, bf16[64,1536]{1,0:T(8,128)(2,1)S(1)}, u32[]{:S(2)}, u32[]{:S(2)}) collective-permute-start(bf16[64,1536]{1,0:T(8,128)(2,1)S(1)} %get-tuple-element.28.refs_5_), channel_id=1, source_target_pairs={{0,1},{1,0},{2,3},{3,2},{4,5},{5,4},{6,7},{7,6},{8,9},{9,8},{10,11... | collective-permute-start | bytes 589832 | tf_op jit(solution)/shard_map/ppermute | solution.py:396
  15.9 2.6 %collective-permute-start.7 = (bf16[64,1536]{1,0:T(8,128)(2,1)S(1)}, bf16[64,1536]{1,0:T(8,128)(2,1)S(1)}, u32[]{:S(2)}, u32[]{:S(2)}) collective-permute-start(bf16[64,1536]{1,0:T(8,128)(2,1)S(1)} %get-tuple-element.32.refs_4_), channel_id=1, source_target_pairs={{0,1},{1,0},{2,3},{3,2},{4,5},{5,4},{6,7},{7,6},{8,9},{9,8},{10,11... | collective-permute-start | bytes 589832 | tf_op jit(solution)/shard_map/ppermute | solution.py:396
  16.2 2.3 %collective-permute-start.8 = (bf16[16,1536]{1,0:T(8,128)(2,1)S(1)}, bf16[16,1536]{1,0:T(8,128)(2,1)S(1)}, u32[]{:S(2)}, u32[]{:S(2)}) collective-permute-start(bf16[16,1536]{1,0:T(8,128)(2,1)S(1)} %shard_map.67.refs_6_), channel_id=1, source_target_pairs={{0,1},{1,0},{2,3},{3,2},{4,5},{5,4},{6,7},{7,6},{8,9},{9,8},{10,11... | collective-permute-start | bytes 147464 | tf_op jit(solution)/shard_map/ppermute | solution.py:396
  18.5 13.5 %copy-start.1 = (bf16[16,4608]{1,0:T(8,128)(2,1)S(1)}, bf16[16,4608]{1,0:T(8,128)(2,1)}, u32[]{:S(2)}) copy-start(bf16[16,4608]{1,0:T(8,128)(2,1)} %value_ref.1) | copy-start | bytes 442372
  18.9 6.7 %collective-permute-start.11 = (bf16[16,1664]{1,0:T(8,128)(2,1)S(1)}, bf16[16,1664]{1,0:T(8,128)(2,1)S(1)}, u32[]{:S(2)}, u32[]{:S(2)}) collective-permute-start(bf16[16,1664]{1,0:T(8,128)(2,1)S(1)} %get-tuple-element.36), channel_id=1, source_target_pairs={{0,12},{1,13},{2,14},{3,15},{4,8},{5,9},{6,10},{7,11},{8,4},{9,5},... | collective-permute-start | bytes 159752 | tf_op jit(solution)/shard_map/ppermute | solution.py:396
  23.3 5.1 %collective-permute-start.10 = (bf16[16,1664]{1,0:T(8,128)(2,1)S(1)}, bf16[16,1664]{1,0:T(8,128)(2,1)S(1)}, u32[]{:S(2)}, u32[]{:S(2)}) collective-permute-start(bf16[16,1664]{1,0:T(8,128)(2,1)S(1)} %get-tuple-element.35), channel_id=1, source_target_pairs={{0,9},{1,8},{2,11},{3,10},{4,13},{5,12},{6,15},{7,14},{8,1},{9,0},... | collective-permute-start | bytes 159752 | tf_op jit(solution)/shard_map/ppermute | solution.py:396
  23.3 5.3 %collective-permute-start.9 = (bf16[16,1664]{1,0:T(8,128)(2,1)S(1)}, bf16[16,1664]{1,0:T(8,128)(2,1)S(1)}, u32[]{:S(2)}, u32[]{:S(2)}) collective-permute-start(bf16[16,1664]{1,0:T(8,128)(2,1)S(1)} %get-tuple-element.34), channel_id=1, source_target_pairs={{0,5},{1,4},{2,7},{3,6},{4,1},{5,0},{6,3},{7,2},{8,13},{9,12},{10,... | collective-permute-start | bytes 159752 | tf_op jit(solution)/shard_map/ppermute | solution.py:396
  28.6 3.3 %collective-permute-start.12 = (bf16[8,1664]{1,0:T(8,128)(2,1)S(1)}, bf16[8,1664]{1,0:T(8,128)(2,1)S(1)}, u32[]{:S(2)}, u32[]{:S(2)}) collective-permute-start(bf16[8,1664]{1,0:T(8,128)(2,1)S(1)} %get-tuple-element.39), channel_id=1, source_target_pairs={{0,3},{1,2},{2,1},{3,0},{4,7},{5,6},{6,5},{7,4},{8,11},{9,10},{10,... | collective-permute-start | bytes 79880 | tf_op jit(solution)/shard_map/ppermute | solution.py:396

commit v6 on v5

--- a/solution.py
+++ b/solution.py
@@ -131,19 +131,31 @@
 
 
 def pack_kernel(
-    new_ref, parents_hbm_ref, cache_ref, keep_ref, send_ref, other_ref, query_ref, key_ref, parents_ref, sems
+    new_ref,
+    parents_hbm_ref,
+    cache_ref,
+    keep_ref,
+    send_ref,
+    keys_ref,
+    values_ref,
+    query_ref,
+    key_ref,
+    parents_ref,
+    sems,
 ):
     rows, feature = query_ref.shape
     other = 1 - class_of(lax.axis_index("utt").astype(jnp.int32))
-    slicing = pltpu.make_async_copy(cache_ref.at[:, other], other_ref, sems.at[3])
+    slicing = [
+        pltpu.make_async_copy(cache_ref.at[:, other, :, :feature], keys_ref, sems.at[3]),
+        pltpu.make_async_copy(cache_ref.at[:, other, :, feature:], values_ref, sems.at[4]),
+    ]
     copies = [
         pltpu.make_async_copy(new_ref.at[:, :feature], query_ref, sems.at[0]),
         pltpu.make_async_copy(new_ref.at[:, feature : 2 * feature], key_ref, sems.at[1]),
         pltpu.make_async_copy(parents_hbm_ref, parents_ref, sems.at[2]),
     ]
-    for copy in copies:
+    for copy in copies + slicing:
         copy.start()
-    slicing.start()
     half = rows // 2
     beams = parents_ref.shape[1]
     order = class_order(rows, lax.axis_index("utt"))
@@ -172,7 +184,8 @@
         tile = jnp.dot(order, tile, preferred_element_type=jnp.float32)
         keep_ref[:, at : at + LANES] = tile[:half].astype(jnp.bfloat16)
         send_ref[:, at : at + LANES] = tile[half:].astype(jnp.bfloat16)
-    slicing.wait()
+    for copy in slicing:
+        copy.wait()
 
 
 def cross_weights_kernel(
@@ -405,17 +418,17 @@
 
     near = cache_kv.reshape(beams // (2 * CLASS), 2, CLASS * history, 2 * feature)
     half_rows = jax.ShapeDtypeStruct((rows // 2, width), jnp.bfloat16)
-    half_cache = jax.ShapeDtypeStruct(near.shape[:1] + near.shape[2:], jnp.bfloat16)
-    own, other, other_cache = pl.pallas_call(
+    half_cache = jax.ShapeDtypeStruct(near.shape[:1] + near.shape[2:3] + (feature,), jnp.bfloat16)
+    own, other, other_keys, other_values = pl.pallas_call(
         pack_kernel,
-        out_shape=(half_rows, half_rows, half_cache),
+        out_shape=(half_rows, half_rows, half_cache, half_cache),
         in_specs=[pl.BlockSpec(memory_space=pltpu.HBM)] * 3,
-        out_specs=(whole(half_rows.shape), whole(half_rows.shape), whole(half_cache.shape)),
+        out_specs=(whole(half_rows.shape),) * 2 + (whole(half_cache.shape),) * 2,
         scratch_shapes=[
             pltpu.VMEM((rows, feature), jnp.bfloat16),
             pltpu.VMEM((rows, feature), jnp.bfloat16),
             pltpu.VMEM(parents.shape, jnp.int32),
-            pltpu.SemaphoreType.DMA((4,)),
+            pltpu.SemaphoreType.DMA((5,)),
         ],
         compiler_params=params,
     )(
@@ -424,8 +437,8 @@
         in_hbm(near),
     )
     pair_rows = swap(other, PAIR)
-    far = swap(near, CORE)
-    pair_near = swap(other_cache, PAIR).reshape(keys // 2, 2 * feature)
+    pair_keys = swap(other_keys, PAIR).reshape(keys // 2, feature)
+    pair_values = swap(other_values, PAIR).reshape(keys // 2, feature)
 
     lists = jnp.pad(
         swap(after(parents, other), CORE).astype(jnp.bfloat16),
@@ -433,7 +446,6 @@
     )
     frame_count = jnp.broadcast_to(lengths.reshape(1, 1), (1, LANES))
     held = after(jnp.concatenate([own + lists, pair_rows], axis=0), frame_count)
-    gathered, masks, held_masks = [held], [0], [0]
 
     frames_kv = in_hbm(enc_kv.reshape(frames, 2 * feature))
     cross_weights = pl.pallas_call(
@@ -448,13 +460,12 @@
         ],
         compiler_params=params,
     )(frame_count, in_hbm(after(cross_queries, held)), frames_kv)
+    far = swap(after(near, other), CORE)
+    blocks = {0: held}
     for bits in hops:
-        came = swap(held, bits)
-        gathered.append(came)
-        masks = masks + [mask ^ bits for mask in held_masks]
-        held_masks = masks
-        if bits != hops[-1]:
-            held = after(jnp.concatenate([held, came], axis=0), cross_weights)
+        for mask, block in list(blocks.items()):
+            blocks[mask ^ bits] = swap(after(block, cross_weights) if mask else block, bits)
+    masks, gathered = list(blocks), list(blocks.values())
 
     cross_near = pl.pallas_call(
         cross_values_kernel,
@@ -467,11 +478,10 @@
             pltpu.SemaphoreType.DMA(()),
         ],
         compiler_params=params,
-    )(after(cross_weights, held), frames_kv)
+    )(after(cross_weights, *gathered[:-1]), frames_kv)
     cross_far = swap(cross_near, CORE)
 
-    pair_keys, pair_values = pair_near[:, :feature], pair_near[:, feature:]
-    pair_far_keys = swap(after(pair_keys, held), CORE)
+    pair_far_keys = swap(after(pair_keys, blocks[hops[0]]), CORE)
     pair_far_values = swap(after(pair_values, gathered[-1], cross_near), CORE)
 
     all_rows = rows * len(masks)
@@ -506,9 +516,12 @@
         compiler_params=params,
     )(weights, shares, near, far, pair_values, pair_far_values, cross_near, cross_far)
 
-    mixed = parts[0]
-    for mask, part in zip(sorted(masks)[1:], parts[1:]):
-        mixed = mixed + swap(part, mask)
+    parts = dict(zip(sorted(masks), parts))
+    for bits in hops[::-1]:
+        for mask in sorted(parts, reverse=True):
+            if mask ^ bits in parts and mask ^ bits < mask:
+                parts[mask ^ bits] = parts[mask ^ bits] + swap(parts.pop(mask), bits)
+    (mixed,) = parts.values()
     keep = mixed[: rows // 2]
     came = swap(mixed[rows // 2 :], PAIR)
 

time: 33.1 us -> 32 us (0.967); the launches traced: 32.9 us -> 31.4 us
  waiting for transfers between devices: 9.03 us -> 6.57 us
  starting transfers between devices: 16 us -> 16.9 us
    ppermute x13 -> x15, waiting for transfers between devices: 9.03 us -> 6.57 us  [swap(): return lax.ppermute(array, 'utt', [(i, i ^ bits) for i in range(devices)])]
    ppermute x13 -> x15, starting transfers between devices: 16 us -> 16.9 us  [swap(): return lax.ppermute(array, 'utt', [(i, i ^ bits) for i in range(devices)])]
  transfers between devices with their start and end apart: 13 -> 15, of which waited for: 7 -> 5; matrix products, arithmetic and copies ran while one was open for 0% -> 0% of each run, Pallas kernels for 13% -> 14%
where the time goes in v6:
time: 32 us; the launch traced here: 31.4 us
  starting transfers between devices  16.9 us (53%)
  Pallas kernels  6.96 us (22%)
  waiting for transfers between devices  6.57 us (21%)
  between operations  0.8 us (2%)
    ppermute x15, starting transfers between devices, swap(): return lax.ppermute(array, 'utt', [(i, i ^ bits) for i in range(devices)])  16.9 us
    ppermute x15, waiting for transfers between devices, swap(): return lax.ppermute(array, 'utt', [(i, i ^ bits) for i in range(devices)])  6.57 us
    pallas_call x1, Pallas kernels, body_by_parent(): pl.pallas_call(cross_weights_kernel, out_shape=jax.ShapeDtypeStruct((head...  1.72 us
    pallas_call x1, Pallas kernels, body_by_parent(): pl.pallas_call(functools.partial(self_weights_kernel, tuple(masks), len(g...  1.4 us
    pallas_call x1, Pallas kernels, body_by_parent(): pl.pallas_call(cross_values_kernel, out_shape=jax.ShapeDtypeStruct((rows,...  1.36 us
    pallas_call x1, Pallas kernels, body_by_parent(): pl.pallas_call(pack_kernel, out_shape=(half_rows, half_rows, half_cache,...  1.14 us
    pallas_call x1, Pallas kernels, body_by_parent(): pl.pallas_call(functools.partial(finish_kernel, history), out_shape=jax.S...  0.93 us
  transfers between devices with their start and end apart: 15, of which 5 were waited for; matrix products, arithmetic and copies ran while one was open for 0% of the time, Pallas kernels for 14%

profile of v6, /device:TPU:0, one launch (start us, length us, event | category | flops | bytes accessed | tf_op | source)
XLA Modules:
  0.0 31.4 jit_solution(17387408043405308466)
XLA Ops:
  0.0 1.1 %shard_map.64 = (bf16[8,1664]{1,0:T(8,128)(2,1)S(1)}, bf16[8,1664]{1,0:T(8,128)(2,1)S(1)}, bf16[4,16,1536]{2,1,0:T(8,128)(2,1)S(1)}, bf16[4,16,1536]{2,1,0:T(8,128)(2,1)S(1)}) custom-call(bf16[16,4608]{1,0:T(8,128)(2,1)} %value_ref.1, s32[1,16]{1,0:T(1,128)} %parents_hbm_ref.1, bf16[4,2,16,3072]{3,2,1,0:T(8,128)(2,1)} %bitcast.6), custom_call_target="tpu_custom_call" | custom-call | tf_op jit(solution)/shard_map/pallas_call | solution.py:422
  1.1 2.5 %collective-permute-start.1 = (bf16[8,1664]{1,0:T(8,128)(2,1)S(1)}, bf16[8,1664]{1,0:T(8,128)(2,1)S(1)}, u32[]{:S(2)}, u32[]{:S(2)}) collective-permute-start(bf16[8,1664]{1,0:T(8,128)(2,1)S(1)} %get-tuple-element.24), channel_id=1, source_target_pairs={{0,3},{1,2},{2,1},{3,0},{4,7},{5,6},{6,5},{7,4},{8,11},{9,10},{10,... | collective-permute-start | bytes 79880 | tf_op jit(solution)/shard_map/ppermute | solution.py:409
  3.6 0.7 %collective-permute-start = (s32[1,16]{1,0:T(1,128)}, s32[1,16]{1,0:T(1,128)S(1)}, u32[]{:S(2)}, u32[]{:S(2)}) collective-permute-start(s32[1,16]{1,0:T(1,128)} %parents_hbm_ref.1), channel_id=1, source_target_pairs={{0,1},{1,0},{2,3},{3,2},{4,5},{5,4},{6,7},{7,6},{8,9},{9,8},{10,11... | collective-permute-start | bytes 200 | tf_op jit(solution)/shard_map/ppermute | solution.py:409
  4.3 0.2 collective-permute-start.6
  4.5 1.6 %collective-permute-start.8 = (bf16[4,16,1536]{2,1,0:T(8,128)(2,1)S(1)}, bf16[4,16,1536]{2,1,0:T(8,128)(2,1)S(1)}, u32[]{:S(2)}, u32[]{:S(2)}) collective-permute-start(bf16[4,16,1536]{2,1,0:T(8,128)(2,1)S(1)} %get-tuple-element.34), channel_id=1, source_target_pairs={{0,3},{1,2},{2,1},{3,0},{4,7},{5,6},{6,5},{7,4},{8,11},{9,10},{10,... | collective-permute-start | bytes 589832 | tf_op jit(solution)/shard_map/ppermute | solution.py:409
  6.9 2.8 %collective-permute-start.2 = (bf16[16,1664]{1,0:T(8,128)(2,1)S(1)}, bf16[16,1664]{1,0:T(8,128)(2,1)S(1)}, u32[]{:S(2)}, u32[]{:S(2)}) collective-permute-start(bf16[16,1664]{1,0:T(8,128)(2,1)S(1)} %pad_maximum_fusion.refs_0_), channel_id=1, source_target_pairs={{0,9},{1,8},{2,11},{3,10},{4,13},{5,12},{6,15},{7,14},{8,1},{9,0},... | collective-permute-start | bytes 159752 | tf_op jit(solution)/shard_map/ppermute | solution.py:409
  9.6 1.2 %collective-permute-start.3 = (bf16[16,1664]{1,0:T(8,128)(2,1)S(1)}, bf16[16,1664]{1,0:T(8,128)(2,1)S(1)}, u32[]{:S(2)}, u32[]{:S(2)}) collective-permute-start(bf16[16,1664]{1,0:T(8,128)(2,1)S(1)} %pad_maximum_fusion.refs_0_), channel_id=1, source_target_pairs={{0,5},{1,4},{2,7},{3,6},{4,1},{5,0},{6,3},{7,2},{8,13},{9,12},{10,... | collective-permute-start | bytes 159752 | tf_op jit(solution)/shard_map/ppermute | solution.py:409
  10.8 1.7 %shard_map.65.weights_ref = bf16[12,16,256]{2,1,0:T(8,128)(2,1)S(1)} custom-call(s32[1,128]{1,0:T(1,128)S(1)} %broadcast_in_dim.8.lengths_ref, bf16[16,1536]{1,0:T(8,128)(2,1)} %query_hbm_ref, bf16[256,3072]{1,0:T(8,128)(2,1)} %bitcast.14), custom_call_target="tpu_custom_call" | custom-call | tf_op jit(solution)/shard_map/pallas_call | solution.py:451
  12.5 1.0 %collective-permute-start.4 = (bf16[16,1664]{1,0:T(8,128)(2,1)S(1)}, bf16[16,1664]{1,0:T(8,128)(2,1)S(1)}, u32[]{:S(2)}, u32[]{:S(2)}) collective-permute-start(bf16[16,1664]{1,0:T(8,128)(2,1)S(1)} %collective-permute-done.2.refs_1_), channel_id=1, source_target_pairs={{0,5},{1,4},{2,7},{3,6},{4,1},{5,0},{6,3},{7,2},{8,13},{9,12},{10,... | collective-permute-start | bytes 159752 | tf_op jit(solution)/shard_map/ppermute | solution.py:409
  13.6 0.1 collective-permute-done.3.refs_2_
  13.7 1.4 %shard_map.67.refs_6_ = bf16[16,1536]{1,0:T(8,128)(2,1)S(1)} custom-call(bf16[12,16,256]{2,1,0:T(8,128)(2,1)S(1)} %shard_map.65.weights_ref, bf16[256,3072]{1,0:T(8,128)(2,1)} %bitcast.15), custom_call_target="tpu_custom_call" | custom-call | tf_op jit(solution)/shard_map/pallas_call | solution.py:470
  15.1 0.3 collective-permute-start.7
  15.4 0.8 %collective-permute-done.4.refs_3_ = bf16[16,1664]{1,0:T(8,128)(2,1)S(1)} collective-permute-done((bf16[16,1664]{1,0:T(8,128)(2,1)S(1)}, bf16[16,1664]{1,0:T(8,128)(2,1)S(1)}, u32[]{:S(2)}, u32[]{:S(2)}) %collective-permute-start.4) | collective-permute-done | bytes 53280 | tf_op jit(solution)/shard_map/ppermute | solution.py:409
  16.2 0.5 %collective-permute-start.9 = (bf16[64,1536]{1,0:T(8,128)(2,1)S(1)}, bf16[64,1536]{1,0:T(8,128)(2,1)S(1)}, u32[]{:S(2)}, u32[]{:S(2)}) collective-permute-start(bf16[64,1536]{1,0:T(8,128)(2,1)S(1)} %bitcast.10), channel_id=1, source_target_pairs={{0,1},{1,0},{2,3},{3,2},{4,5},{5,4},{6,7},{7,6},{8,9},{9,8},{10,11... | collective-permute-start | bytes 589832 | tf_op jit(solution)/shard_map/ppermute | solution.py:409
  16.7 1.4 %shard_map.66 = (bf16[12,64,256]{2,1,0:T(8,128)(2,1)S(1)}, bf16[64,128]{1,0:T(8,128)(2,1)S(1)}) custom-call(bf16[16,1664]{1,0:T(8,128)(2,1)S(1)} %pad_maximum_fusion.refs_0_, bf16[16,1664]{1,0:T(8,128)(2,1)S(1)} %collective-permute-done.2.refs_1_, bf16[16,1664]{1,0:T(8,128)(2,1)S(1)} %collective-permute-done.3.refs_2_, ...), custom_call_target="tpu_custom_call" | custom-call | tf_op jit(solution)/shard_map/pallas_call | solution.py:495
  18.1 0.4 %shard_map.68 = (bf16[16,1664]{1,0:T(8,128)(2,1)S(1)}, bf16[16,1664]{1,0:T(8,128)(2,1)S(1)}, bf16[16,1664]{1,0:T(8,128)(2,1)S(1)}, bf16[16,1664]{1,0:T(8,128)(2,1)S(1)}) custom-call(bf16[12,64,256]{2,1,0:T(8,128)(2,1)S(1)} %get-tuple-element.32.refs_0_, bf16[64,128]{1,0:T(8,128)(2,1)S(1)} %get-tuple-element.33.refs_1_, bf16[4,2,16,3072]{3,2,1,0:T(8,128)(2,1)S(1)} %bitcast.9, ...), custom_call_target="tpu_custom_call" | custom-call | tf_op jit(solution)/shard_map/pallas_call | solution.py:508
  18.6 1.3 %collective-permute-start.12 = (bf16[16,1664]{1,0:T(8,128)(2,1)S(1)}, bf16[16,1664]{1,0:T(8,128)(2,1)S(1)}, u32[]{:S(2)}, u32[]{:S(2)}) collective-permute-start(bf16[16,1664]{1,0:T(8,128)(2,1)S(1)} %get-tuple-element.40), channel_id=1, source_target_pairs={{0,5},{1,4},{2,7},{3,6},{4,1},{5,0},{6,3},{7,2},{8,13},{9,12},{10,... | collective-permute-start | bytes 159752 | tf_op jit(solution)/shard_map/ppermute | solution.py:409
  19.9 0.5 %collective-permute-start.11 = (bf16[16,1664]{1,0:T(8,128)(2,1)S(1)}, bf16[16,1664]{1,0:T(8,128)(2,1)S(1)}, u32[]{:S(2)}, u32[]{:S(2)}) collective-permute-start(bf16[16,1664]{1,0:T(8,128)(2,1)S(1)} %get-tuple-element.38), channel_id=1, source_target_pairs={{0,5},{1,4},{2,7},{3,6},{4,1},{5,0},{6,3},{7,2},{8,13},{9,12},{10,... | collective-permute-start | bytes 159752 | tf_op jit(solution)/shard_map/ppermute | solution.py:409
  20.4 1.8 %collective-permute-done.12 = bf16[16,1664]{1,0:T(8,128)(2,1)S(1)} collective-permute-done((bf16[16,1664]{1,0:T(8,128)(2,1)S(1)}, bf16[16,1664]{1,0:T(8,128)(2,1)S(1)}, u32[]{:S(2)}, u32[]{:S(2)}) %collective-permute-start.12) | collective-permute-done | bytes 53280 | tf_op jit(solution)/shard_map/ppermute | solution.py:409
  22.2 3.0 %collective-permute-start.13 = (bf16[16,1664]{1,0:T(8,128)(2,1)S(1)}, bf16[16,1664]{1,0:T(8,128)(2,1)S(1)}, u32[]{:S(2)}, u32[]{:S(2)}) collective-permute-start(bf16[16,1664]{1,0:T(8,128)(2,1)S(1)} %add.25), channel_id=1, source_target_pairs={{0,9},{1,8},{2,11},{3,10},{4,13},{5,12},{6,15},{7,14},{8,1},{9,0},... | collective-permute-start | bytes 159752 | tf_op jit(solution)/shard_map/ppermute | solution.py:409
  25.2 1.8 %collective-permute-done.13 = bf16[16,1664]{1,0:T(8,128)(2,1)S(1)} collective-permute-done((bf16[16,1664]{1,0:T(8,128)(2,1)S(1)}, bf16[16,1664]{1,0:T(8,128)(2,1)S(1)}, u32[]{:S(2)}, u32[]{:S(2)}) %collective-permute-start.13) | collective-permute-done | bytes 53280 | tf_op jit(solution)/shard_map/ppermute | solution.py:409
  27.1 1.3 %collective-permute-start.14 = (bf16[8,1664]{1,0:T(8,128)(2,1)S(1)}, bf16[8,1664]{1,0:T(8,128)(2,1)S(1)}, u32[]{:S(2)}, u32[]{:S(2)}) collective-permute-start(bf16[8,1664]{1,0:T(8,128)(2,1)S(1)} %get-tuple-element.41), channel_id=1, source_target_pairs={{0,3},{1,2},{2,1},{3,0},{4,7},{5,6},{6,5},{7,4},{8,11},{9,10},{10,... | collective-permute-start | bytes 79880 | tf_op jit(solution)/shard_map/ppermute | solution.py:409
  28.4 2.0 %collective-permute-done.14.came_ref = bf16[8,1664]{1,0:T(8,128)(2,1)S(1)} collective-permute-done((bf16[8,1664]{1,0:T(8,128)(2,1)S(1)}, bf16[8,1664]{1,0:T(8,128)(2,1)S(1)}, u32[]{:S(2)}, u32[]{:S(2)}) %collective-permute-start.14) | collective-permute-done | bytes 26656 | tf_op jit(solution)/shard_map/ppermute | solution.py:409
  30.4 0.9 %shard_map.69 = bf16[16,1536]{1,0:T(8,128)(2,1)} custom-call(bf16[8,1664]{1,0:T(8,128)(2,1)S(1)} %get-tuple-element.42.mine_ref, bf16[8,1664]{1,0:T(8,128)(2,1)S(1)} %collective-permute-done.14.came_ref, bf16[16,4608]{1,0:T(8,128)(2,1)S(1)} %copy-done.1), custom_call_target="tpu_custom_call" | custom-call | tf_op jit(solution)/shard_map/pallas_call | solution.py:528
  (24 shorter events, 0.2 us)
Async XLA Ops:
  1.1 5.7 %collective-permute-start.1 = (bf16[8,1664]{1,0:T(8,128)(2,1)S(1)}, bf16[8,1664]{1,0:T(8,128)(2,1)S(1)}, u32[]{:S(2)}, u32[]{:S(2)}) collective-permute-start(bf16[8,1664]{1,0:T(8,128)(2,1)S(1)} %get-tuple-element.24), channel_id=1, source_target_pairs={{0,3},{1,2},{2,1},{3,0},{4,7},{5,6},{6,5},{7,4},{8,11},{9,10},{10,... | collective-permute-start | bytes 79880 | tf_op jit(solution)/shard_map/ppermute | solution.py:409
  3.6 3.1 %collective-permute-start = (s32[1,16]{1,0:T(1,128)}, s32[1,16]{1,0:T(1,128)S(1)}, u32[]{:S(2)}, u32[]{:S(2)}) collective-permute-start(s32[1,16]{1,0:T(1,128)} %parents_hbm_ref.1), channel_id=1, source_target_pairs={{0,1},{1,0},{2,3},{3,2},{4,5},{5,4},{6,7},{7,6},{8,9},{9,8},{10,11... | collective-permute-start | bytes 200 | tf_op jit(solution)/shard_map/ppermute | solution.py:409
  4.3 12.4 %collective-permute-start.5 = (bf16[4,2,16,3072]{3,2,1,0:T(8,128)(2,1)}, bf16[4,2,16,3072]{3,2,1,0:T(8,128)(2,1)S(1)}, u32[]{:S(2)}, u32[]{:S(2)}) collective-permute-start(bf16[4,2,16,3072]{3,2,1,0:T(8,128)(2,1)} %bitcast.7), channel_id=1, source_target_pairs={{0,1},{1,0},{2,3},{3,2},{4,5},{5,4},{6,7},{7,6},{8,9},{9,8},{10,11... | collective-permute-start | bytes 2359304 | tf_op jit(solution)/shard_map/ppermute | solution.py:409
  4.3 10.8 %collective-permute-start.6 = (bf16[4,16,1536]{2,1,0:T(8,128)(2,1)S(1)}, bf16[4,16,1536]{2,1,0:T(8,128)(2,1)S(1)}, u32[]{:S(2)}, u32[]{:S(2)}) collective-permute-start(bf16[4,16,1536]{2,1,0:T(8,128)(2,1)S(1)} %get-tuple-element.30), channel_id=1, source_target_pairs={{0,3},{1,2},{2,1},{3,0},{4,7},{5,6},{6,5},{7,4},{8,11},{9,10},{10,... | collective-permute-start | bytes 589832 | tf_op jit(solution)/shard_map/ppermute | solution.py:409
  4.5 11.7 %collective-permute-start.8 = (bf16[4,16,1536]{2,1,0:T(8,128)(2,1)S(1)}, bf16[4,16,1536]{2,1,0:T(8,128)(2,1)S(1)}, u32[]{:S(2)}, u32[]{:S(2)}) collective-permute-start(bf16[4,16,1536]{2,1,0:T(8,128)(2,1)S(1)} %get-tuple-element.34), channel_id=1, source_target_pairs={{0,3},{1,2},{2,1},{3,0},{4,7},{5,6},{6,5},{7,4},{8,11},{9,10},{10,... | collective-permute-start | bytes 589832 | tf_op jit(solution)/shard_map/ppermute | solution.py:409
  6.9 5.7 %collective-permute-start.2 = (bf16[16,1664]{1,0:T(8,128)(2,1)S(1)}, bf16[16,1664]{1,0:T(8,128)(2,1)S(1)}, u32[]{:S(2)}, u32[]{:S(2)}) collective-permute-start(bf16[16,1664]{1,0:T(8,128)(2,1)S(1)} %pad_maximum_fusion.refs_0_), channel_id=1, source_target_pairs={{0,9},{1,8},{2,11},{3,10},{4,13},{5,12},{6,15},{7,14},{8,1},{9,0},... | collective-permute-start | bytes 159752 | tf_op jit(solution)/shard_map/ppermute | solution.py:409
  9.6 4.1 %collective-permute-start.3 = (bf16[16,1664]{1,0:T(8,128)(2,1)S(1)}, bf16[16,1664]{1,0:T(8,128)(2,1)S(1)}, u32[]{:S(2)}, u32[]{:S(2)}) collective-permute-start(bf16[16,1664]{1,0:T(8,128)(2,1)S(1)} %pad_maximum_fusion.refs_0_), channel_id=1, source_target_pairs={{0,5},{1,4},{2,7},{3,6},{4,1},{5,0},{6,3},{7,2},{8,13},{9,12},{10,... | collective-permute-start | bytes 159752 | tf_op jit(solution)/shard_map/ppermute | solution.py:409
  10.8 5.9 %copy-start = (bf16[16,8,3072]{2,1,0:T(8,128)(2,1)S(1)}, bf16[16,8,3072]{2,1,0:T(8,128)(2,1)}, u32[]{:S(2)}) copy-start(bf16[16,8,3072]{2,1,0:T(8,128)(2,1)} %param.6) | copy-start | bytes 2359300
  12.5 3.6 %collective-permute-start.4 = (bf16[16,1664]{1,0:T(8,128)(2,1)S(1)}, bf16[16,1664]{1,0:T(8,128)(2,1)S(1)}, u32[]{:S(2)}, u32[]{:S(2)}) collective-permute-start(bf16[16,1664]{1,0:T(8,128)(2,1)S(1)} %collective-permute-done.2.refs_1_), channel_id=1, source_target_pairs={{0,5},{1,4},{2,7},{3,6},{4,1},{5,0},{6,3},{7,2},{8,13},{9,12},{10,... | collective-permute-start | bytes 159752 | tf_op jit(solution)/shard_map/ppermute | solution.py:409
  15.1 1.6 %collective-permute-start.7 = (bf16[64,1536]{1,0:T(8,128)(2,1)S(1)}, bf16[64,1536]{1,0:T(8,128)(2,1)S(1)}, u32[]{:S(2)}, u32[]{:S(2)}) collective-permute-start(bf16[64,1536]{1,0:T(8,128)(2,1)S(1)} %bitcast.12), channel_id=1, source_target_pairs={{0,1},{1,0},{2,3},{3,2},{4,5},{5,4},{6,7},{7,6},{8,9},{9,8},{10,11... | collective-permute-start | bytes 589832 | tf_op jit(solution)/shard_map/ppermute | solution.py:409
  16.2 2.0 %collective-permute-start.9 = (bf16[64,1536]{1,0:T(8,128)(2,1)S(1)}, bf16[64,1536]{1,0:T(8,128)(2,1)S(1)}, u32[]{:S(2)}, u32[]{:S(2)}) collective-permute-start(bf16[64,1536]{1,0:T(8,128)(2,1)S(1)} %bitcast.10), channel_id=1, source_target_pairs={{0,1},{1,0},{2,3},{3,2},{4,5},{5,4},{6,7},{7,6},{8,9},{9,8},{10,11... | collective-permute-start | bytes 589832 | tf_op jit(solution)/shard_map/ppermute | solution.py:409
  16.7 1.4 %collective-permute-start.10 = (bf16[16,1536]{1,0:T(8,128)(2,1)S(1)}, bf16[16,1536]{1,0:T(8,128)(2,1)S(1)}, u32[]{:S(2)}, u32[]{:S(2)}) collective-permute-start(bf16[16,1536]{1,0:T(8,128)(2,1)S(1)} %shard_map.67.refs_6_), channel_id=1, source_target_pairs={{0,1},{1,0},{2,3},{3,2},{4,5},{5,4},{6,7},{7,6},{8,9},{9,8},{10,11... | collective-permute-start | bytes 147464 | tf_op jit(solution)/shard_map/ppermute | solution.py:409
  18.1 12.3 %copy-start.1 = (bf16[16,4608]{1,0:T(8,128)(2,1)S(1)}, bf16[16,4608]{1,0:T(8,128)(2,1)}, u32[]{:S(2)}) copy-start(bf16[16,4608]{1,0:T(8,128)(2,1)} %value_ref.1) | copy-start | bytes 442372
  18.6 3.6 %collective-permute-start.12 = (bf16[16,1664]{1,0:T(8,128)(2,1)S(1)}, bf16[16,1664]{1,0:T(8,128)(2,1)S(1)}, u32[]{:S(2)}, u32[]{:S(2)}) collective-permute-start(bf16[16,1664]{1,0:T(8,128)(2,1)S(1)} %get-tuple-element.40), channel_id=1, source_target_pairs={{0,5},{1,4},{2,7},{3,6},{4,1},{5,0},{6,3},{7,2},{8,13},{9,12},{10,... | collective-permute-start | bytes 159752 | tf_op jit(solution)/shard_map/ppermute | solution.py:409
  19.9 5.4 %collective-permute-start.11 = (bf16[16,1664]{1,0:T(8,128)(2,1)S(1)}, bf16[16,1664]{1,0:T(8,128)(2,1)S(1)}, u32[]{:S(2)}, u32[]{:S(2)}) collective-permute-start(bf16[16,1664]{1,0:T(8,128)(2,1)S(1)} %get-tuple-element.38), channel_id=1, source_target_pairs={{0,5},{1,4},{2,7},{3,6},{4,1},{5,0},{6,3},{7,2},{8,13},{9,12},{10,... | collective-permute-start | bytes 159752 | tf_op jit(solution)/shard_map/ppermute | solution.py:409
  22.2 4.8 %collective-permute-start.13 = (bf16[16,1664]{1,0:T(8,128)(2,1)S(1)}, bf16[16,1664]{1,0:T(8,128)(2,1)S(1)}, u32[]{:S(2)}, u32[]{:S(2)}) collective-permute-start(bf16[16,1664]{1,0:T(8,128)(2,1)S(1)} %add.25), channel_id=1, source_target_pairs={{0,9},{1,8},{2,11},{3,10},{4,13},{5,12},{6,15},{7,14},{8,1},{9,0},... | collective-permute-start | bytes 159752 | tf_op jit(solution)/shard_map/ppermute | solution.py:409
  27.1 3.3 %collective-permute-start.14 = (bf16[8,1664]{1,0:T(8,128)(2,1)S(1)}, bf16[8,1664]{1,0:T(8,128)(2,1)S(1)}, u32[]{:S(2)}, u32[]{:S(2)}) collective-permute-start(bf16[8,1664]{1,0:T(8,128)(2,1)S(1)} %get-tuple-element.41), channel_id=1, source_target_pairs={{0,3},{1,2},{2,1},{3,0},{4,7},{5,6},{6,5},{7,4},{8,11},{9,10},{10,... | collective-permute-start | bytes 79880 | tf_op jit(solution)/shard_map/ppermute | solution.py:409

commit v7 on v6

--- a/solution.py
+++ b/solution.py
@@ -188,18 +188,8 @@
         copy.wait()
 
 
-def cross_weights_kernel(
-    lengths_ref, query_hbm_ref, frames_ref, out_ref, query_ref, keys_ref, sems
-):
+def cross_weights_kernel(lengths_ref, query_ref, keys_ref, out_ref):
     rows, feature = query_ref.shape
-    copies = [
-        pltpu.make_async_copy(frames_ref.at[:, :feature], keys_ref, sems.at[0]),
-        pltpu.make_async_copy(query_hbm_ref, query_ref, sems.at[1]),
-    ]
-    for copy in copies:
-        copy.start()
-    for copy in copies:
-        copy.wait()
     frames = keys_ref.shape[0]
     heads = feature // HD
     live = lax.broadcasted_iota(jnp.int32, (rows, frames), 1) < lengths_ref[:, :1]
@@ -218,11 +208,7 @@
         out_ref[head] = weights.astype(jnp.bfloat16)
 
 
-def cross_values_kernel(weights_ref, frames_ref, out_ref, values_ref, sem):
-    feature = values_ref.shape[1]
-    copy = pltpu.make_async_copy(frames_ref.at[:, feature:], values_ref, sem)
-    copy.start()
-    copy.wait()
+def cross_values_kernel(weights_ref, values_ref, out_ref):
     for head in range(weights_ref.shape[0]):
         at = slice(head * HD, (head + 1) * HD)
         out_ref[:, at] = jnp.dot(
@@ -431,6 +417,9 @@
             pltpu.SemaphoreType.DMA((5,)),
         ],
         compiler_params=params,
+        cost_estimate=pl.CostEstimate(
+            flops=4_000_000_000, bytes_accessed=4 * near.size, transcendentals=0
+        ),
     )(
         in_hbm(new_rows),
         in_hbm(parents),
@@ -445,21 +434,21 @@
         ((0, 0), (feature + PARENT_LANE + beams, LANES - PARENT_LANE - 2 * beams)),
     )
     frame_count = jnp.broadcast_to(lengths.reshape(1, 1), (1, LANES))
-    held = after(jnp.concatenate([own + lists, pair_rows], axis=0), frame_count)
-
-    frames_kv = in_hbm(enc_kv.reshape(frames, 2 * feature))
+    held = jnp.concatenate([own + lists, pair_rows], axis=0)
+
+    frames_kv = enc_kv.reshape(frames, 2 * feature)
     cross_weights = pl.pallas_call(
         cross_weights_kernel,
         out_shape=jax.ShapeDtypeStruct((heads, rows, frames), jnp.bfloat16),
-        in_specs=[whole((1, LANES))] + [pl.BlockSpec(memory_space=pltpu.HBM)] * 2,
+        grid=(1,),
+        in_specs=[
+            whole((1, LANES)),
+            whole((rows, feature)),
+            pl.BlockSpec((frames, feature), lambda i: (0, 0)),
+        ],
         out_specs=whole((heads, rows, frames)),
-        scratch_shapes=[
-            pltpu.VMEM((rows, feature), jnp.bfloat16),
-            pltpu.VMEM((frames, feature), jnp.bfloat16),
-            pltpu.SemaphoreType.DMA((2,)),
-        ],
         compiler_params=params,
-    )(frame_count, in_hbm(after(cross_queries, held)), frames_kv)
+    )(frame_count, after(cross_queries, held), frames_kv)
     far = swap(after(near, other), CORE)
     blocks = {0: held}
     for bits in hops:
@@ -471,12 +460,11 @@
         cross_values_kernel,
         out_shape=jax.ShapeDtypeStruct((rows, feature), jnp.bfloat16),
         grid=(1,),
-        in_specs=[whole((heads, rows, frames)), pl.BlockSpec(memory_space=pltpu.HBM)],
+        in_specs=[
+            whole((heads, rows, frames)),
+            pl.BlockSpec((frames, feature), lambda i: (0, 1)),
+        ],
         out_specs=whole((rows, feature)),
-        scratch_shapes=[
-            pltpu.VMEM((frames, feature), jnp.bfloat16),
-            pltpu.SemaphoreType.DMA(()),
-        ],
         compiler_params=params,
     )(after(cross_weights, *gathered[:-1]), frames_kv)
     cross_far = swap(cross_near, CORE)

time: 32 us -> 31.7 us (level)
  Pallas kernels: 6.96 us -> 4.83 us
  waiting for transfers between devices: 6.57 us -> 7.77 us
  starting transfers between devices: 16.9 us -> 17.6 us
    ppermute x15, waiting for transfers between devices: 6.57 us -> 7.77 us  [swap(): return lax.ppermute(array, 'utt', [(i, i ^ bits) for i in range(devices)])]
    pallas_call x1, Pallas kernels: 1.72 us -> 0.52 us  [body_by_parent(): pl.pallas_call(cross_weights_kernel, out_shape=jax.ShapeDtypeStruct((head...]
    pallas_call x1, Pallas kernels: 1.36 us -> 0.25 us  [body_by_parent(): pl.pallas_call(cross_values_kernel, out_shape=jax.ShapeDtypeStruct((rows,...]
    ppermute x15, starting transfers between devices: 16.9 us -> 17.6 us  [swap(): return lax.ppermute(array, 'utt', [(i, i ^ bits) for i in range(devices)])]
  transfers between devices with their start and end apart: 15 -> 15, of which waited for: 5 -> 6; matrix products, arithmetic and copies ran while one was open for 0% -> 0% of each run, Pallas kernels for 14% -> 7%
where the time goes in v7:
time: 31.7 us; the launch traced here: 31.1 us
  starting transfers between devices  17.6 us (56%)
  waiting for transfers between devices  7.77 us (25%)
  Pallas kernels  4.83 us (15%)
  between operations  0.75 us (2%)
    ppermute x15, starting transfers between devices, swap(): return lax.ppermute(array, 'utt', [(i, i ^ bits) for i in range(devices)])  17.6 us
    ppermute x15, waiting for transfers between devices, swap(): return lax.ppermute(array, 'utt', [(i, i ^ bits) for i in range(devices)])  7.77 us
    pallas_call x1, Pallas kernels, body_by_parent(): pl.pallas_call(functools.partial(self_weights_kernel, tuple(masks), len(g...  1.41 us
    pallas_call x1, Pallas kernels, body_by_parent(): pl.pallas_call(pack_kernel, out_shape=(half_rows, half_rows, half_cache,...  1.29 us
    pallas_call x1, Pallas kernels, body_by_parent(): pl.pallas_call(functools.partial(finish_kernel, history), out_shape=jax.S...  0.93 us
  transfers between devices with their start and end apart: 15, of which 6 were waited for; matrix products, arithmetic and copies ran while one was open for 0% of the time, Pallas kernels for 7%

profile of v7, /device:TPU:0, one launch (start us, length us, event | category | flops | bytes accessed | tf_op | source)
XLA Modules:
  0.0 31.1 jit_solution(14538643184200516183)
XLA Ops:
  0.0 1.3 %shard_map.64 = (bf16[8,1664]{1,0:T(8,128)(2,1)S(1)}, bf16[8,1664]{1,0:T(8,128)(2,1)S(1)}, bf16[4,16,1536]{2,1,0:T(8,128)(2,1)S(1)}, bf16[4,16,1536]{2,1,0:T(8,128)(2,1)S(1)}) custom-call(bf16[16,4608]{1,0:T(8,128)(2,1)} %value_ref.1, s32[1,16]{1,0:T(1,128)} %parents_hbm_ref.1, bf16[4,2,16,3072]{3,2,1,0:T(8,128)(2,1)} %bitcast.8), custom_call_target="tpu_custom_call" | custom-call | flops 4000000000 | bytes 1572864 | tf_op jit(solution)/shard_map/pallas_call | solution.py:408
  1.3 2.5 %collective-permute-start.1 = (bf16[8,1664]{1,0:T(8,128)(2,1)S(1)}, bf16[8,1664]{1,0:T(8,128)(2,1)S(1)}, u32[]{:S(2)}, u32[]{:S(2)}) collective-permute-start(bf16[8,1664]{1,0:T(8,128)(2,1)S(1)} %get-tuple-element.23), channel_id=1, source_target_pairs={{0,3},{1,2},{2,1},{3,0},{4,7},{5,6},{6,5},{7,4},{8,11},{9,10},{10,... | collective-permute-start | bytes 79880 | tf_op jit(solution)/shard_map/ppermute | solution.py:395
  3.8 0.7 %collective-permute-start = (s32[1,16]{1,0:T(1,128)S(1)}, s32[1,16]{1,0:T(1,128)S(1)}, u32[]{:S(2)}, u32[]{:S(2)}) collective-permute-start(s32[1,16]{1,0:T(1,128)S(1)} %copy-done.4), channel_id=1, source_target_pairs={{0,1},{1,0},{2,3},{3,2},{4,5},{5,4},{6,7},{7,6},{8,9},{9,8},{10,11... | collective-permute-start | bytes 200 | tf_op jit(solution)/shard_map/ppermute | solution.py:395
  4.6 1.6 %collective-permute-start.8 = (bf16[4,16,1536]{2,1,0:T(8,128)(2,1)S(1)}, bf16[4,16,1536]{2,1,0:T(8,128)(2,1)S(1)}, u32[]{:S(2)}, u32[]{:S(2)}) collective-permute-start(bf16[4,16,1536]{2,1,0:T(8,128)(2,1)S(1)} %get-tuple-element.32), channel_id=1, source_target_pairs={{0,3},{1,2},{2,1},{3,0},{4,7},{5,6},{6,5},{7,4},{8,11},{9,10},{10,... | collective-permute-start | bytes 589832 | tf_op jit(solution)/shard_map/ppermute | solution.py:395
  6.4 2.7 %collective-permute-start.2 = (bf16[16,1664]{1,0:T(8,128)(2,1)S(1)}, bf16[16,1664]{1,0:T(8,128)(2,1)S(1)}, u32[]{:S(2)}, u32[]{:S(2)}) collective-permute-start(bf16[16,1664]{1,0:T(8,128)(2,1)S(1)} %pad_maximum_fusion.refs_0_), channel_id=1, source_target_pairs={{0,9},{1,8},{2,11},{3,10},{4,13},{5,12},{6,15},{7,14},{8,1},{9,0},... | collective-permute-start | bytes 159752 | tf_op jit(solution)/shard_map/ppermute | solution.py:395
  9.8 1.3 %collective-permute-start.3 = (bf16[16,1664]{1,0:T(8,128)(2,1)S(1)}, bf16[16,1664]{1,0:T(8,128)(2,1)S(1)}, u32[]{:S(2)}, u32[]{:S(2)}) collective-permute-start(bf16[16,1664]{1,0:T(8,128)(2,1)S(1)} %pad_maximum_fusion.refs_0_), channel_id=1, source_target_pairs={{0,5},{1,4},{2,7},{3,6},{4,1},{5,0},{6,3},{7,2},{8,13},{9,12},{10,... | collective-permute-start | bytes 159752 | tf_op jit(solution)/shard_map/ppermute | solution.py:395
  11.1 0.5 %shard_map.65.weights_ref = bf16[12,16,256]{2,1,0:T(8,128)(2,1)S(1)} custom-call(s32[1,128]{1,0:T(1,128)S(1)} %broadcast_in_dim.8.lengths_ref, bf16[16,1536]{1,0:T(8,128)(2,1)S(1)} %copy-done.3, bf16[256,3072]{1,0:T(8,128)(2,1)S(1)} %bitcast.6), custom_call_target="tpu_custom_call" | custom-call | tf_op jit(solution)/shard_map/pallas_call | solution.py:440
  11.6 1.4 %collective-permute-start.4 = (bf16[16,1664]{1,0:T(8,128)(2,1)S(1)}, bf16[16,1664]{1,0:T(8,128)(2,1)S(1)}, u32[]{:S(2)}, u32[]{:S(2)}) collective-permute-start(bf16[16,1664]{1,0:T(8,128)(2,1)S(1)} %collective-permute-done.2.refs_1_), channel_id=1, source_target_pairs={{0,5},{1,4},{2,7},{3,6},{4,1},{5,0},{6,3},{7,2},{8,13},{9,12},{10,... | collective-permute-start | bytes 159752 | tf_op jit(solution)/shard_map/ppermute | solution.py:395
  13.0 0.7 %collective-permute-done.3.refs_2_ = bf16[16,1664]{1,0:T(8,128)(2,1)S(1)} collective-permute-done((bf16[16,1664]{1,0:T(8,128)(2,1)S(1)}, bf16[16,1664]{1,0:T(8,128)(2,1)S(1)}, u32[]{:S(2)}, u32[]{:S(2)}) %collective-permute-start.3) | collective-permute-done | bytes 53280 | tf_op jit(solution)/shard_map/ppermute | solution.py:395
  13.7 0.3 shard_map.67.refs_6_
  14.0 0.4 %collective-permute-start.7 = (bf16[64,1536]{1,0:T(8,128)(2,1)S(1)}, bf16[64,1536]{1,0:T(8,128)(2,1)S(1)}, u32[]{:S(2)}, u32[]{:S(2)}) collective-permute-start(bf16[64,1536]{1,0:T(8,128)(2,1)S(1)} %bitcast.14), channel_id=1, source_target_pairs={{0,1},{1,0},{2,3},{3,2},{4,5},{5,4},{6,7},{7,6},{8,9},{9,8},{10,11... | collective-permute-start | bytes 589832 | tf_op jit(solution)/shard_map/ppermute | solution.py:395
  14.4 0.8 %collective-permute-done.4.refs_3_ = bf16[16,1664]{1,0:T(8,128)(2,1)S(1)} collective-permute-done((bf16[16,1664]{1,0:T(8,128)(2,1)S(1)}, bf16[16,1664]{1,0:T(8,128)(2,1)S(1)}, u32[]{:S(2)}, u32[]{:S(2)}) %collective-permute-start.4) | collective-permute-done | bytes 53280 | tf_op jit(solution)/shard_map/ppermute | solution.py:395
  15.3 0.1 collective-permute-done.8
  15.4 0.7 %collective-permute-start.9 = (bf16[64,1536]{1,0:T(8,128)(2,1)S(1)}, bf16[64,1536]{1,0:T(8,128)(2,1)S(1)}, u32[]{:S(2)}, u32[]{:S(2)}) collective-permute-start(bf16[64,1536]{1,0:T(8,128)(2,1)S(1)} %bitcast.12), channel_id=1, source_target_pairs={{0,1},{1,0},{2,3},{3,2},{4,5},{5,4},{6,7},{7,6},{8,9},{9,8},{10,11... | collective-permute-start | bytes 589832 | tf_op jit(solution)/shard_map/ppermute | solution.py:395
  16.1 1.4 %shard_map.66 = (bf16[12,64,256]{2,1,0:T(8,128)(2,1)S(1)}, bf16[64,128]{1,0:T(8,128)(2,1)S(1)}) custom-call(bf16[16,1664]{1,0:T(8,128)(2,1)S(1)} %pad_maximum_fusion.refs_0_, bf16[16,1664]{1,0:T(8,128)(2,1)S(1)} %collective-permute-done.2.refs_1_, bf16[16,1664]{1,0:T(8,128)(2,1)S(1)} %collective-permute-done.3.refs_2_, ...), custom_call_target="tpu_custom_call" | custom-call | tf_op jit(solution)/shard_map/pallas_call | solution.py:483
  17.6 0.4 %shard_map.68 = (bf16[16,1664]{1,0:T(8,128)(2,1)S(1)}, bf16[16,1664]{1,0:T(8,128)(2,1)S(1)}, bf16[16,1664]{1,0:T(8,128)(2,1)S(1)}, bf16[16,1664]{1,0:T(8,128)(2,1)S(1)}) custom-call(bf16[12,64,256]{2,1,0:T(8,128)(2,1)S(1)} %get-tuple-element.30.refs_0_, bf16[64,128]{1,0:T(8,128)(2,1)S(1)} %get-tuple-element.31.refs_1_, ...), custom_call_target="tpu_custom_call" | custom-call | tf_op jit(solution)/shard_map/pallas_call | solution.py:496
  18.0 1.5 %collective-permute-start.12 = (bf16[16,1664]{1,0:T(8,128)(2,1)S(1)}, bf16[16,1664]{1,0:T(8,128)(2,1)S(1)}, u32[]{:S(2)}, u32[]{:S(2)}) collective-permute-start(bf16[16,1664]{1,0:T(8,128)(2,1)S(1)} %get-tuple-element.38), channel_id=1, source_target_pairs={{0,5},{1,4},{2,7},{3,6},{4,1},{5,0},{6,3},{7,2},{8,13},{9,12},{10,... | collective-permute-start | bytes 159752 | tf_op jit(solution)/shard_map/ppermute | solution.py:395
  19.5 0.3 %collective-permute-start.11 = (bf16[16,1664]{1,0:T(8,128)(2,1)S(1)}, bf16[16,1664]{1,0:T(8,128)(2,1)S(1)}, u32[]{:S(2)}, u32[]{:S(2)}) collective-permute-start(bf16[16,1664]{1,0:T(8,128)(2,1)S(1)} %get-tuple-element.36), channel_id=1, source_target_pairs={{0,5},{1,4},{2,7},{3,6},{4,1},{5,0},{6,3},{7,2},{8,13},{9,12},{10,... | collective-permute-start | bytes 159752 | tf_op jit(solution)/shard_map/ppermute | solution.py:395
  19.8 1.9 %collective-permute-done.12 = bf16[16,1664]{1,0:T(8,128)(2,1)S(1)} collective-permute-done((bf16[16,1664]{1,0:T(8,128)(2,1)S(1)}, bf16[16,1664]{1,0:T(8,128)(2,1)S(1)}, u32[]{:S(2)}, u32[]{:S(2)}) %collective-permute-start.12) | collective-permute-done | bytes 53280 | tf_op jit(solution)/shard_map/ppermute | solution.py:395
  21.7 3.0 %collective-permute-start.13 = (bf16[16,1664]{1,0:T(8,128)(2,1)S(1)}, bf16[16,1664]{1,0:T(8,128)(2,1)S(1)}, u32[]{:S(2)}, u32[]{:S(2)}) collective-permute-start(bf16[16,1664]{1,0:T(8,128)(2,1)S(1)} %add.25), channel_id=1, source_target_pairs={{0,9},{1,8},{2,11},{3,10},{4,13},{5,12},{6,15},{7,14},{8,1},{9,0},... | collective-permute-start | bytes 159752 | tf_op jit(solution)/shard_map/ppermute | solution.py:395
  24.7 2.0 %collective-permute-done.13 = bf16[16,1664]{1,0:T(8,128)(2,1)S(1)} collective-permute-done((bf16[16,1664]{1,0:T(8,128)(2,1)S(1)}, bf16[16,1664]{1,0:T(8,128)(2,1)S(1)}, u32[]{:S(2)}, u32[]{:S(2)}) %collective-permute-start.13) | collective-permute-done | bytes 53280 | tf_op jit(solution)/shard_map/ppermute | solution.py:395
  26.8 1.2 %collective-permute-start.14 = (bf16[8,1664]{1,0:T(8,128)(2,1)S(1)}, bf16[8,1664]{1,0:T(8,128)(2,1)S(1)}, u32[]{:S(2)}, u32[]{:S(2)}) collective-permute-start(bf16[8,1664]{1,0:T(8,128)(2,1)S(1)} %get-tuple-element.39), channel_id=1, source_target_pairs={{0,3},{1,2},{2,1},{3,0},{4,7},{5,6},{6,5},{7,4},{8,11},{9,10},{10,... | collective-permute-start | bytes 79880 | tf_op jit(solution)/shard_map/ppermute | solution.py:395
  28.1 2.1 %collective-permute-done.14.came_ref = bf16[8,1664]{1,0:T(8,128)(2,1)S(1)} collective-permute-done((bf16[8,1664]{1,0:T(8,128)(2,1)S(1)}, bf16[8,1664]{1,0:T(8,128)(2,1)S(1)}, u32[]{:S(2)}, u32[]{:S(2)}) %collective-permute-start.14) | collective-permute-done | bytes 26656 | tf_op jit(solution)/shard_map/ppermute | solution.py:395
  30.2 0.9 %shard_map.69 = bf16[16,1536]{1,0:T(8,128)(2,1)} custom-call(bf16[8,1664]{1,0:T(8,128)(2,1)S(1)} %get-tuple-element.40.mine_ref, bf16[8,1664]{1,0:T(8,128)(2,1)S(1)} %collective-permute-done.14.came_ref, bf16[16,4608]{1,0:T(8,128)(2,1)S(1)} %copy-done.2), custom_call_target="tpu_custom_call" | custom-call | tf_op jit(solution)/shard_map/pallas_call | solution.py:516
  (30 shorter events, 0.4 us)
Async XLA Ops:
  0.0 3.8 %copy-start.4 = (s32[1,16]{1,0:T(1,128)S(1)}, s32[1,16]{1,0:T(1,128)}, u32[]{:S(2)}) copy-start(s32[1,16]{1,0:T(1,128)} %parents_hbm_ref.1) | copy-start | bytes 196
  0.0 4.5 %copy-start.1 = (bf16[16,8,3072]{2,1,0:T(8,128)(2,1)S(1)}, bf16[16,8,3072]{2,1,0:T(8,128)(2,1)}, u32[]{:S(2)}) copy-start(bf16[16,8,3072]{2,1,0:T(8,128)(2,1)} %param.6) | copy-start | bytes 2359300
  0.0 11.1 %copy-start = (bf16[1,256,3072]{2,1,0:T(8,128)(2,1)S(1)}, bf16[1,256,3072]{2,1,0:T(8,128)(2,1)}, u32[]{:S(2)}) copy-start(bf16[1,256,3072]{2,1,0:T(8,128)(2,1)} %param.9) | copy-start | bytes 4718596
  0.0 11.1 %copy-start.3 = (bf16[16,1536]{1,0:T(8,128)(2,1)S(1)}, bf16[16,1536]{1,0:T(8,128)(2,1)}, u32[]{:S(2)}) copy-start(bf16[16,1536]{1,0:T(8,128)(2,1)} %query_ref) | copy-start | bytes 147460
  1.3 5.1 %collective-permute-start.1 = (bf16[8,1664]{1,0:T(8,128)(2,1)S(1)}, bf16[8,1664]{1,0:T(8,128)(2,1)S(1)}, u32[]{:S(2)}, u32[]{:S(2)}) collective-permute-start(bf16[8,1664]{1,0:T(8,128)(2,1)S(1)} %get-tuple-element.23), channel_id=1, source_target_pairs={{0,3},{1,2},{2,1},{3,0},{4,7},{5,6},{6,5},{7,4},{8,11},{9,10},{10,... | collective-permute-start | bytes 79880 | tf_op jit(solution)/shard_map/ppermute | solution.py:395
  3.8 2.5 %collective-permute-start = (s32[1,16]{1,0:T(1,128)S(1)}, s32[1,16]{1,0:T(1,128)S(1)}, u32[]{:S(2)}, u32[]{:S(2)}) collective-permute-start(s32[1,16]{1,0:T(1,128)S(1)} %copy-done.4), channel_id=1, source_target_pairs={{0,1},{1,0},{2,3},{3,2},{4,5},{5,4},{6,7},{7,6},{8,9},{9,8},{10,11... | collective-permute-start | bytes 200 | tf_op jit(solution)/shard_map/ppermute | solution.py:395
  4.5 11.6 %collective-permute-start.5 = (bf16[4,2,16,3072]{3,2,1,0:T(8,128)(2,1)S(1)}, bf16[4,2,16,3072]{3,2,1,0:T(8,128)(2,1)S(1)}, u32[]{:S(2)}, u32[]{:S(2)}) collective-permute-start(bf16[4,2,16,3072]{3,2,1,0:T(8,128)(2,1)S(1)} %bitcast.9), channel_id=1, source_target_pairs={{0,1},{1,0},{2,3},{3,2},{4,5},{5,4},{6,7},{7,6},{8,9},{9,8},{10,11... | collective-permute-start | bytes 2359304 | tf_op jit(solution)/shard_map/ppermute | solution.py:395
  4.5 9.4 %collective-permute-start.6 = (bf16[4,16,1536]{2,1,0:T(8,128)(2,1)S(1)}, bf16[4,16,1536]{2,1,0:T(8,128)(2,1)S(1)}, u32[]{:S(2)}, u32[]{:S(2)}) collective-permute-start(bf16[4,16,1536]{2,1,0:T(8,128)(2,1)S(1)} %get-tuple-element.28), channel_id=1, source_target_pairs={{0,3},{1,2},{2,1},{3,0},{4,7},{5,6},{6,5},{7,4},{8,11},{9,10},{10,... | collective-permute-start | bytes 589832 | tf_op jit(solution)/shard_map/ppermute | solution.py:395
  4.6 10.7 %collective-permute-start.8 = (bf16[4,16,1536]{2,1,0:T(8,128)(2,1)S(1)}, bf16[4,16,1536]{2,1,0:T(8,128)(2,1)S(1)}, u32[]{:S(2)}, u32[]{:S(2)}) collective-permute-start(bf16[4,16,1536]{2,1,0:T(8,128)(2,1)S(1)} %get-tuple-element.32), channel_id=1, source_target_pairs={{0,3},{1,2},{2,1},{3,0},{4,7},{5,6},{6,5},{7,4},{8,11},{9,10},{10,... | collective-permute-start | bytes 589832 | tf_op jit(solution)/shard_map/ppermute | solution.py:395
  6.4 5.2 %collective-permute-start.2 = (bf16[16,1664]{1,0:T(8,128)(2,1)S(1)}, bf16[16,1664]{1,0:T(8,128)(2,1)S(1)}, u32[]{:S(2)}, u32[]{:S(2)}) collective-permute-start(bf16[16,1664]{1,0:T(8,128)(2,1)S(1)} %pad_maximum_fusion.refs_0_), channel_id=1, source_target_pairs={{0,9},{1,8},{2,11},{3,10},{4,13},{5,12},{6,15},{7,14},{8,1},{9,0},... | collective-permute-start | bytes 159752 | tf_op jit(solution)/shard_map/ppermute | solution.py:395
  9.8 3.9 %collective-permute-start.3 = (bf16[16,1664]{1,0:T(8,128)(2,1)S(1)}, bf16[16,1664]{1,0:T(8,128)(2,1)S(1)}, u32[]{:S(2)}, u32[]{:S(2)}) collective-permute-start(bf16[16,1664]{1,0:T(8,128)(2,1)S(1)} %pad_maximum_fusion.refs_0_), channel_id=1, source_target_pairs={{0,5},{1,4},{2,7},{3,6},{4,1},{5,0},{6,3},{7,2},{8,13},{9,12},{10,... | collective-permute-start | bytes 159752 | tf_op jit(solution)/shard_map/ppermute | solution.py:395
  11.6 3.6 %collective-permute-start.4 = (bf16[16,1664]{1,0:T(8,128)(2,1)S(1)}, bf16[16,1664]{1,0:T(8,128)(2,1)S(1)}, u32[]{:S(2)}, u32[]{:S(2)}) collective-permute-start(bf16[16,1664]{1,0:T(8,128)(2,1)S(1)} %collective-permute-done.2.refs_1_), channel_id=1, source_target_pairs={{0,5},{1,4},{2,7},{3,6},{4,1},{5,0},{6,3},{7,2},{8,13},{9,12},{10,... | collective-permute-start | bytes 159752 | tf_op jit(solution)/shard_map/ppermute | solution.py:395
  14.0 2.1 %collective-permute-start.7 = (bf16[64,1536]{1,0:T(8,128)(2,1)S(1)}, bf16[64,1536]{1,0:T(8,128)(2,1)S(1)}, u32[]{:S(2)}, u32[]{:S(2)}) collective-permute-start(bf16[64,1536]{1,0:T(8,128)(2,1)S(1)} %bitcast.14), channel_id=1, source_target_pairs={{0,1},{1,0},{2,3},{3,2},{4,5},{5,4},{6,7},{7,6},{8,9},{9,8},{10,11... | collective-permute-start | bytes 589832 | tf_op jit(solution)/shard_map/ppermute | solution.py:395
  15.4 2.2 %collective-permute-start.9 = (bf16[64,1536]{1,0:T(8,128)(2,1)S(1)}, bf16[64,1536]{1,0:T(8,128)(2,1)S(1)}, u32[]{:S(2)}, u32[]{:S(2)}) collective-permute-start(bf16[64,1536]{1,0:T(8,128)(2,1)S(1)} %bitcast.12), channel_id=1, source_target_pairs={{0,1},{1,0},{2,3},{3,2},{4,5},{5,4},{6,7},{7,6},{8,9},{9,8},{10,11... | collective-permute-start | bytes 589832 | tf_op jit(solution)/shard_map/ppermute | solution.py:395
  16.1 1.4 %collective-permute-start.10 = (bf16[16,1536]{1,0:T(8,128)(2,1)S(1)}, bf16[16,1536]{1,0:T(8,128)(2,1)S(1)}, u32[]{:S(2)}, u32[]{:S(2)}) collective-permute-start(bf16[16,1536]{1,0:T(8,128)(2,1)S(1)} %shard_map.67.refs_6_), channel_id=1, source_target_pairs={{0,1},{1,0},{2,3},{3,2},{4,5},{5,4},{6,7},{7,6},{8,9},{9,8},{10,11... | collective-permute-start | bytes 147464 | tf_op jit(solution)/shard_map/ppermute | solution.py:395
  17.5 12.6 %copy-start.2 = (bf16[16,4608]{1,0:T(8,128)(2,1)S(1)}, bf16[16,4608]{1,0:T(8,128)(2,1)}, u32[]{:S(2)}) copy-start(bf16[16,4608]{1,0:T(8,128)(2,1)} %value_ref.1) | copy-start | bytes 442372
  18.0 3.7 %collective-permute-start.12 = (bf16[16,1664]{1,0:T(8,128)(2,1)S(1)}, bf16[16,1664]{1,0:T(8,128)(2,1)S(1)}, u32[]{:S(2)}, u32[]{:S(2)}) collective-permute-start(bf16[16,1664]{1,0:T(8,128)(2,1)S(1)} %get-tuple-element.38), channel_id=1, source_target_pairs={{0,5},{1,4},{2,7},{3,6},{4,1},{5,0},{6,3},{7,2},{8,13},{9,12},{10,... | collective-permute-start | bytes 159752 | tf_op jit(solution)/shard_map/ppermute | solution.py:395
  19.5 5.2 %collective-permute-start.11 = (bf16[16,1664]{1,0:T(8,128)(2,1)S(1)}, bf16[16,1664]{1,0:T(8,128)(2,1)S(1)}, u32[]{:S(2)}, u32[]{:S(2)}) collective-permute-start(bf16[16,1664]{1,0:T(8,128)(2,1)S(1)} %get-tuple-element.36), channel_id=1, source_target_pairs={{0,5},{1,4},{2,7},{3,6},{4,1},{5,0},{6,3},{7,2},{8,13},{9,12},{10,... | collective-permute-start | bytes 159752 | tf_op jit(solution)/shard_map/ppermute | solution.py:395
  21.7 5.0 %collective-permute-start.13 = (bf16[16,1664]{1,0:T(8,128)(2,1)S(1)}, bf16[16,1664]{1,0:T(8,128)(2,1)S(1)}, u32[]{:S(2)}, u32[]{:S(2)}) collective-permute-start(bf16[16,1664]{1,0:T(8,128)(2,1)S(1)} %add.25), channel_id=1, source_target_pairs={{0,9},{1,8},{2,11},{3,10},{4,13},{5,12},{6,15},{7,14},{8,1},{9,0},... | collective-permute-start | bytes 159752 | tf_op jit(solution)/shard_map/ppermute | solution.py:395
  26.8 3.3 %collective-permute-start.14 = (bf16[8,1664]{1,0:T(8,128)(2,1)S(1)}, bf16[8,1664]{1,0:T(8,128)(2,1)S(1)}, u32[]{:S(2)}, u32[]{:S(2)}) collective-permute-start(bf16[8,1664]{1,0:T(8,128)(2,1)S(1)} %get-tuple-element.39), channel_id=1, source_target_pairs={{0,3},{1,2},{2,1},{3,0},{4,7},{5,6},{6,5},{7,4},{8,11},{9,10},{10,... | collective-permute-start | bytes 79880 | tf_op jit(solution)/shard_map/ppermute | solution.py:395

commit v8 on v7

--- a/solution.py
+++ b/solution.py
@@ -122,11 +122,16 @@
     return rank // CLASS * (2 * CLASS) + class_of(device) * CLASS + rank % CLASS
 
 
+def rank_of_row(row, half):
+    return half - 1 - row % half
+
+
 def class_order(beams, device):
     row = lax.broadcasted_iota(jnp.int32, (beams, beams), 0)
     col = lax.broadcasted_iota(jnp.int32, (beams, beams), 1)
     half = beams // 2
-    place = rank_in_class(col) + jnp.where(class_of(col) == class_of(device), 0, half)
+    place = rank_of_row(rank_in_class(col), half)
+    place = place + jnp.where(class_of(col) == class_of(device), 0, half)
     return (row == place).astype(jnp.bfloat16)
 
 
@@ -188,9 +193,9 @@
         copy.wait()
 
 
-def cross_weights_kernel(lengths_ref, query_ref, keys_ref, out_ref):
+def cross_kernel(lengths_ref, query_ref, frames_ref, out_ref):
     rows, feature = query_ref.shape
-    frames = keys_ref.shape[0]
+    frames = frames_ref.shape[0]
     heads = feature // HD
     live = lax.broadcasted_iota(jnp.int32, (rows, frames), 1) < lengths_ref[:, :1]
     scores = []
@@ -198,21 +203,19 @@
         at = slice(head * HD, (head + 1) * HD)
         scores.append(
             lax.dot_general(
-                query_ref[:, at], keys_ref[:, at], OVER_LAST, preferred_element_type=jnp.float32
+                query_ref[:, at], frames_ref[:, at], OVER_LAST, preferred_element_type=jnp.float32
             )
         )
+    weights = []
     for head in range(heads):
         masked = jnp.where(live, scores[head] * HD ** (-0.5), MASKED)
         raised = jnp.where(live, jnp.exp(masked - jnp.max(masked, axis=1, keepdims=True)), 0.0)
-        weights = raised / jnp.sum(raised, axis=1, keepdims=True)
-        out_ref[head] = weights.astype(jnp.bfloat16)
-
-
-def cross_values_kernel(weights_ref, values_ref, out_ref):
-    for head in range(weights_ref.shape[0]):
+        weights.append((raised / jnp.sum(raised, axis=1, keepdims=True)).astype(jnp.bfloat16))
+    for head in range(heads):
         at = slice(head * HD, (head + 1) * HD)
+        value_at = slice(feature + head * HD, feature + (head + 1) * HD)
         out_ref[:, at] = jnp.dot(
-            weights_ref[head], values_ref[:, at], preferred_element_type=jnp.float32
+            weights[head], frames_ref[:, value_at], preferred_element_type=jnp.float32
         ).astype(jnp.bfloat16)
 
 
@@ -227,7 +230,7 @@
 
 def self_weights_kernel(masks, counts, *refs):
     query_refs, refs = refs[:counts], refs[counts:]
-    *cache_refs, weight_ref, share_ref, terms_ref, spread_ref = refs
+    *cache_refs, weight_ref, share_ref, spread_ref = refs
     me = lax.axis_index("utt").astype(jnp.int32)
     mine = class_of(me)
     pair_keys, feature = cache_refs[-1].shape
@@ -238,7 +241,8 @@
     queries = jnp.concatenate([ref[...] for ref in query_refs], axis=0)
     extra = queries[:, feature:].astype(jnp.float32)
 
-    utt = utt_of_rank(lax.broadcasted_iota(jnp.int32, (half_beams, LANES), 0), me)
+    utt = lax.broadcasted_iota(jnp.int32, (half_beams, LANES), 0)
+    utt = utt_of_rank(rank_of_row(utt, half_beams), me)
     lane = lax.broadcasted_iota(jnp.int32, (half_beams, LANES), 1)
     table = jnp.zeros((half_beams, LANES), jnp.float32)
     for at, mask in enumerate(masks):
@@ -256,7 +260,7 @@
         axis=0,
     ).astype(jnp.int32)
 
-    row_rank = lax.broadcasted_iota(jnp.int32, (rows, keys), 0) % half_beams
+    row_rank = rank_of_row(lax.broadcasted_iota(jnp.int32, (rows, keys), 0), half_beams)
     key = lax.broadcasted_iota(jnp.int32, (rows, keys), 1)
     key_rank = key % pair_keys // history
     run = key // pair_keys
@@ -268,27 +272,28 @@
     row_live = (chosen // (group + 1)) == (me // (group + 1))
 
     tiles = [slice(at, at + LANES) for at in range(0, keys, LANES)]
+    row_lane = lax.broadcasted_iota(jnp.int32, (rows, LANES), 1)
+    packed = jnp.zeros((rows, LANES), jnp.float32)
     for head in range(heads):
         at = slice(head * HD, (head + 1) * HD)
         scores = lax.dot_general(
             queries[:, at], cached(*cache_refs, mine, at), OVER_LAST, preferred_element_type=jnp.float32
         )
         scores = jnp.where(live, scores, 0.0)
-        rest = sum(scores[:, tile] for tile in tiles)
-        for term_at in range(3):
-            term = rest.astype(jnp.bfloat16)
-            rest = rest - term.astype(jnp.float32)
-            terms_ref[head * rows : (head + 1) * rows, term_at * LANES : (term_at + 1) * LANES] = term
-    row_lane = lax.broadcasted_iota(jnp.int32, (rows, LANES), 1)
-    fold = lax.broadcasted_iota(jnp.int32, (3 * LANES, LANES), 0) % history
-    fold = fold == lax.broadcasted_iota(jnp.int32, (3 * LANES, LANES), 1) % history
+        scores = sum(scores[:, tile] for tile in tiles)
+        scores = scores + pltpu.roll(scores, pair_keys, 1)
+        shift = (head + 1) * history % pair_keys
+        scores = jnp.concatenate(
+            [
+                pltpu.roll(scores[row : row + half_beams], shift, 1, stride=history, stride_axis=0)
+                for row in range(0, rows, half_beams)
+            ],
+            axis=0,
+        )
+        packed = jnp.where(row_lane // history == head, scores, packed)
+    fold = lax.broadcasted_iota(jnp.int32, (LANES, LANES), 0) % history
+    fold = fold == lax.broadcasted_iota(jnp.int32, (LANES, LANES), 1) % history
     fold = fold.astype(jnp.bfloat16)
-    folded = jnp.dot(terms_ref[...], fold, preferred_element_type=jnp.float32)
-    packed = jnp.zeros((rows, LANES), jnp.float32)
-    for head in range(heads):
-        packed = jnp.where(
-            row_lane // history == head, folded[head * rows : (head + 1) * rows], packed
-        )
     packed = packed * HD ** (-0.5)
     part = lax.broadcasted_iota(jnp.int32, (LANES, LANES), 0)
     spread = lax.broadcasted_iota(jnp.int32, (LANES, LANES), 1) // history
@@ -316,7 +321,7 @@
         spread_ref[head * rows : (head + 1) * rows] = jnp.where(
             row_lane // history == head, packed, jnp.zeros_like(packed)
         )
-    weights = jnp.dot(spread_ref[...], fold[:LANES], preferred_element_type=jnp.float32)
+    weights = jnp.dot(spread_ref[...], fold, preferred_element_type=jnp.float32)
     for head in range(heads):
         for tile in tiles:
             weight_ref[head, :, tile] = jnp.where(
@@ -338,7 +343,8 @@
         out_ref[:, feature:] = share_ref[block]
 
     place = lax.broadcasted_iota(jnp.int32, (rows, beams), 1)
-    pick_utt = utt_of_rank(lax.broadcasted_iota(jnp.int32, (rows, beams), 0) % half_beams, me)
+    pick_utt = lax.broadcasted_iota(jnp.int32, (rows, beams), 0)
+    pick_utt = utt_of_rank(rank_of_row(pick_utt, half_beams), me)
     row_beam = me ^ jnp.concatenate(
         [jnp.full((half_beams, beams), mask, jnp.int32) for mask in rows_of(masks, beams)], axis=0
     )
@@ -436,40 +442,24 @@
     frame_count = jnp.broadcast_to(lengths.reshape(1, 1), (1, LANES))
     held = jnp.concatenate([own + lists, pair_rows], axis=0)
 
-    frames_kv = enc_kv.reshape(frames, 2 * feature)
-    cross_weights = pl.pallas_call(
-        cross_weights_kernel,
-        out_shape=jax.ShapeDtypeStruct((heads, rows, frames), jnp.bfloat16),
+    cross_near = pl.pallas_call(
+        cross_kernel,
+        out_shape=jax.ShapeDtypeStruct((rows, feature), jnp.bfloat16),
         grid=(1,),
-        in_specs=[
-            whole((1, LANES)),
-            whole((rows, feature)),
-            pl.BlockSpec((frames, feature), lambda i: (0, 0)),
-        ],
-        out_specs=whole((heads, rows, frames)),
+        in_specs=[whole((1, LANES)), whole((rows, feature)), whole((frames, 2 * feature))],
+        out_specs=whole((rows, feature)),
         compiler_params=params,
-    )(frame_count, after(cross_queries, held), frames_kv)
+    )(frame_count, after(cross_queries, held), enc_kv.reshape(frames, 2 * feature))
     far = swap(after(near, other), CORE)
     blocks = {0: held}
     for bits in hops:
         for mask, block in list(blocks.items()):
-            blocks[mask ^ bits] = swap(after(block, cross_weights) if mask else block, bits)
+            blocks[mask ^ bits] = swap(after(block, cross_near) if mask else block, bits)
     masks, gathered = list(blocks), list(blocks.values())
 
-    cross_near = pl.pallas_call(
-        cross_values_kernel,
-        out_shape=jax.ShapeDtypeStruct((rows, feature), jnp.bfloat16),
-        grid=(1,),
-        in_specs=[
-            whole((heads, rows, frames)),
-            pl.BlockSpec((frames, feature), lambda i: (0, 1)),
-        ],
-        out_specs=whole((rows, feature)),
-        compiler_params=params,
-    )(after(cross_weights, *gathered[:-1]), frames_kv)
     cross_far = swap(cross_near, CORE)
 
-    pair_far_keys = swap(after(pair_keys, blocks[hops[0]]), CORE)
+    pair_far_keys = swap(after(pair_keys, *gathered[:-1]), CORE)
     pair_far_values = swap(after(pair_values, gathered[-1], cross_near), CORE)
 
     all_rows = rows * len(masks)
@@ -487,10 +477,7 @@
         in_specs=[whole(block.shape) for block in gathered]
         + [in_keys, in_keys, pair_spec, pair_spec],
         out_specs=(whole(weight_shape.shape), whole(share_shape.shape)),
-        scratch_shapes=[
-            pltpu.VMEM((heads * all_rows, 3 * LANES), jnp.bfloat16),
-            pltpu.VMEM((heads * all_rows, LANES), jnp.bfloat16),
-        ],
+        scratch_shapes=[pltpu.VMEM((heads * all_rows, LANES), jnp.bfloat16)],
         compiler_params=params,
     )(*gathered, near, far, pair_keys, pair_far_keys)
     parts = pl.pallas_call(
@@ -550,6 +537,7 @@
             and beams % 16 == 0
             and history & (history - 1) == 0
             and heads * history <= LANES
+            and beams * history == LANES
             and 3 * heads <= PARENT_LANE
             and PARENT_LANE + 2 * beams <= LANES
         )

time: 31.7 us -> 31.5 us (level)
  waiting for transfers between devices: 7.77 us -> 8.41 us
  starting transfers between devices: 17.6 us -> 17 us
    ppermute x15, waiting for transfers between devices: 7.77 us -> 8.41 us  [swap(): return lax.ppermute(array, 'utt', [(i, i ^ bits) for i in range(devices)])]
    ppermute x15, starting transfers between devices: 17.6 us -> 17 us  [swap(): return lax.ppermute(array, 'utt', [(i, i ^ bits) for i in range(devices)])]
    pallas_call x2 -> x1, Pallas kernels: 0.77 us -> 0.6 us  [body_by_parent(): pl.pallas_call(cross_kernel, out_shape=jax.ShapeDtypeStruct((rows, featur...]
  transfers between devices with their start and end apart: 15 -> 15, of which waited for: 6 -> 6; matrix products, arithmetic and copies ran while one was open for 0% -> 0% of each run, Pallas kernels for 7% -> 6%
where the time goes in v8:
time: 31.5 us; the launch traced here: 30.9 us
  starting transfers between devices  17 us (54%)
  waiting for transfers between devices  8.41 us (27%)
  Pallas kernels  4.52 us (14%)
  between operations  0.74 us (2%)
    ppermute x15, starting transfers between devices, swap(): return lax.ppermute(array, 'utt', [(i, i ^ bits) for i in range(devices)])  17 us
    ppermute x15, waiting for transfers between devices, swap(): return lax.ppermute(array, 'utt', [(i, i ^ bits) for i in range(devices)])  8.41 us
    pallas_call x1, Pallas kernels, body_by_parent(): pl.pallas_call(pack_kernel, out_shape=(half_rows, half_rows, half_cache,...  1.29 us
    pallas_call x1, Pallas kernels, body_by_parent(): pl.pallas_call(functools.partial(self_weights_kernel, tuple(masks), len(g...  1.27 us
    pallas_call x1, Pallas kernels, body_by_parent(): pl.pallas_call(functools.partial(finish_kernel, history), out_shape=jax.S...  0.93 us
  transfers between devices with their start and end apart: 15, of which 6 were waited for; matrix products, arithmetic and copies ran while one was open for 0% of the time, Pallas kernels for 6%

profile of v8, /device:TPU:0, one launch (start us, length us, event | category | flops | bytes accessed | tf_op | source)
XLA Modules:
  0.0 30.9 jit_solution(15567654463186045115)
XLA Ops:
  0.0 1.3 %shard_map.64 = (bf16[8,1664]{1,0:T(8,128)(2,1)S(1)}, bf16[8,1664]{1,0:T(8,128)(2,1)S(1)}, bf16[4,16,1536]{2,1,0:T(8,128)(2,1)S(1)}, bf16[4,16,1536]{2,1,0:T(8,128)(2,1)S(1)}) custom-call(bf16[16,4608]{1,0:T(8,128)(2,1)} %value_ref.1, s32[1,16]{1,0:T(1,128)} %parents_hbm_ref.1, bf16[4,2,16,3072]{3,2,1,0:T(8,128)(2,1)} %bitcast.6), custom_call_target="tpu_custom_call" | custom-call | flops 4000000000 | bytes 1572864 | tf_op jit(solution)/shard_map/pallas_call | solution.py:414
  1.3 2.5 %collective-permute-start.1 = (bf16[8,1664]{1,0:T(8,128)(2,1)S(1)}, bf16[8,1664]{1,0:T(8,128)(2,1)S(1)}, u32[]{:S(2)}, u32[]{:S(2)}) collective-permute-start(bf16[8,1664]{1,0:T(8,128)(2,1)S(1)} %get-tuple-element.22), channel_id=1, source_target_pairs={{0,3},{1,2},{2,1},{3,0},{4,7},{5,6},{6,5},{7,4},{8,11},{9,10},{10,... | collective-permute-start | bytes 79880 | tf_op jit(solution)/shard_map/ppermute | solution.py:401
  3.8 0.7 %collective-permute-start = (s32[1,16]{1,0:T(1,128)S(1)}, s32[1,16]{1,0:T(1,128)S(1)}, u32[]{:S(2)}, u32[]{:S(2)}) collective-permute-start(s32[1,16]{1,0:T(1,128)S(1)} %copy-done.4), channel_id=1, source_target_pairs={{0,1},{1,0},{2,3},{3,2},{4,5},{5,4},{6,7},{7,6},{8,9},{9,8},{10,11... | collective-permute-start | bytes 200 | tf_op jit(solution)/shard_map/ppermute | solution.py:401
  4.6 1.6 %collective-permute-start.8 = (bf16[4,16,1536]{2,1,0:T(8,128)(2,1)S(1)}, bf16[4,16,1536]{2,1,0:T(8,128)(2,1)S(1)}, u32[]{:S(2)}, u32[]{:S(2)}) collective-permute-start(bf16[4,16,1536]{2,1,0:T(8,128)(2,1)S(1)} %get-tuple-element.31), channel_id=1, source_target_pairs={{0,3},{1,2},{2,1},{3,0},{4,7},{5,6},{6,5},{7,4},{8,11},{9,10},{10,... | collective-permute-start | bytes 589832 | tf_op jit(solution)/shard_map/ppermute | solution.py:401
  6.4 2.8 %collective-permute-start.2 = (bf16[16,1664]{1,0:T(8,128)(2,1)S(1)}, bf16[16,1664]{1,0:T(8,128)(2,1)S(1)}, u32[]{:S(2)}, u32[]{:S(2)}) collective-permute-start(bf16[16,1664]{1,0:T(8,128)(2,1)S(1)} %pad_maximum_fusion.refs_0_), channel_id=1, source_target_pairs={{0,9},{1,8},{2,11},{3,10},{4,13},{5,12},{6,15},{7,14},{8,1},{9,0},... | collective-permute-start | bytes 159752 | tf_op jit(solution)/shard_map/ppermute | solution.py:401
  9.8 1.2 %collective-permute-start.3 = (bf16[16,1664]{1,0:T(8,128)(2,1)S(1)}, bf16[16,1664]{1,0:T(8,128)(2,1)S(1)}, u32[]{:S(2)}, u32[]{:S(2)}) collective-permute-start(bf16[16,1664]{1,0:T(8,128)(2,1)S(1)} %pad_maximum_fusion.refs_0_), channel_id=1, source_target_pairs={{0,5},{1,4},{2,7},{3,6},{4,1},{5,0},{6,3},{7,2},{8,13},{9,12},{10,... | collective-permute-start | bytes 159752 | tf_op jit(solution)/shard_map/ppermute | solution.py:401
  11.0 0.6 %shard_map.65.refs_6_ = bf16[16,1536]{1,0:T(8,128)(2,1)S(1)} custom-call(s32[1,128]{1,0:T(1,128)S(1)} %broadcast_in_dim.8.lengths_ref, bf16[16,1536]{1,0:T(8,128)(2,1)S(1)} %copy-done.3, bf16[256,3072]{1,0:T(8,128)(2,1)S(1)} %bitcast.10), custom_call_target="tpu_custom_call" | custom-call | tf_op jit(solution)/shard_map/pallas_call | solution.py:445
  11.6 1.2 %collective-permute-start.4 = (bf16[16,1664]{1,0:T(8,128)(2,1)S(1)}, bf16[16,1664]{1,0:T(8,128)(2,1)S(1)}, u32[]{:S(2)}, u32[]{:S(2)}) collective-permute-start(bf16[16,1664]{1,0:T(8,128)(2,1)S(1)} %collective-permute-done.2.refs_1_), channel_id=1, source_target_pairs={{0,5},{1,4},{2,7},{3,6},{4,1},{5,0},{6,3},{7,2},{8,13},{9,12},{10,... | collective-permute-start | bytes 159752 | tf_op jit(solution)/shard_map/ppermute | solution.py:401
  12.9 0.9 %collective-permute-done.3.refs_2_ = bf16[16,1664]{1,0:T(8,128)(2,1)S(1)} collective-permute-done((bf16[16,1664]{1,0:T(8,128)(2,1)S(1)}, bf16[16,1664]{1,0:T(8,128)(2,1)S(1)}, u32[]{:S(2)}, u32[]{:S(2)}) %collective-permute-start.3) | collective-permute-done | bytes 53280 | tf_op jit(solution)/shard_map/ppermute | solution.py:401
  13.8 0.3 collective-permute-start.7
  14.1 1.2 %collective-permute-done.4.refs_3_ = bf16[16,1664]{1,0:T(8,128)(2,1)S(1)} collective-permute-done((bf16[16,1664]{1,0:T(8,128)(2,1)S(1)}, bf16[16,1664]{1,0:T(8,128)(2,1)S(1)}, u32[]{:S(2)}, u32[]{:S(2)}) %collective-permute-start.4) | collective-permute-done | bytes 53280 | tf_op jit(solution)/shard_map/ppermute | solution.py:401
  15.3 0.4 %collective-permute-done.8 = bf16[4,16,1536]{2,1,0:T(8,128)(2,1)S(1)} collective-permute-done((bf16[4,16,1536]{2,1,0:T(8,128)(2,1)S(1)}, bf16[4,16,1536]{2,1,0:T(8,128)(2,1)S(1)}, u32[]{:S(2)}, u32[]{:S(2)}) %collective-permute-start.8) | collective-permute-done | bytes 196640 | tf_op jit(solution)/shard_map/ppermute | solution.py:401
  15.7 0.4 %collective-permute-start.9 = (bf16[64,1536]{1,0:T(8,128)(2,1)S(1)}, bf16[64,1536]{1,0:T(8,128)(2,1)S(1)}, u32[]{:S(2)}, u32[]{:S(2)}) collective-permute-start(bf16[64,1536]{1,0:T(8,128)(2,1)S(1)} %bitcast.11), channel_id=1, source_target_pairs={{0,1},{1,0},{2,3},{3,2},{4,5},{5,4},{6,7},{7,6},{8,9},{9,8},{10,11... | collective-permute-start | bytes 589832 | tf_op jit(solution)/shard_map/ppermute | solution.py:401
  16.1 0.1 collective-permute-start.10
  16.2 1.3 %shard_map.66 = (bf16[12,64,256]{2,1,0:T(8,128)(2,1)S(1)}, bf16[64,128]{1,0:T(8,128)(2,1)S(1)}) custom-call(bf16[16,1664]{1,0:T(8,128)(2,1)S(1)} %pad_maximum_fusion.refs_0_, bf16[16,1664]{1,0:T(8,128)(2,1)S(1)} %collective-permute-done.2.refs_1_, bf16[16,1664]{1,0:T(8,128)(2,1)S(1)} %collective-permute-done.3.refs_2_, ...), custom_call_target="tpu_custom_call" | custom-call | tf_op jit(solution)/shard_map/pallas_call | solution.py:473
  17.5 0.4 %shard_map.67 = (bf16[16,1664]{1,0:T(8,128)(2,1)S(1)}, bf16[16,1664]{1,0:T(8,128)(2,1)S(1)}, bf16[16,1664]{1,0:T(8,128)(2,1)S(1)}, bf16[16,1664]{1,0:T(8,128)(2,1)S(1)}) custom-call(bf16[12,64,256]{2,1,0:T(8,128)(2,1)S(1)} %get-tuple-element.29.refs_0_, bf16[64,128]{1,0:T(8,128)(2,1)S(1)} %get-tuple-element.30.refs_1_, bf16[4,2,16,3072]{3,2,1,0:T(8,128)(2,1)S(1)} %bitcast.9, ...), custom_call_target="tpu_custom_call" | custom-call | tf_op jit(solution)/shard_map/pallas_call | solution.py:483
  18.0 1.4 %collective-permute-start.12 = (bf16[16,1664]{1,0:T(8,128)(2,1)S(1)}, bf16[16,1664]{1,0:T(8,128)(2,1)S(1)}, u32[]{:S(2)}, u32[]{:S(2)}) collective-permute-start(bf16[16,1664]{1,0:T(8,128)(2,1)S(1)} %get-tuple-element.36), channel_id=1, source_target_pairs={{0,5},{1,4},{2,7},{3,6},{4,1},{5,0},{6,3},{7,2},{8,13},{9,12},{10,... | collective-permute-start | bytes 159752 | tf_op jit(solution)/shard_map/ppermute | solution.py:401
  19.3 0.4 %collective-permute-start.11 = (bf16[16,1664]{1,0:T(8,128)(2,1)S(1)}, bf16[16,1664]{1,0:T(8,128)(2,1)S(1)}, u32[]{:S(2)}, u32[]{:S(2)}) collective-permute-start(bf16[16,1664]{1,0:T(8,128)(2,1)S(1)} %get-tuple-element.34), channel_id=1, source_target_pairs={{0,5},{1,4},{2,7},{3,6},{4,1},{5,0},{6,3},{7,2},{8,13},{9,12},{10,... | collective-permute-start | bytes 159752 | tf_op jit(solution)/shard_map/ppermute | solution.py:401
  19.8 1.8 %collective-permute-done.12 = bf16[16,1664]{1,0:T(8,128)(2,1)S(1)} collective-permute-done((bf16[16,1664]{1,0:T(8,128)(2,1)S(1)}, bf16[16,1664]{1,0:T(8,128)(2,1)S(1)}, u32[]{:S(2)}, u32[]{:S(2)}) %collective-permute-start.12) | collective-permute-done | bytes 53280 | tf_op jit(solution)/shard_map/ppermute | solution.py:401
  21.6 2.9 %collective-permute-start.13 = (bf16[16,1664]{1,0:T(8,128)(2,1)S(1)}, bf16[16,1664]{1,0:T(8,128)(2,1)S(1)}, u32[]{:S(2)}, u32[]{:S(2)}) collective-permute-start(bf16[16,1664]{1,0:T(8,128)(2,1)S(1)} %add.25), channel_id=1, source_target_pairs={{0,9},{1,8},{2,11},{3,10},{4,13},{5,12},{6,15},{7,14},{8,1},{9,0},... | collective-permute-start | bytes 159752 | tf_op jit(solution)/shard_map/ppermute | solution.py:401
  24.5 2.0 %collective-permute-done.13 = bf16[16,1664]{1,0:T(8,128)(2,1)S(1)} collective-permute-done((bf16[16,1664]{1,0:T(8,128)(2,1)S(1)}, bf16[16,1664]{1,0:T(8,128)(2,1)S(1)}, u32[]{:S(2)}, u32[]{:S(2)}) %collective-permute-start.13) | collective-permute-done | bytes 53280 | tf_op jit(solution)/shard_map/ppermute | solution.py:401
  26.6 1.3 %collective-permute-start.14 = (bf16[8,1664]{1,0:T(8,128)(2,1)S(1)}, bf16[8,1664]{1,0:T(8,128)(2,1)S(1)}, u32[]{:S(2)}, u32[]{:S(2)}) collective-permute-start(bf16[8,1664]{1,0:T(8,128)(2,1)S(1)} %get-tuple-element.37), channel_id=1, source_target_pairs={{0,3},{1,2},{2,1},{3,0},{4,7},{5,6},{6,5},{7,4},{8,11},{9,10},{10,... | collective-permute-start | bytes 79880 | tf_op jit(solution)/shard_map/ppermute | solution.py:401
  27.9 2.0 %collective-permute-done.14.came_ref = bf16[8,1664]{1,0:T(8,128)(2,1)S(1)} collective-permute-done((bf16[8,1664]{1,0:T(8,128)(2,1)S(1)}, bf16[8,1664]{1,0:T(8,128)(2,1)S(1)}, u32[]{:S(2)}, u32[]{:S(2)}) %collective-permute-start.14) | collective-permute-done | bytes 26656 | tf_op jit(solution)/shard_map/ppermute | solution.py:401
  29.9 0.9 %shard_map.68 = bf16[16,1536]{1,0:T(8,128)(2,1)} custom-call(bf16[8,1664]{1,0:T(8,128)(2,1)S(1)} %get-tuple-element.38.mine_ref, bf16[8,1664]{1,0:T(8,128)(2,1)S(1)} %collective-permute-done.14.came_ref, bf16[16,4608]{1,0:T(8,128)(2,1)S(1)} %copy-done.2), custom_call_target="tpu_custom_call" | custom-call | tf_op jit(solution)/shard_map/pallas_call | solution.py:503
  (29 shorter events, 0.4 us)
Async XLA Ops:
  0.0 3.8 %copy-start.4 = (s32[1,16]{1,0:T(1,128)S(1)}, s32[1,16]{1,0:T(1,128)}, u32[]{:S(2)}) copy-start(s32[1,16]{1,0:T(1,128)} %parents_hbm_ref.1) | copy-start | bytes 196
  0.0 4.6 %copy-start = (bf16[16,8,3072]{2,1,0:T(8,128)(2,1)S(1)}, bf16[16,8,3072]{2,1,0:T(8,128)(2,1)}, u32[]{:S(2)}) copy-start(bf16[16,8,3072]{2,1,0:T(8,128)(2,1)} %param.6) | copy-start | bytes 2359300
  0.0 11.0 %copy-start.1 = (bf16[1,256,3072]{2,1,0:T(8,128)(2,1)S(1)}, bf16[1,256,3072]{2,1,0:T(8,128)(2,1)}, u32[]{:S(2)}) copy-start(bf16[1,256,3072]{2,1,0:T(8,128)(2,1)} %param.9) | copy-start | bytes 4718596
  0.0 11.0 %copy-start.3 = (bf16[16,1536]{1,0:T(8,128)(2,1)S(1)}, bf16[16,1536]{1,0:T(8,128)(2,1)}, u32[]{:S(2)}) copy-start(bf16[16,1536]{1,0:T(8,128)(2,1)} %query_ref) | copy-start | bytes 147460
  1.3 5.0 %collective-permute-start.1 = (bf16[8,1664]{1,0:T(8,128)(2,1)S(1)}, bf16[8,1664]{1,0:T(8,128)(2,1)S(1)}, u32[]{:S(2)}, u32[]{:S(2)}) collective-permute-start(bf16[8,1664]{1,0:T(8,128)(2,1)S(1)} %get-tuple-element.22), channel_id=1, source_target_pairs={{0,3},{1,2},{2,1},{3,0},{4,7},{5,6},{6,5},{7,4},{8,11},{9,10},{10,... | collective-permute-start | bytes 79880 | tf_op jit(solution)/shard_map/ppermute | solution.py:401
  3.8 2.4 %collective-permute-start = (s32[1,16]{1,0:T(1,128)S(1)}, s32[1,16]{1,0:T(1,128)S(1)}, u32[]{:S(2)}, u32[]{:S(2)}) collective-permute-start(s32[1,16]{1,0:T(1,128)S(1)} %copy-done.4), channel_id=1, source_target_pairs={{0,1},{1,0},{2,3},{3,2},{4,5},{5,4},{6,7},{7,6},{8,9},{9,8},{10,11... | collective-permute-start | bytes 200 | tf_op jit(solution)/shard_map/ppermute | solution.py:401
  4.5 9.3 %collective-permute-start.6 = (bf16[4,16,1536]{2,1,0:T(8,128)(2,1)S(1)}, bf16[4,16,1536]{2,1,0:T(8,128)(2,1)S(1)}, u32[]{:S(2)}, u32[]{:S(2)}) collective-permute-start(bf16[4,16,1536]{2,1,0:T(8,128)(2,1)S(1)} %get-tuple-element.27), channel_id=1, source_target_pairs={{0,3},{1,2},{2,1},{3,0},{4,7},{5,6},{6,5},{7,4},{8,11},{9,10},{10,... | collective-permute-start | bytes 589832 | tf_op jit(solution)/shard_map/ppermute | solution.py:401
  4.6 11.6 %collective-permute-start.5 = (bf16[4,2,16,3072]{3,2,1,0:T(8,128)(2,1)S(1)}, bf16[4,2,16,3072]{3,2,1,0:T(8,128)(2,1)S(1)}, u32[]{:S(2)}, u32[]{:S(2)}) collective-permute-start(bf16[4,2,16,3072]{3,2,1,0:T(8,128)(2,1)S(1)} %bitcast.7), channel_id=1, source_target_pairs={{0,1},{1,0},{2,3},{3,2},{4,5},{5,4},{6,7},{7,6},{8,9},{9,8},{10,11... | collective-permute-start | bytes 2359304 | tf_op jit(solution)/shard_map/ppermute | solution.py:401
  4.6 11.1 %collective-permute-start.8 = (bf16[4,16,1536]{2,1,0:T(8,128)(2,1)S(1)}, bf16[4,16,1536]{2,1,0:T(8,128)(2,1)S(1)}, u32[]{:S(2)}, u32[]{:S(2)}) collective-permute-start(bf16[4,16,1536]{2,1,0:T(8,128)(2,1)S(1)} %get-tuple-element.31), channel_id=1, source_target_pairs={{0,3},{1,2},{2,1},{3,0},{4,7},{5,6},{6,5},{7,4},{8,11},{9,10},{10,... | collective-permute-start | bytes 589832 | tf_op jit(solution)/shard_map/ppermute | solution.py:401
  6.4 5.3 %collective-permute-start.2 = (bf16[16,1664]{1,0:T(8,128)(2,1)S(1)}, bf16[16,1664]{1,0:T(8,128)(2,1)S(1)}, u32[]{:S(2)}, u32[]{:S(2)}) collective-permute-start(bf16[16,1664]{1,0:T(8,128)(2,1)S(1)} %pad_maximum_fusion.refs_0_), channel_id=1, source_target_pairs={{0,9},{1,8},{2,11},{3,10},{4,13},{5,12},{6,15},{7,14},{8,1},{9,0},... | collective-permute-start | bytes 159752 | tf_op jit(solution)/shard_map/ppermute | solution.py:401
  9.8 4.0 %collective-permute-start.3 = (bf16[16,1664]{1,0:T(8,128)(2,1)S(1)}, bf16[16,1664]{1,0:T(8,128)(2,1)S(1)}, u32[]{:S(2)}, u32[]{:S(2)}) collective-permute-start(bf16[16,1664]{1,0:T(8,128)(2,1)S(1)} %pad_maximum_fusion.refs_0_), channel_id=1, source_target_pairs={{0,5},{1,4},{2,7},{3,6},{4,1},{5,0},{6,3},{7,2},{8,13},{9,12},{10,... | collective-permute-start | bytes 159752 | tf_op jit(solution)/shard_map/ppermute | solution.py:401
  11.6 3.6 %collective-permute-start.4 = (bf16[16,1664]{1,0:T(8,128)(2,1)S(1)}, bf16[16,1664]{1,0:T(8,128)(2,1)S(1)}, u32[]{:S(2)}, u32[]{:S(2)}) collective-permute-start(bf16[16,1664]{1,0:T(8,128)(2,1)S(1)} %collective-permute-done.2.refs_1_), channel_id=1, source_target_pairs={{0,5},{1,4},{2,7},{3,6},{4,1},{5,0},{6,3},{7,2},{8,13},{9,12},{10,... | collective-permute-start | bytes 159752 | tf_op jit(solution)/shard_map/ppermute | solution.py:401
  13.8 2.4 %collective-permute-start.7 = (bf16[64,1536]{1,0:T(8,128)(2,1)S(1)}, bf16[64,1536]{1,0:T(8,128)(2,1)S(1)}, u32[]{:S(2)}, u32[]{:S(2)}) collective-permute-start(bf16[64,1536]{1,0:T(8,128)(2,1)S(1)} %bitcast.13), channel_id=1, source_target_pairs={{0,1},{1,0},{2,3},{3,2},{4,5},{5,4},{6,7},{7,6},{8,9},{9,8},{10,11... | collective-permute-start | bytes 589832 | tf_op jit(solution)/shard_map/ppermute | solution.py:401
  15.7 1.8 %collective-permute-start.9 = (bf16[64,1536]{1,0:T(8,128)(2,1)S(1)}, bf16[64,1536]{1,0:T(8,128)(2,1)S(1)}, u32[]{:S(2)}, u32[]{:S(2)}) collective-permute-start(bf16[64,1536]{1,0:T(8,128)(2,1)S(1)} %bitcast.11), channel_id=1, source_target_pairs={{0,1},{1,0},{2,3},{3,2},{4,5},{5,4},{6,7},{7,6},{8,9},{9,8},{10,11... | collective-permute-start | bytes 589832 | tf_op jit(solution)/shard_map/ppermute | solution.py:401
  16.1 1.4 %collective-permute-start.10 = (bf16[16,1536]{1,0:T(8,128)(2,1)S(1)}, bf16[16,1536]{1,0:T(8,128)(2,1)S(1)}, u32[]{:S(2)}, u32[]{:S(2)}) collective-permute-start(bf16[16,1536]{1,0:T(8,128)(2,1)S(1)} %shard_map.65.refs_6_), channel_id=1, source_target_pairs={{0,1},{1,0},{2,3},{3,2},{4,5},{5,4},{6,7},{7,6},{8,9},{9,8},{10,11... | collective-permute-start | bytes 147464 | tf_op jit(solution)/shard_map/ppermute | solution.py:401
  17.5 12.4 %copy-start.2 = (bf16[16,4608]{1,0:T(8,128)(2,1)S(1)}, bf16[16,4608]{1,0:T(8,128)(2,1)}, u32[]{:S(2)}) copy-start(bf16[16,4608]{1,0:T(8,128)(2,1)} %value_ref.1) | copy-start | bytes 442372
  18.0 3.6 %collective-permute-start.12 = (bf16[16,1664]{1,0:T(8,128)(2,1)S(1)}, bf16[16,1664]{1,0:T(8,128)(2,1)S(1)}, u32[]{:S(2)}, u32[]{:S(2)}) collective-permute-start(bf16[16,1664]{1,0:T(8,128)(2,1)S(1)} %get-tuple-element.36), channel_id=1, source_target_pairs={{0,5},{1,4},{2,7},{3,6},{4,1},{5,0},{6,3},{7,2},{8,13},{9,12},{10,... | collective-permute-start | bytes 159752 | tf_op jit(solution)/shard_map/ppermute | solution.py:401
  19.3 5.2 %collective-permute-start.11 = (bf16[16,1664]{1,0:T(8,128)(2,1)S(1)}, bf16[16,1664]{1,0:T(8,128)(2,1)S(1)}, u32[]{:S(2)}, u32[]{:S(2)}) collective-permute-start(bf16[16,1664]{1,0:T(8,128)(2,1)S(1)} %get-tuple-element.34), channel_id=1, source_target_pairs={{0,5},{1,4},{2,7},{3,6},{4,1},{5,0},{6,3},{7,2},{8,13},{9,12},{10,... | collective-permute-start | bytes 159752 | tf_op jit(solution)/shard_map/ppermute | solution.py:401
  21.6 5.0 %collective-permute-start.13 = (bf16[16,1664]{1,0:T(8,128)(2,1)S(1)}, bf16[16,1664]{1,0:T(8,128)(2,1)S(1)}, u32[]{:S(2)}, u32[]{:S(2)}) collective-permute-start(bf16[16,1664]{1,0:T(8,128)(2,1)S(1)} %add.25), channel_id=1, source_target_pairs={{0,9},{1,8},{2,11},{3,10},{4,13},{5,12},{6,15},{7,14},{8,1},{9,0},... | collective-permute-start | bytes 159752 | tf_op jit(solution)/shard_map/ppermute | solution.py:401
  26.6 3.3 %collective-permute-start.14 = (bf16[8,1664]{1,0:T(8,128)(2,1)S(1)}, bf16[8,1664]{1,0:T(8,128)(2,1)S(1)}, u32[]{:S(2)}, u32[]{:S(2)}) collective-permute-start(bf16[8,1664]{1,0:T(8,128)(2,1)S(1)} %get-tuple-element.37), channel_id=1, source_target_pairs={{0,3},{1,2},{2,1},{3,0},{4,7},{5,6},{6,5},{7,4},{8,11},{9,10},{10,... | collective-permute-start | bytes 79880 | tf_op jit(solution)/shard_map/ppermute | solution.py:401

commit v9 on v8

--- a/solution.py
+++ b/solution.py
@@ -424,7 +424,7 @@
         ],
         compiler_params=params,
         cost_estimate=pl.CostEstimate(
-            flops=4_000_000_000, bytes_accessed=4 * near.size, transcendentals=0
+            flops=1_500_000_000, bytes_accessed=4 * near.size, transcendentals=0
         ),
     )(
         in_hbm(new_rows),
@@ -457,9 +457,9 @@
             blocks[mask ^ bits] = swap(after(block, cross_near) if mask else block, bits)
     masks, gathered = list(blocks), list(blocks.values())
 
-    cross_far = swap(cross_near, CORE)
-
-    pair_far_keys = swap(after(pair_keys, *gathered[:-1]), CORE)
+    cross_far = swap(after(cross_near, gathered[2]), CORE)
+
+    pair_far_keys = swap(after(pair_keys, *gathered[:-1], cross_far), CORE)
     pair_far_values = swap(after(pair_values, gathered[-1], cross_near), CORE)
 
     all_rows = rows * len(masks)

time: 31.5 us -> 31.2 us (level)
  transfers between devices with their start and end apart: 15 -> 15, of which waited for: 6 -> 8; matrix products, arithmetic and copies ran while one was open for 0% -> 0% of each run, Pallas kernels for 6% -> 6%
where the time goes in v9:
time: 31.2 us; the launch traced here: 30.8 us
  starting transfers between devices  17.1 us (55%)
  waiting for transfers between devices  8.23 us (26%)
  Pallas kernels  4.52 us (14%)
  between operations  0.76 us (2%)
    ppermute x15, starting transfers between devices, swap(): return lax.ppermute(array, 'utt', [(i, i ^ bits) for i in range(devices)])  17.1 us
    ppermute x15, waiting for transfers between devices, swap(): return lax.ppermute(array, 'utt', [(i, i ^ bits) for i in range(devices)])  8.23 us
    pallas_call x1, Pallas kernels, body_by_parent(): pl.pallas_call(pack_kernel, out_shape=(half_rows, half_rows, half_cache,...  1.29 us
    pallas_call x1, Pallas kernels, body_by_parent(): pl.pallas_call(functools.partial(self_weights_kernel, tuple(masks), len(g...  1.26 us
    pallas_call x1, Pallas kernels, body_by_parent(): pl.pallas_call(functools.partial(finish_kernel, history), out_shape=jax.S...  0.93 us
  transfers between devices with their start and end apart: 15, of which 8 were waited for; matrix products, arithmetic and copies ran while one was open for 0% of the time, Pallas kernels for 6%

profile of v9, /device:TPU:0, one launch (start us, length us, event | category | flops | bytes accessed | tf_op | source)
XLA Modules:
  0.0 30.8 jit_solution(14023996683020978879)
XLA Ops:
  0.0 1.3 %shard_map.64 = (bf16[8,1664]{1,0:T(8,128)(2,1)S(1)}, bf16[8,1664]{1,0:T(8,128)(2,1)S(1)}, bf16[4,16,1536]{2,1,0:T(8,128)(2,1)S(1)}, bf16[4,16,1536]{2,1,0:T(8,128)(2,1)S(1)}) custom-call(bf16[16,4608]{1,0:T(8,128)(2,1)} %value_ref.1, s32[1,16]{1,0:T(1,128)} %parents_hbm_ref.1, bf16[4,2,16,3072]{3,2,1,0:T(8,128)(2,1)} %bitcast.6), custom_call_target="tpu_custom_call" | custom-call | flops 1500000000 | bytes 1572864 | tf_op jit(solution)/shard_map/pallas_call | solution.py:414
  1.3 2.5 %collective-permute-start.1 = (bf16[8,1664]{1,0:T(8,128)(2,1)S(1)}, bf16[8,1664]{1,0:T(8,128)(2,1)S(1)}, u32[]{:S(2)}, u32[]{:S(2)}) collective-permute-start(bf16[8,1664]{1,0:T(8,128)(2,1)S(1)} %get-tuple-element.23), channel_id=1, source_target_pairs={{0,3},{1,2},{2,1},{3,0},{4,7},{5,6},{6,5},{7,4},{8,11},{9,10},{10,... | collective-permute-start | bytes 79880 | tf_op jit(solution)/shard_map/ppermute | solution.py:401
  3.8 0.7 %collective-permute-start = (s32[1,16]{1,0:T(1,128)S(1)}, s32[1,16]{1,0:T(1,128)S(1)}, u32[]{:S(2)}, u32[]{:S(2)}) collective-permute-start(s32[1,16]{1,0:T(1,128)S(1)} %copy-done.4), channel_id=1, source_target_pairs={{0,1},{1,0},{2,3},{3,2},{4,5},{5,4},{6,7},{7,6},{8,9},{9,8},{10,11... | collective-permute-start | bytes 200 | tf_op jit(solution)/shard_map/ppermute | solution.py:401
  4.6 1.6 %collective-permute-start.9 = (bf16[4,16,1536]{2,1,0:T(8,128)(2,1)S(1)}, bf16[4,16,1536]{2,1,0:T(8,128)(2,1)S(1)}, u32[]{:S(2)}, u32[]{:S(2)}) collective-permute-start(bf16[4,16,1536]{2,1,0:T(8,128)(2,1)S(1)} %get-tuple-element.33), channel_id=1, source_target_pairs={{0,3},{1,2},{2,1},{3,0},{4,7},{5,6},{6,5},{7,4},{8,11},{9,10},{10,... | collective-permute-start | bytes 589832 | tf_op jit(solution)/shard_map/ppermute | solution.py:401
  6.4 2.8 %collective-permute-start.2 = (bf16[16,1664]{1,0:T(8,128)(2,1)S(1)}, bf16[16,1664]{1,0:T(8,128)(2,1)S(1)}, u32[]{:S(2)}, u32[]{:S(2)}) collective-permute-start(bf16[16,1664]{1,0:T(8,128)(2,1)S(1)} %pad_maximum_fusion.refs_0_), channel_id=1, source_target_pairs={{0,9},{1,8},{2,11},{3,10},{4,13},{5,12},{6,15},{7,14},{8,1},{9,0},... | collective-permute-start | bytes 159752 | tf_op jit(solution)/shard_map/ppermute | solution.py:401
  9.1 1.2 %collective-permute-start.3 = (bf16[16,1664]{1,0:T(8,128)(2,1)S(1)}, bf16[16,1664]{1,0:T(8,128)(2,1)S(1)}, u32[]{:S(2)}, u32[]{:S(2)}) collective-permute-start(bf16[16,1664]{1,0:T(8,128)(2,1)S(1)} %pad_maximum_fusion.refs_0_), channel_id=1, source_target_pairs={{0,5},{1,4},{2,7},{3,6},{4,1},{5,0},{6,3},{7,2},{8,13},{9,12},{10,... | collective-permute-start | bytes 159752 | tf_op jit(solution)/shard_map/ppermute | solution.py:401
  11.0 0.6 %shard_map.65.refs_6_ = bf16[16,1536]{1,0:T(8,128)(2,1)S(1)} custom-call(s32[1,128]{1,0:T(1,128)S(1)} %broadcast_in_dim.8.lengths_ref, bf16[16,1536]{1,0:T(8,128)(2,1)S(1)} %copy-done.3, bf16[256,3072]{1,0:T(8,128)(2,1)S(1)} %bitcast.10), custom_call_target="tpu_custom_call" | custom-call | tf_op jit(solution)/shard_map/pallas_call | solution.py:445
  11.6 1.5 %collective-permute-start.4 = (bf16[16,1664]{1,0:T(8,128)(2,1)S(1)}, bf16[16,1664]{1,0:T(8,128)(2,1)S(1)}, u32[]{:S(2)}, u32[]{:S(2)}) collective-permute-start(bf16[16,1664]{1,0:T(8,128)(2,1)S(1)} %collective-permute-done.2.refs_1_), channel_id=1, source_target_pairs={{0,5},{1,4},{2,7},{3,6},{4,1},{5,0},{6,3},{7,2},{8,13},{9,12},{10,... | collective-permute-start | bytes 159752 | tf_op jit(solution)/shard_map/ppermute | solution.py:401
  13.1 0.1 collective-permute-done.3.refs_2_
  13.2 0.2 collective-permute-start.7
  13.5 1.0 %collective-permute-done.7.refs_7_ = bf16[16,1536]{1,0:T(8,128)(2,1)S(1)} collective-permute-done((bf16[16,1536]{1,0:T(8,128)(2,1)S(1)}, bf16[16,1536]{1,0:T(8,128)(2,1)S(1)}, u32[]{:S(2)}, u32[]{:S(2)}) %collective-permute-start.7) | collective-permute-done | bytes 49184 | tf_op jit(solution)/shard_map/ppermute | solution.py:401
  14.5 0.2 collective-permute-start.8
  14.7 0.5 %collective-permute-done.4.refs_3_ = bf16[16,1664]{1,0:T(8,128)(2,1)S(1)} collective-permute-done((bf16[16,1664]{1,0:T(8,128)(2,1)S(1)}, bf16[16,1664]{1,0:T(8,128)(2,1)S(1)}, u32[]{:S(2)}, u32[]{:S(2)}) %collective-permute-start.4) | collective-permute-done | bytes 53280 | tf_op jit(solution)/shard_map/ppermute | solution.py:401
  15.2 0.5 %collective-permute-done.9 = bf16[4,16,1536]{2,1,0:T(8,128)(2,1)S(1)} collective-permute-done((bf16[4,16,1536]{2,1,0:T(8,128)(2,1)S(1)}, bf16[4,16,1536]{2,1,0:T(8,128)(2,1)S(1)}, u32[]{:S(2)}, u32[]{:S(2)}) %collective-permute-start.9) | collective-permute-done | bytes 196640 | tf_op jit(solution)/shard_map/ppermute | solution.py:401
  15.9 1.3 %shard_map.66 = (bf16[12,64,256]{2,1,0:T(8,128)(2,1)S(1)}, bf16[64,128]{1,0:T(8,128)(2,1)S(1)}) custom-call(bf16[16,1664]{1,0:T(8,128)(2,1)S(1)} %pad_maximum_fusion.refs_0_, bf16[16,1664]{1,0:T(8,128)(2,1)S(1)} %collective-permute-done.2.refs_1_, bf16[16,1664]{1,0:T(8,128)(2,1)S(1)} %collective-permute-done.3.refs_2_, ...), custom_call_target="tpu_custom_call" | custom-call | tf_op jit(solution)/shard_map/pallas_call | solution.py:473
  17.2 0.4 %shard_map.67 = (bf16[16,1664]{1,0:T(8,128)(2,1)S(1)}, bf16[16,1664]{1,0:T(8,128)(2,1)S(1)}, bf16[16,1664]{1,0:T(8,128)(2,1)S(1)}, bf16[16,1664]{1,0:T(8,128)(2,1)S(1)}) custom-call(bf16[12,64,256]{2,1,0:T(8,128)(2,1)S(1)} %get-tuple-element.31.refs_0_, bf16[64,128]{1,0:T(8,128)(2,1)S(1)} %get-tuple-element.32.refs_1_, bf16[4,2,16,3072]{3,2,1,0:T(8,128)(2,1)S(1)} %bitcast.9, ...), custom_call_target="tpu_custom_call" | custom-call | tf_op jit(solution)/shard_map/pallas_call | solution.py:483
  17.6 1.6 %collective-permute-start.12 = (bf16[16,1664]{1,0:T(8,128)(2,1)S(1)}, bf16[16,1664]{1,0:T(8,128)(2,1)S(1)}, u32[]{:S(2)}, u32[]{:S(2)}) collective-permute-start(bf16[16,1664]{1,0:T(8,128)(2,1)S(1)} %get-tuple-element.38), channel_id=1, source_target_pairs={{0,5},{1,4},{2,7},{3,6},{4,1},{5,0},{6,3},{7,2},{8,13},{9,12},{10,... | collective-permute-start | bytes 159752 | tf_op jit(solution)/shard_map/ppermute | solution.py:401
  19.2 0.2 collective-permute-start.11
  19.4 2.0 %collective-permute-done.12 = bf16[16,1664]{1,0:T(8,128)(2,1)S(1)} collective-permute-done((bf16[16,1664]{1,0:T(8,128)(2,1)S(1)}, bf16[16,1664]{1,0:T(8,128)(2,1)S(1)}, u32[]{:S(2)}, u32[]{:S(2)}) %collective-permute-start.12) | collective-permute-done | bytes 53280 | tf_op jit(solution)/shard_map/ppermute | solution.py:401
  21.4 3.0 %collective-permute-start.13 = (bf16[16,1664]{1,0:T(8,128)(2,1)S(1)}, bf16[16,1664]{1,0:T(8,128)(2,1)S(1)}, u32[]{:S(2)}, u32[]{:S(2)}) collective-permute-start(bf16[16,1664]{1,0:T(8,128)(2,1)S(1)} %add.25), channel_id=1, source_target_pairs={{0,9},{1,8},{2,11},{3,10},{4,13},{5,12},{6,15},{7,14},{8,1},{9,0},... | collective-permute-start | bytes 159752 | tf_op jit(solution)/shard_map/ppermute | solution.py:401
  24.4 2.1 %collective-permute-done.13 = bf16[16,1664]{1,0:T(8,128)(2,1)S(1)} collective-permute-done((bf16[16,1664]{1,0:T(8,128)(2,1)S(1)}, bf16[16,1664]{1,0:T(8,128)(2,1)S(1)}, u32[]{:S(2)}, u32[]{:S(2)}) %collective-permute-start.13) | collective-permute-done | bytes 53280 | tf_op jit(solution)/shard_map/ppermute | solution.py:401
  26.5 1.4 %collective-permute-start.14 = (bf16[8,1664]{1,0:T(8,128)(2,1)S(1)}, bf16[8,1664]{1,0:T(8,128)(2,1)S(1)}, u32[]{:S(2)}, u32[]{:S(2)}) collective-permute-start(bf16[8,1664]{1,0:T(8,128)(2,1)S(1)} %get-tuple-element.39), channel_id=1, source_target_pairs={{0,3},{1,2},{2,1},{3,0},{4,7},{5,6},{6,5},{7,4},{8,11},{9,10},{10,... | collective-permute-start | bytes 79880 | tf_op jit(solution)/shard_map/ppermute | solution.py:401
  27.9 2.0 %collective-permute-done.14.came_ref = bf16[8,1664]{1,0:T(8,128)(2,1)S(1)} collective-permute-done((bf16[8,1664]{1,0:T(8,128)(2,1)S(1)}, bf16[8,1664]{1,0:T(8,128)(2,1)S(1)}, u32[]{:S(2)}, u32[]{:S(2)}) %collective-permute-start.14) | collective-permute-done | bytes 26656 | tf_op jit(solution)/shard_map/ppermute | solution.py:401
  29.9 0.9 %shard_map.68 = bf16[16,1536]{1,0:T(8,128)(2,1)} custom-call(bf16[8,1664]{1,0:T(8,128)(2,1)S(1)} %get-tuple-element.40.mine_ref, bf16[8,1664]{1,0:T(8,128)(2,1)S(1)} %collective-permute-done.14.came_ref, bf16[16,4608]{1,0:T(8,128)(2,1)S(1)} %copy-done.2), custom_call_target="tpu_custom_call" | custom-call | tf_op jit(solution)/shard_map/pallas_call | solution.py:503
  (29 shorter events, 0.6 us)
Async XLA Ops:
  0.0 3.8 %copy-start.4 = (s32[1,16]{1,0:T(1,128)S(1)}, s32[1,16]{1,0:T(1,128)}, u32[]{:S(2)}) copy-start(s32[1,16]{1,0:T(1,128)} %parents_hbm_ref.1) | copy-start | bytes 196
  0.0 4.6 %copy-start = (bf16[16,8,3072]{2,1,0:T(8,128)(2,1)S(1)}, bf16[16,8,3072]{2,1,0:T(8,128)(2,1)}, u32[]{:S(2)}) copy-start(bf16[16,8,3072]{2,1,0:T(8,128)(2,1)} %param.6) | copy-start | bytes 2359300
  0.0 11.0 %copy-start.1 = (bf16[1,256,3072]{2,1,0:T(8,128)(2,1)S(1)}, bf16[1,256,3072]{2,1,0:T(8,128)(2,1)}, u32[]{:S(2)}) copy-start(bf16[1,256,3072]{2,1,0:T(8,128)(2,1)} %param.9) | copy-start | bytes 4718596
  0.0 11.0 %copy-start.3 = (bf16[16,1536]{1,0:T(8,128)(2,1)S(1)}, bf16[16,1536]{1,0:T(8,128)(2,1)}, u32[]{:S(2)}) copy-start(bf16[16,1536]{1,0:T(8,128)(2,1)} %query_ref) | copy-start | bytes 147460
  1.3 5.0 %collective-permute-start.1 = (bf16[8,1664]{1,0:T(8,128)(2,1)S(1)}, bf16[8,1664]{1,0:T(8,128)(2,1)S(1)}, u32[]{:S(2)}, u32[]{:S(2)}) collective-permute-start(bf16[8,1664]{1,0:T(8,128)(2,1)S(1)} %get-tuple-element.23), channel_id=1, source_target_pairs={{0,3},{1,2},{2,1},{3,0},{4,7},{5,6},{6,5},{7,4},{8,11},{9,10},{10,... | collective-permute-start | bytes 79880 | tf_op jit(solution)/shard_map/ppermute | solution.py:401
  3.8 2.4 %collective-permute-start = (s32[1,16]{1,0:T(1,128)S(1)}, s32[1,16]{1,0:T(1,128)S(1)}, u32[]{:S(2)}, u32[]{:S(2)}) collective-permute-start(s32[1,16]{1,0:T(1,128)S(1)} %copy-done.4), channel_id=1, source_target_pairs={{0,1},{1,0},{2,3},{3,2},{4,5},{5,4},{6,7},{7,6},{8,9},{9,8},{10,11... | collective-permute-start | bytes 200 | tf_op jit(solution)/shard_map/ppermute | solution.py:401
  4.5 10.0 %collective-permute-start.6 = (bf16[4,16,1536]{2,1,0:T(8,128)(2,1)S(1)}, bf16[4,16,1536]{2,1,0:T(8,128)(2,1)S(1)}, u32[]{:S(2)}, u32[]{:S(2)}) collective-permute-start(bf16[4,16,1536]{2,1,0:T(8,128)(2,1)S(1)} %get-tuple-element.28), channel_id=1, source_target_pairs={{0,3},{1,2},{2,1},{3,0},{4,7},{5,6},{6,5},{7,4},{8,11},{9,10},{10,... | collective-permute-start | bytes 589832 | tf_op jit(solution)/shard_map/ppermute | solution.py:401
  4.6 11.3 %collective-permute-start.5 = (bf16[4,2,16,3072]{3,2,1,0:T(8,128)(2,1)S(1)}, bf16[4,2,16,3072]{3,2,1,0:T(8,128)(2,1)S(1)}, u32[]{:S(2)}, u32[]{:S(2)}) collective-permute-start(bf16[4,2,16,3072]{3,2,1,0:T(8,128)(2,1)S(1)} %bitcast.7), channel_id=1, source_target_pairs={{0,1},{1,0},{2,3},{3,2},{4,5},{5,4},{6,7},{7,6},{8,9},{9,8},{10,11... | collective-permute-start | bytes 2359304 | tf_op jit(solution)/shard_map/ppermute | solution.py:401
  4.6 11.1 %collective-permute-start.9 = (bf16[4,16,1536]{2,1,0:T(8,128)(2,1)S(1)}, bf16[4,16,1536]{2,1,0:T(8,128)(2,1)S(1)}, u32[]{:S(2)}, u32[]{:S(2)}) collective-permute-start(bf16[4,16,1536]{2,1,0:T(8,128)(2,1)S(1)} %get-tuple-element.33), channel_id=1, source_target_pairs={{0,3},{1,2},{2,1},{3,0},{4,7},{5,6},{6,5},{7,4},{8,11},{9,10},{10,... | collective-permute-start | bytes 589832 | tf_op jit(solution)/shard_map/ppermute | solution.py:401
  6.4 5.2 %collective-permute-start.2 = (bf16[16,1664]{1,0:T(8,128)(2,1)S(1)}, bf16[16,1664]{1,0:T(8,128)(2,1)S(1)}, u32[]{:S(2)}, u32[]{:S(2)}) collective-permute-start(bf16[16,1664]{1,0:T(8,128)(2,1)S(1)} %pad_maximum_fusion.refs_0_), channel_id=1, source_target_pairs={{0,9},{1,8},{2,11},{3,10},{4,13},{5,12},{6,15},{7,14},{8,1},{9,0},... | collective-permute-start | bytes 159752 | tf_op jit(solution)/shard_map/ppermute | solution.py:401
  9.1 4.1 %collective-permute-start.3 = (bf16[16,1664]{1,0:T(8,128)(2,1)S(1)}, bf16[16,1664]{1,0:T(8,128)(2,1)S(1)}, u32[]{:S(2)}, u32[]{:S(2)}) collective-permute-start(bf16[16,1664]{1,0:T(8,128)(2,1)S(1)} %pad_maximum_fusion.refs_0_), channel_id=1, source_target_pairs={{0,5},{1,4},{2,7},{3,6},{4,1},{5,0},{6,3},{7,2},{8,13},{9,12},{10,... | collective-permute-start | bytes 159752 | tf_op jit(solution)/shard_map/ppermute | solution.py:401
  11.6 3.6 %collective-permute-start.4 = (bf16[16,1664]{1,0:T(8,128)(2,1)S(1)}, bf16[16,1664]{1,0:T(8,128)(2,1)S(1)}, u32[]{:S(2)}, u32[]{:S(2)}) collective-permute-start(bf16[16,1664]{1,0:T(8,128)(2,1)S(1)} %collective-permute-done.2.refs_1_), channel_id=1, source_target_pairs={{0,5},{1,4},{2,7},{3,6},{4,1},{5,0},{6,3},{7,2},{8,13},{9,12},{10,... | collective-permute-start | bytes 159752 | tf_op jit(solution)/shard_map/ppermute | solution.py:401
  13.2 1.2 %collective-permute-start.7 = (bf16[16,1536]{1,0:T(8,128)(2,1)S(1)}, bf16[16,1536]{1,0:T(8,128)(2,1)S(1)}, u32[]{:S(2)}, u32[]{:S(2)}) collective-permute-start(bf16[16,1536]{1,0:T(8,128)(2,1)S(1)} %shard_map.65.refs_6_), channel_id=1, source_target_pairs={{0,1},{1,0},{2,3},{3,2},{4,5},{5,4},{6,7},{7,6},{8,9},{9,8},{10,11... | collective-permute-start | bytes 147464 | tf_op jit(solution)/shard_map/ppermute | solution.py:401
  14.5 1.4 %collective-permute-start.8 = (bf16[64,1536]{1,0:T(8,128)(2,1)S(1)}, bf16[64,1536]{1,0:T(8,128)(2,1)S(1)}, u32[]{:S(2)}, u32[]{:S(2)}) collective-permute-start(bf16[64,1536]{1,0:T(8,128)(2,1)S(1)} %bitcast.13), channel_id=1, source_target_pairs={{0,1},{1,0},{2,3},{3,2},{4,5},{5,4},{6,7},{7,6},{8,9},{9,8},{10,11... | collective-permute-start | bytes 589832 | tf_op jit(solution)/shard_map/ppermute | solution.py:401
  15.7 1.5 %collective-permute-start.10 = (bf16[64,1536]{1,0:T(8,128)(2,1)S(1)}, bf16[64,1536]{1,0:T(8,128)(2,1)S(1)}, u32[]{:S(2)}, u32[]{:S(2)}) collective-permute-start(bf16[64,1536]{1,0:T(8,128)(2,1)S(1)} %bitcast.11), channel_id=1, source_target_pairs={{0,1},{1,0},{2,3},{3,2},{4,5},{5,4},{6,7},{7,6},{8,9},{9,8},{10,11... | collective-permute-start | bytes 589832 | tf_op jit(solution)/shard_map/ppermute | solution.py:401
  17.2 12.7 %copy-start.2 = (bf16[16,4608]{1,0:T(8,128)(2,1)S(1)}, bf16[16,4608]{1,0:T(8,128)(2,1)}, u32[]{:S(2)}) copy-start(bf16[16,4608]{1,0:T(8,128)(2,1)} %value_ref.1) | copy-start | bytes 442372
  17.6 3.8 %collective-permute-start.12 = (bf16[16,1664]{1,0:T(8,128)(2,1)S(1)}, bf16[16,1664]{1,0:T(8,128)(2,1)S(1)}, u32[]{:S(2)}, u32[]{:S(2)}) collective-permute-start(bf16[16,1664]{1,0:T(8,128)(2,1)S(1)} %get-tuple-element.38), channel_id=1, source_target_pairs={{0,5},{1,4},{2,7},{3,6},{4,1},{5,0},{6,3},{7,2},{8,13},{9,12},{10,... | collective-permute-start | bytes 159752 | tf_op jit(solution)/shard_map/ppermute | solution.py:401
  19.2 5.2 %collective-permute-start.11 = (bf16[16,1664]{1,0:T(8,128)(2,1)S(1)}, bf16[16,1664]{1,0:T(8,128)(2,1)S(1)}, u32[]{:S(2)}, u32[]{:S(2)}) collective-permute-start(bf16[16,1664]{1,0:T(8,128)(2,1)S(1)} %get-tuple-element.36), channel_id=1, source_target_pairs={{0,5},{1,4},{2,7},{3,6},{4,1},{5,0},{6,3},{7,2},{8,13},{9,12},{10,... | collective-permute-start | bytes 159752 | tf_op jit(solution)/shard_map/ppermute | solution.py:401
  21.4 5.1 %collective-permute-start.13 = (bf16[16,1664]{1,0:T(8,128)(2,1)S(1)}, bf16[16,1664]{1,0:T(8,128)(2,1)S(1)}, u32[]{:S(2)}, u32[]{:S(2)}) collective-permute-start(bf16[16,1664]{1,0:T(8,128)(2,1)S(1)} %add.25), channel_id=1, source_target_pairs={{0,9},{1,8},{2,11},{3,10},{4,13},{5,12},{6,15},{7,14},{8,1},{9,0},... | collective-permute-start | bytes 159752 | tf_op jit(solution)/shard_map/ppermute | solution.py:401
  26.5 3.3 %collective-permute-start.14 = (bf16[8,1664]{1,0:T(8,128)(2,1)S(1)}, bf16[8,1664]{1,0:T(8,128)(2,1)S(1)}, u32[]{:S(2)}, u32[]{:S(2)}) collective-permute-start(bf16[8,1664]{1,0:T(8,128)(2,1)S(1)} %get-tuple-element.39), channel_id=1, source_target_pairs={{0,3},{1,2},{2,1},{3,0},{4,7},{5,6},{6,5},{7,4},{8,11},{9,10},{10,... | collective-permute-start | bytes 79880 | tf_op jit(solution)/shard_map/ppermute | solution.py:401

commit v10 on v9

--- a/solution.py
+++ b/solution.py
@@ -492,13 +492,12 @@
     )(weights, shares, near, far, pair_values, pair_far_values, cross_near, cross_far)
 
     parts = dict(zip(sorted(masks), parts))
-    for bits in hops[::-1]:
-        for mask in sorted(parts, reverse=True):
-            if mask ^ bits in parts and mask ^ bits < mask:
-                parts[mask ^ bits] = parts[mask ^ bits] + swap(parts.pop(mask), bits)
-    (mixed,) = parts.values()
-    keep = mixed[: rows // 2]
-    came = swap(mixed[rows // 2 :], PAIR)
+    far_hop, near_hop = hops
+    half = rows // 2
+    relayed = parts[far_hop] + swap(parts[far_hop ^ near_hop], near_hop)
+    mixed = parts[0] + swap(parts[near_hop], near_hop)
+    keep = mixed[:half] + swap(relayed[:half], far_hop)
+    came = swap(mixed[half:], PAIR) + swap(relayed[half:], far_hop ^ PAIR)
 
     return pl.pallas_call(
         functools.partial(finish_kernel, history),

time: 31.2 us -> 31.2 us (level)
  starting transfers between devices: 17.1 us -> 18.4 us
  waiting for transfers between devices: 8.23 us -> 7.2 us
    ppermute x15 -> x16, starting transfers between devices: 17.1 us -> 18.4 us  [swap(): return lax.ppermute(array, 'utt', [(i, i ^ bits) for i in range(devices)])]
    ppermute x15 -> x16, waiting for transfers between devices: 8.23 us -> 7.2 us  [swap(): return lax.ppermute(array, 'utt', [(i, i ^ bits) for i in range(devices)])]
  transfers between devices with their start and end apart: 15 -> 16, of which waited for: 8 -> 8; matrix products, arithmetic and copies ran while one was open for 0% -> 1% of each run, Pallas kernels for 6% -> 6%
where the time goes in v10:
time: 31.2 us; the launch traced here: 31.1 us
  starting transfers between devices  18.4 us (59%)
  waiting for transfers between devices  7.2 us (23%)
  Pallas kernels  4.52 us (14%)
  between operations  0.77 us (2%)
    ppermute x16, starting transfers between devices, swap(): return lax.ppermute(array, 'utt', [(i, i ^ bits) for i in range(devices)])  18.4 us
    ppermute x16, waiting for transfers between devices, swap(): return lax.ppermute(array, 'utt', [(i, i ^ bits) for i in range(devices)])  7.2 us
    pallas_call x1, Pallas kernels, body_by_parent(): pl.pallas_call(pack_kernel, out_shape=(half_rows, half_rows, half_cache,...  1.29 us
    pallas_call x1, Pallas kernels, body_by_parent(): pl.pallas_call(functools.partial(self_weights_kernel, tuple(masks), len(g...  1.26 us
    pallas_call x1, Pallas kernels, body_by_parent(): pl.pallas_call(functools.partial(finish_kernel, history), out_shape=jax.S...  0.93 us
  transfers between devices with their start and end apart: 16, of which 8 were waited for; matrix products, arithmetic and copies ran while one was open for 1% of the time, Pallas kernels for 6%

profile of v10, /device:TPU:0, one launch (start us, length us, event | category | flops | bytes accessed | tf_op | source)
XLA Modules:
  0.0 31.1 jit_solution(676599362936698778)
XLA Ops:
  0.0 1.3 %shard_map.64 = (bf16[8,1664]{1,0:T(8,128)(2,1)S(1)}, bf16[8,1664]{1,0:T(8,128)(2,1)S(1)}, bf16[4,16,1536]{2,1,0:T(8,128)(2,1)S(1)}, bf16[4,16,1536]{2,1,0:T(8,128)(2,1)S(1)}) custom-call(bf16[16,4608]{1,0:T(8,128)(2,1)} %value_ref.1, s32[1,16]{1,0:T(1,128)} %parents_hbm_ref.1, bf16[4,2,16,3072]{3,2,1,0:T(8,128)(2,1)} %bitcast.6), custom_call_target="tpu_custom_call" | custom-call | flops 1500000000 | bytes 1572864 | tf_op jit(solution)/shard_map/pallas_call | solution.py:414
  1.3 2.5 %collective-permute-start.1 = (bf16[8,1664]{1,0:T(8,128)(2,1)S(1)}, bf16[8,1664]{1,0:T(8,128)(2,1)S(1)}, u32[]{:S(2)}, u32[]{:S(2)}) collective-permute-start(bf16[8,1664]{1,0:T(8,128)(2,1)S(1)} %get-tuple-element.23), channel_id=1, source_target_pairs={{0,3},{1,2},{2,1},{3,0},{4,7},{5,6},{6,5},{7,4},{8,11},{9,10},{10,... | collective-permute-start | bytes 79880 | tf_op jit(solution)/shard_map/ppermute | solution.py:401
  3.8 0.7 %collective-permute-start = (s32[1,16]{1,0:T(1,128)S(1)}, s32[1,16]{1,0:T(1,128)S(1)}, u32[]{:S(2)}, u32[]{:S(2)}) collective-permute-start(s32[1,16]{1,0:T(1,128)S(1)} %copy-done.4), channel_id=1, source_target_pairs={{0,1},{1,0},{2,3},{3,2},{4,5},{5,4},{6,7},{7,6},{8,9},{9,8},{10,11... | collective-permute-start | bytes 200 | tf_op jit(solution)/shard_map/ppermute | solution.py:401
  4.6 1.6 %collective-permute-start.9 = (bf16[4,16,1536]{2,1,0:T(8,128)(2,1)S(1)}, bf16[4,16,1536]{2,1,0:T(8,128)(2,1)S(1)}, u32[]{:S(2)}, u32[]{:S(2)}) collective-permute-start(bf16[4,16,1536]{2,1,0:T(8,128)(2,1)S(1)} %get-tuple-element.33), channel_id=1, source_target_pairs={{0,3},{1,2},{2,1},{3,0},{4,7},{5,6},{6,5},{7,4},{8,11},{9,10},{10,... | collective-permute-start | bytes 589832 | tf_op jit(solution)/shard_map/ppermute | solution.py:401
  6.4 2.8 %collective-permute-start.2 = (bf16[16,1664]{1,0:T(8,128)(2,1)S(1)}, bf16[16,1664]{1,0:T(8,128)(2,1)S(1)}, u32[]{:S(2)}, u32[]{:S(2)}) collective-permute-start(bf16[16,1664]{1,0:T(8,128)(2,1)S(1)} %pad_maximum_fusion.refs_0_), channel_id=1, source_target_pairs={{0,9},{1,8},{2,11},{3,10},{4,13},{5,12},{6,15},{7,14},{8,1},{9,0},... | collective-permute-start | bytes 159752 | tf_op jit(solution)/shard_map/ppermute | solution.py:401
  9.1 1.2 %collective-permute-start.3 = (bf16[16,1664]{1,0:T(8,128)(2,1)S(1)}, bf16[16,1664]{1,0:T(8,128)(2,1)S(1)}, u32[]{:S(2)}, u32[]{:S(2)}) collective-permute-start(bf16[16,1664]{1,0:T(8,128)(2,1)S(1)} %pad_maximum_fusion.refs_0_), channel_id=1, source_target_pairs={{0,5},{1,4},{2,7},{3,6},{4,1},{5,0},{6,3},{7,2},{8,13},{9,12},{10,... | collective-permute-start | bytes 159752 | tf_op jit(solution)/shard_map/ppermute | solution.py:401
  11.0 0.6 %shard_map.65.refs_6_ = bf16[16,1536]{1,0:T(8,128)(2,1)S(1)} custom-call(s32[1,128]{1,0:T(1,128)S(1)} %broadcast_in_dim.8.lengths_ref, bf16[16,1536]{1,0:T(8,128)(2,1)S(1)} %copy-done.3, bf16[256,3072]{1,0:T(8,128)(2,1)S(1)} %bitcast.10), custom_call_target="tpu_custom_call" | custom-call | tf_op jit(solution)/shard_map/pallas_call | solution.py:445
  11.6 1.5 %collective-permute-start.4 = (bf16[16,1664]{1,0:T(8,128)(2,1)S(1)}, bf16[16,1664]{1,0:T(8,128)(2,1)S(1)}, u32[]{:S(2)}, u32[]{:S(2)}) collective-permute-start(bf16[16,1664]{1,0:T(8,128)(2,1)S(1)} %collective-permute-done.2.refs_1_), channel_id=1, source_target_pairs={{0,5},{1,4},{2,7},{3,6},{4,1},{5,0},{6,3},{7,2},{8,13},{9,12},{10,... | collective-permute-start | bytes 159752 | tf_op jit(solution)/shard_map/ppermute | solution.py:401
  13.2 0.2 collective-permute-start.7
  13.5 1.0 %collective-permute-done.7.refs_7_ = bf16[16,1536]{1,0:T(8,128)(2,1)S(1)} collective-permute-done((bf16[16,1536]{1,0:T(8,128)(2,1)S(1)}, bf16[16,1536]{1,0:T(8,128)(2,1)S(1)}, u32[]{:S(2)}, u32[]{:S(2)}) %collective-permute-start.7) | collective-permute-done | bytes 49184 | tf_op jit(solution)/shard_map/ppermute | solution.py:401
  14.5 0.2 collective-permute-start.8
  14.7 0.5 %collective-permute-done.4.refs_3_ = bf16[16,1664]{1,0:T(8,128)(2,1)S(1)} collective-permute-done((bf16[16,1664]{1,0:T(8,128)(2,1)S(1)}, bf16[16,1664]{1,0:T(8,128)(2,1)S(1)}, u32[]{:S(2)}, u32[]{:S(2)}) %collective-permute-start.4) | collective-permute-done | bytes 53280 | tf_op jit(solution)/shard_map/ppermute | solution.py:401
  15.2 0.5 %collective-permute-done.9 = bf16[4,16,1536]{2,1,0:T(8,128)(2,1)S(1)} collective-permute-done((bf16[4,16,1536]{2,1,0:T(8,128)(2,1)S(1)}, bf16[4,16,1536]{2,1,0:T(8,128)(2,1)S(1)}, u32[]{:S(2)}, u32[]{:S(2)}) %collective-permute-start.9) | collective-permute-done | bytes 196640 | tf_op jit(solution)/shard_map/ppermute | solution.py:401
  15.9 1.3 %shard_map.66 = (bf16[12,64,256]{2,1,0:T(8,128)(2,1)S(1)}, bf16[64,128]{1,0:T(8,128)(2,1)S(1)}) custom-call(bf16[16,1664]{1,0:T(8,128)(2,1)S(1)} %pad_maximum_fusion.refs_0_, bf16[16,1664]{1,0:T(8,128)(2,1)S(1)} %collective-permute-done.2.refs_1_, bf16[16,1664]{1,0:T(8,128)(2,1)S(1)} %collective-permute-done.3.refs_2_, ...), custom_call_target="tpu_custom_call" | custom-call | tf_op jit(solution)/shard_map/pallas_call | solution.py:473
  17.2 0.4 %shard_map.67 = (bf16[16,1664]{1,0:T(8,128)(2,1)S(1)}, bf16[16,1664]{1,0:T(8,128)(2,1)S(1)}, bf16[16,1664]{1,0:T(8,128)(2,1)S(1)}, bf16[16,1664]{1,0:T(8,128)(2,1)S(1)}) custom-call(bf16[12,64,256]{2,1,0:T(8,128)(2,1)S(1)} %get-tuple-element.31.refs_0_, bf16[64,128]{1,0:T(8,128)(2,1)S(1)} %get-tuple-element.32.refs_1_, bf16[4,2,16,3072]{3,2,1,0:T(8,128)(2,1)S(1)} %bitcast.9, ...), custom_call_target="tpu_custom_call" | custom-call | tf_op jit(solution)/shard_map/pallas_call | solution.py:483
  17.6 1.6 %collective-permute-start.12 = (bf16[16,1664]{1,0:T(8,128)(2,1)S(1)}, bf16[16,1664]{1,0:T(8,128)(2,1)S(1)}, u32[]{:S(2)}, u32[]{:S(2)}) collective-permute-start(bf16[16,1664]{1,0:T(8,128)(2,1)S(1)} %get-tuple-element.38), channel_id=1, source_target_pairs={{0,5},{1,4},{2,7},{3,6},{4,1},{5,0},{6,3},{7,2},{8,13},{9,12},{10,... | collective-permute-start | bytes 159752 | tf_op jit(solution)/shard_map/ppermute | solution.py:401
  19.2 0.2 collective-permute-start.11
  19.4 2.0 %collective-permute-done.12 = bf16[16,1664]{1,0:T(8,128)(2,1)S(1)} collective-permute-done((bf16[16,1664]{1,0:T(8,128)(2,1)S(1)}, bf16[16,1664]{1,0:T(8,128)(2,1)S(1)}, u32[]{:S(2)}, u32[]{:S(2)}) %collective-permute-start.12) | collective-permute-done | bytes 53280 | tf_op jit(solution)/shard_map/ppermute | solution.py:401
  21.4 3.0 %collective-permute-start.13 = (bf16[8,1664]{1,0:T(8,128)(2,1)S(1)}, bf16[8,1664]{1,0:T(8,128)(2,1)S(1)}, u32[]{:S(2)}, u32[]{:S(2)}) collective-permute-start(bf16[8,1664]{1,0:T(8,128)(2,1)S(1)} %get-tuple-element.40), channel_id=1, source_target_pairs={{0,9},{1,8},{2,11},{3,10},{4,13},{5,12},{6,15},{7,14},{8,1},{9,0},... | collective-permute-start | bytes 79880 | tf_op jit(solution)/shard_map/ppermute | solution.py:401
  24.4 1.2 %collective-permute-start.15 = (bf16[8,1664]{1,0:T(8,128)(2,1)S(1)}, bf16[8,1664]{1,0:T(8,128)(2,1)S(1)}, u32[]{:S(2)}, u32[]{:S(2)}) collective-permute-start(bf16[8,1664]{1,0:T(8,128)(2,1)S(1)} %get-tuple-element.39), channel_id=1, source_target_pairs={{0,10},{1,11},{2,8},{3,9},{4,14},{5,15},{6,12},{7,13},{8,2},{9,3},... | collective-permute-start | bytes 79880 | tf_op jit(solution)/shard_map/ppermute | solution.py:401
  25.7 0.3 %collective-permute-done.13 = bf16[8,1664]{1,0:T(8,128)(2,1)S(1)} collective-permute-done((bf16[8,1664]{1,0:T(8,128)(2,1)S(1)}, bf16[8,1664]{1,0:T(8,128)(2,1)S(1)}, u32[]{:S(2)}, u32[]{:S(2)}) %collective-permute-start.13) | collective-permute-done | bytes 26656 | tf_op jit(solution)/shard_map/ppermute | solution.py:401
  26.0 1.5 %collective-permute-start.14 = (bf16[8,1664]{1,0:T(8,128)(2,1)S(1)}, bf16[8,1664]{1,0:T(8,128)(2,1)S(1)}, u32[]{:S(2)}, u32[]{:S(2)}) collective-permute-start(bf16[8,1664]{1,0:T(8,128)(2,1)S(1)} %get-tuple-element.41), channel_id=1, source_target_pairs={{0,3},{1,2},{2,1},{3,0},{4,7},{5,6},{6,5},{7,4},{8,11},{9,10},{10,... | collective-permute-start | bytes 79880 | tf_op jit(solution)/shard_map/ppermute | solution.py:401
  27.4 2.7 %collective-permute-done.15 = bf16[8,1664]{1,0:T(8,128)(2,1)S(1)} collective-permute-done((bf16[8,1664]{1,0:T(8,128)(2,1)S(1)}, bf16[8,1664]{1,0:T(8,128)(2,1)S(1)}, u32[]{:S(2)}, u32[]{:S(2)}) %collective-permute-start.15) | collective-permute-done | bytes 26656 | tf_op jit(solution)/shard_map/ppermute | solution.py:401
  30.1 0.9 %shard_map.68 = bf16[16,1536]{1,0:T(8,128)(2,1)} custom-call(bf16[8,1664]{1,0:T(8,128)(2,1)S(1)} %get-tuple-element.42.mine_ref, bf16[8,1664]{1,0:T(8,128)(2,1)S(1)} %add.30.came_ref, bf16[16,4608]{1,0:T(8,128)(2,1)S(1)} %copy-done.2), custom_call_target="tpu_custom_call" | custom-call | tf_op jit(solution)/shard_map/pallas_call | solution.py:502
  (33 shorter events, 0.7 us)
Async XLA Ops:
  0.0 3.8 %copy-start.4 = (s32[1,16]{1,0:T(1,128)S(1)}, s32[1,16]{1,0:T(1,128)}, u32[]{:S(2)}) copy-start(s32[1,16]{1,0:T(1,128)} %parents_hbm_ref.1) | copy-start | bytes 196
  0.0 4.6 %copy-start = (bf16[16,8,3072]{2,1,0:T(8,128)(2,1)S(1)}, bf16[16,8,3072]{2,1,0:T(8,128)(2,1)}, u32[]{:S(2)}) copy-start(bf16[16,8,3072]{2,1,0:T(8,128)(2,1)} %param.6) | copy-start | bytes 2359300
  0.0 11.0 %copy-start.1 = (bf16[1,256,3072]{2,1,0:T(8,128)(2,1)S(1)}, bf16[1,256,3072]{2,1,0:T(8,128)(2,1)}, u32[]{:S(2)}) copy-start(bf16[1,256,3072]{2,1,0:T(8,128)(2,1)} %param.9) | copy-start | bytes 4718596
  0.0 11.0 %copy-start.3 = (bf16[16,1536]{1,0:T(8,128)(2,1)S(1)}, bf16[16,1536]{1,0:T(8,128)(2,1)}, u32[]{:S(2)}) copy-start(bf16[16,1536]{1,0:T(8,128)(2,1)} %query_ref) | copy-start | bytes 147460
  1.3 5.0 %collective-permute-start.1 = (bf16[8,1664]{1,0:T(8,128)(2,1)S(1)}, bf16[8,1664]{1,0:T(8,128)(2,1)S(1)}, u32[]{:S(2)}, u32[]{:S(2)}) collective-permute-start(bf16[8,1664]{1,0:T(8,128)(2,1)S(1)} %get-tuple-element.23), channel_id=1, source_target_pairs={{0,3},{1,2},{2,1},{3,0},{4,7},{5,6},{6,5},{7,4},{8,11},{9,10},{10,... | collective-permute-start | bytes 79880 | tf_op jit(solution)/shard_map/ppermute | solution.py:401
  3.8 2.4 %collective-permute-start = (s32[1,16]{1,0:T(1,128)S(1)}, s32[1,16]{1,0:T(1,128)S(1)}, u32[]{:S(2)}, u32[]{:S(2)}) collective-permute-start(s32[1,16]{1,0:T(1,128)S(1)} %copy-done.4), channel_id=1, source_target_pairs={{0,1},{1,0},{2,3},{3,2},{4,5},{5,4},{6,7},{7,6},{8,9},{9,8},{10,11... | collective-permute-start | bytes 200 | tf_op jit(solution)/shard_map/ppermute | solution.py:401
  4.5 10.0 %collective-permute-start.6 = (bf16[4,16,1536]{2,1,0:T(8,128)(2,1)S(1)}, bf16[4,16,1536]{2,1,0:T(8,128)(2,1)S(1)}, u32[]{:S(2)}, u32[]{:S(2)}) collective-permute-start(bf16[4,16,1536]{2,1,0:T(8,128)(2,1)S(1)} %get-tuple-element.28), channel_id=1, source_target_pairs={{0,3},{1,2},{2,1},{3,0},{4,7},{5,6},{6,5},{7,4},{8,11},{9,10},{10,... | collective-permute-start | bytes 589832 | tf_op jit(solution)/shard_map/ppermute | solution.py:401
  4.6 11.3 %collective-permute-start.5 = (bf16[4,2,16,3072]{3,2,1,0:T(8,128)(2,1)S(1)}, bf16[4,2,16,3072]{3,2,1,0:T(8,128)(2,1)S(1)}, u32[]{:S(2)}, u32[]{:S(2)}) collective-permute-start(bf16[4,2,16,3072]{3,2,1,0:T(8,128)(2,1)S(1)} %bitcast.7), channel_id=1, source_target_pairs={{0,1},{1,0},{2,3},{3,2},{4,5},{5,4},{6,7},{7,6},{8,9},{9,8},{10,11... | collective-permute-start | bytes 2359304 | tf_op jit(solution)/shard_map/ppermute | solution.py:401
  4.6 11.1 %collective-permute-start.9 = (bf16[4,16,1536]{2,1,0:T(8,128)(2,1)S(1)}, bf16[4,16,1536]{2,1,0:T(8,128)(2,1)S(1)}, u32[]{:S(2)}, u32[]{:S(2)}) collective-permute-start(bf16[4,16,1536]{2,1,0:T(8,128)(2,1)S(1)} %get-tuple-element.33), channel_id=1, source_target_pairs={{0,3},{1,2},{2,1},{3,0},{4,7},{5,6},{6,5},{7,4},{8,11},{9,10},{10,... | collective-permute-start | bytes 589832 | tf_op jit(solution)/shard_map/ppermute | solution.py:401
  6.4 5.2 %collective-permute-start.2 = (bf16[16,1664]{1,0:T(8,128)(2,1)S(1)}, bf16[16,1664]{1,0:T(8,128)(2,1)S(1)}, u32[]{:S(2)}, u32[]{:S(2)}) collective-permute-start(bf16[16,1664]{1,0:T(8,128)(2,1)S(1)} %pad_maximum_fusion.refs_0_), channel_id=1, source_target_pairs={{0,9},{1,8},{2,11},{3,10},{4,13},{5,12},{6,15},{7,14},{8,1},{9,0},... | collective-permute-start | bytes 159752 | tf_op jit(solution)/shard_map/ppermute | solution.py:401
  9.1 4.1 %collective-permute-start.3 = (bf16[16,1664]{1,0:T(8,128)(2,1)S(1)}, bf16[16,1664]{1,0:T(8,128)(2,1)S(1)}, u32[]{:S(2)}, u32[]{:S(2)}) collective-permute-start(bf16[16,1664]{1,0:T(8,128)(2,1)S(1)} %pad_maximum_fusion.refs_0_), channel_id=1, source_target_pairs={{0,5},{1,4},{2,7},{3,6},{4,1},{5,0},{6,3},{7,2},{8,13},{9,12},{10,... | collective-permute-start | bytes 159752 | tf_op jit(solution)/shard_map/ppermute | solution.py:401
  11.6 3.6 %collective-permute-start.4 = (bf16[16,1664]{1,0:T(8,128)(2,1)S(1)}, bf16[16,1664]{1,0:T(8,128)(2,1)S(1)}, u32[]{:S(2)}, u32[]{:S(2)}) collective-permute-start(bf16[16,1664]{1,0:T(8,128)(2,1)S(1)} %collective-permute-done.2.refs_1_), channel_id=1, source_target_pairs={{0,5},{1,4},{2,7},{3,6},{4,1},{5,0},{6,3},{7,2},{8,13},{9,12},{10,... | collective-permute-start | bytes 159752 | tf_op jit(solution)/shard_map/ppermute | solution.py:401
  13.2 1.2 %collective-permute-start.7 = (bf16[16,1536]{1,0:T(8,128)(2,1)S(1)}, bf16[16,1536]{1,0:T(8,128)(2,1)S(1)}, u32[]{:S(2)}, u32[]{:S(2)}) collective-permute-start(bf16[16,1536]{1,0:T(8,128)(2,1)S(1)} %shard_map.65.refs_6_), channel_id=1, source_target_pairs={{0,1},{1,0},{2,3},{3,2},{4,5},{5,4},{6,7},{7,6},{8,9},{9,8},{10,11... | collective-permute-start | bytes 147464 | tf_op jit(solution)/shard_map/ppermute | solution.py:401
  14.5 1.4 %collective-permute-start.8 = (bf16[64,1536]{1,0:T(8,128)(2,1)S(1)}, bf16[64,1536]{1,0:T(8,128)(2,1)S(1)}, u32[]{:S(2)}, u32[]{:S(2)}) collective-permute-start(bf16[64,1536]{1,0:T(8,128)(2,1)S(1)} %bitcast.13), channel_id=1, source_target_pairs={{0,1},{1,0},{2,3},{3,2},{4,5},{5,4},{6,7},{7,6},{8,9},{9,8},{10,11... | collective-permute-start | bytes 589832 | tf_op jit(solution)/shard_map/ppermute | solution.py:401
  15.7 1.5 %collective-permute-start.10 = (bf16[64,1536]{1,0:T(8,128)(2,1)S(1)}, bf16[64,1536]{1,0:T(8,128)(2,1)S(1)}, u32[]{:S(2)}, u32[]{:S(2)}) collective-permute-start(bf16[64,1536]{1,0:T(8,128)(2,1)S(1)} %bitcast.11), channel_id=1, source_target_pairs={{0,1},{1,0},{2,3},{3,2},{4,5},{5,4},{6,7},{7,6},{8,9},{9,8},{10,11... | collective-permute-start | bytes 589832 | tf_op jit(solution)/shard_map/ppermute | solution.py:401
  17.2 13.0 %copy-start.2 = (bf16[16,4608]{1,0:T(8,128)(2,1)S(1)}, bf16[16,4608]{1,0:T(8,128)(2,1)}, u32[]{:S(2)}) copy-start(bf16[16,4608]{1,0:T(8,128)(2,1)} %value_ref.1) | copy-start | bytes 442372
  17.6 3.8 %collective-permute-start.12 = (bf16[16,1664]{1,0:T(8,128)(2,1)S(1)}, bf16[16,1664]{1,0:T(8,128)(2,1)S(1)}, u32[]{:S(2)}, u32[]{:S(2)}) collective-permute-start(bf16[16,1664]{1,0:T(8,128)(2,1)S(1)} %get-tuple-element.38), channel_id=1, source_target_pairs={{0,5},{1,4},{2,7},{3,6},{4,1},{5,0},{6,3},{7,2},{8,13},{9,12},{10,... | collective-permute-start | bytes 159752 | tf_op jit(solution)/shard_map/ppermute | solution.py:401
  19.2 6.4 %collective-permute-start.11 = (bf16[16,1664]{1,0:T(8,128)(2,1)S(1)}, bf16[16,1664]{1,0:T(8,128)(2,1)S(1)}, u32[]{:S(2)}, u32[]{:S(2)}) collective-permute-start(bf16[16,1664]{1,0:T(8,128)(2,1)S(1)} %get-tuple-element.36), channel_id=1, source_target_pairs={{0,5},{1,4},{2,7},{3,6},{4,1},{5,0},{6,3},{7,2},{8,13},{9,12},{10,... | collective-permute-start | bytes 159752 | tf_op jit(solution)/shard_map/ppermute | solution.py:401
  21.4 4.5 %collective-permute-start.13 = (bf16[8,1664]{1,0:T(8,128)(2,1)S(1)}, bf16[8,1664]{1,0:T(8,128)(2,1)S(1)}, u32[]{:S(2)}, u32[]{:S(2)}) collective-permute-start(bf16[8,1664]{1,0:T(8,128)(2,1)S(1)} %get-tuple-element.40), channel_id=1, source_target_pairs={{0,9},{1,8},{2,11},{3,10},{4,13},{5,12},{6,15},{7,14},{8,1},{9,0},... | collective-permute-start | bytes 79880 | tf_op jit(solution)/shard_map/ppermute | solution.py:401
  24.4 5.7 %collective-permute-start.15 = (bf16[8,1664]{1,0:T(8,128)(2,1)S(1)}, bf16[8,1664]{1,0:T(8,128)(2,1)S(1)}, u32[]{:S(2)}, u32[]{:S(2)}) collective-permute-start(bf16[8,1664]{1,0:T(8,128)(2,1)S(1)} %get-tuple-element.39), channel_id=1, source_target_pairs={{0,10},{1,11},{2,8},{3,9},{4,14},{5,15},{6,12},{7,13},{8,2},{9,3},... | collective-permute-start | bytes 79880 | tf_op jit(solution)/shard_map/ppermute | solution.py:401
  26.0 4.1 %collective-permute-start.14 = (bf16[8,1664]{1,0:T(8,128)(2,1)S(1)}, bf16[8,1664]{1,0:T(8,128)(2,1)S(1)}, u32[]{:S(2)}, u32[]{:S(2)}) collective-permute-start(bf16[8,1664]{1,0:T(8,128)(2,1)S(1)} %get-tuple-element.41), channel_id=1, source_target_pairs={{0,3},{1,2},{2,1},{3,0},{4,7},{5,6},{6,5},{7,4},{8,11},{9,10},{10,... | collective-permute-start | bytes 79880 | tf_op jit(solution)/shard_map/ppermute | solution.py:401

commit v11 on v10

--- a/solution.py
+++ b/solution.py
@@ -495,9 +495,13 @@
     far_hop, near_hop = hops
     half = rows // 2
     relayed = parts[far_hop] + swap(parts[far_hop ^ near_hop], near_hop)
-    mixed = parts[0] + swap(parts[near_hop], near_hop)
-    keep = mixed[:half] + swap(relayed[:half], far_hop)
-    came = swap(mixed[half:], PAIR) + swap(relayed[half:], far_hop ^ PAIR)
+    near_rows = swap(parts[near_hop][:half], near_hop)
+    came = swap(parts[0][half:], PAIR)
+    relayed = after(relayed, came, near_rows)
+    keep = parts[0][:half] + near_rows
+    came = came + swap(parts[near_hop][half:], near_hop ^ PAIR)
+    keep = keep + swap(relayed[:half], far_hop)
+    came = came + swap(relayed[half:], far_hop ^ PAIR)
 
     return pl.pallas_call(
         functools.partial(finish_kernel, history),

time: 31.2 us -> 35.3 us (1.13)
  waiting for transfers between devices: 7.2 us -> 10 us
  starting transfers between devices: 18.4 us -> 19.6 us
    ppermute x16 -> x17, waiting for transfers between devices: 7.2 us -> 10 us  [swap(): return lax.ppermute(array, 'utt', [(i, i ^ bits) for i in range(devices)])]
    ppermute x16 -> x17, starting transfers between devices: 18.4 us -> 19.6 us  [swap(): return lax.ppermute(array, 'utt', [(i, i ^ bits) for i in range(devices)])]
  transfers between devices with their start and end apart: 16 -> 17, of which waited for: 8 -> 10; matrix products, arithmetic and copies ran while one was open for 1% -> 0% of each run, Pallas kernels for 6% -> 5%
where the time goes in v11:
time: 35.3 us; the launch traced here: 35.1 us
  starting transfers between devices  19.6 us (56%)
  waiting for transfers between devices  10 us (28%)
  Pallas kernels  4.52 us (13%)
  between operations  0.76 us (2%)
    ppermute x17, starting transfers between devices, swap(): return lax.ppermute(array, 'utt', [(i, i ^ bits) for i in range(devices)])  19.6 us
    ppermute x17, waiting for transfers between devices, swap(): return lax.ppermute(array, 'utt', [(i, i ^ bits) for i in range(devices)])  10 us
    pallas_call x1, Pallas kernels, body_by_parent(): pl.pallas_call(pack_kernel, out_shape=(half_rows, half_rows, half_cache,...  1.29 us
    pallas_call x1, Pallas kernels, body_by_parent(): pl.pallas_call(functools.partial(self_weights_kernel, tuple(masks), len(g...  1.26 us
    pallas_call x1, Pallas kernels, body_by_parent(): pl.pallas_call(functools.partial(finish_kernel, history), out_shape=jax.S...  0.93 us
  transfers between devices with their start and end apart: 17, of which 10 were waited for; matrix products, arithmetic and copies ran while one was open for 0% of the time, Pallas kernels for 5%

profile of v11, /device:TPU:0, one launch (start us, length us, event | category | flops | bytes accessed | tf_op | source)
XLA Modules:
  0.0 35.1 jit_solution(9126463555143615177)
XLA Ops:
  0.0 1.3 %shard_map.64 = (bf16[8,1664]{1,0:T(8,128)(2,1)S(1)}, bf16[8,1664]{1,0:T(8,128)(2,1)S(1)}, bf16[4,16,1536]{2,1,0:T(8,128)(2,1)S(1)}, bf16[4,16,1536]{2,1,0:T(8,128)(2,1)S(1)}) custom-call(bf16[16,4608]{1,0:T(8,128)(2,1)} %value_ref.1, s32[1,16]{1,0:T(1,128)} %parents_hbm_ref.1, bf16[4,2,16,3072]{3,2,1,0:T(8,128)(2,1)} %bitcast.6), custom_call_target="tpu_custom_call" | custom-call | flops 1500000000 | bytes 1572864 | tf_op jit(solution)/shard_map/pallas_call | solution.py:414
  1.3 2.5 %collective-permute-start.1 = (bf16[8,1664]{1,0:T(8,128)(2,1)S(1)}, bf16[8,1664]{1,0:T(8,128)(2,1)S(1)}, u32[]{:S(2)}, u32[]{:S(2)}) collective-permute-start(bf16[8,1664]{1,0:T(8,128)(2,1)S(1)} %get-tuple-element.24), channel_id=1, source_target_pairs={{0,3},{1,2},{2,1},{3,0},{4,7},{5,6},{6,5},{7,4},{8,11},{9,10},{10,... | collective-permute-start | bytes 79880 | tf_op jit(solution)/shard_map/ppermute | solution.py:401
  3.8 0.7 %collective-permute-start = (s32[1,16]{1,0:T(1,128)S(1)}, s32[1,16]{1,0:T(1,128)S(1)}, u32[]{:S(2)}, u32[]{:S(2)}) collective-permute-start(s32[1,16]{1,0:T(1,128)S(1)} %copy-done.4), channel_id=1, source_target_pairs={{0,1},{1,0},{2,3},{3,2},{4,5},{5,4},{6,7},{7,6},{8,9},{9,8},{10,11... | collective-permute-start | bytes 200 | tf_op jit(solution)/shard_map/ppermute | solution.py:401
  4.6 1.6 %collective-permute-start.9 = (bf16[4,16,1536]{2,1,0:T(8,128)(2,1)S(1)}, bf16[4,16,1536]{2,1,0:T(8,128)(2,1)S(1)}, u32[]{:S(2)}, u32[]{:S(2)}) collective-permute-start(bf16[4,16,1536]{2,1,0:T(8,128)(2,1)S(1)} %get-tuple-element.34), channel_id=1, source_target_pairs={{0,3},{1,2},{2,1},{3,0},{4,7},{5,6},{6,5},{7,4},{8,11},{9,10},{10,... | collective-permute-start | bytes 589832 | tf_op jit(solution)/shard_map/ppermute | solution.py:401
  6.4 2.8 %collective-permute-start.2 = (bf16[16,1664]{1,0:T(8,128)(2,1)S(1)}, bf16[16,1664]{1,0:T(8,128)(2,1)S(1)}, u32[]{:S(2)}, u32[]{:S(2)}) collective-permute-start(bf16[16,1664]{1,0:T(8,128)(2,1)S(1)} %pad_maximum_fusion.refs_0_), channel_id=1, source_target_pairs={{0,9},{1,8},{2,11},{3,10},{4,13},{5,12},{6,15},{7,14},{8,1},{9,0},... | collective-permute-start | bytes 159752 | tf_op jit(solution)/shard_map/ppermute | solution.py:401
  9.1 1.2 %collective-permute-start.3 = (bf16[16,1664]{1,0:T(8,128)(2,1)S(1)}, bf16[16,1664]{1,0:T(8,128)(2,1)S(1)}, u32[]{:S(2)}, u32[]{:S(2)}) collective-permute-start(bf16[16,1664]{1,0:T(8,128)(2,1)S(1)} %pad_maximum_fusion.refs_0_), channel_id=1, source_target_pairs={{0,5},{1,4},{2,7},{3,6},{4,1},{5,0},{6,3},{7,2},{8,13},{9,12},{10,... | collective-permute-start | bytes 159752 | tf_op jit(solution)/shard_map/ppermute | solution.py:401
  11.0 0.6 %shard_map.65.refs_6_ = bf16[16,1536]{1,0:T(8,128)(2,1)S(1)} custom-call(s32[1,128]{1,0:T(1,128)S(1)} %broadcast_in_dim.8.lengths_ref, bf16[16,1536]{1,0:T(8,128)(2,1)S(1)} %copy-done.3, bf16[256,3072]{1,0:T(8,128)(2,1)S(1)} %bitcast.10), custom_call_target="tpu_custom_call" | custom-call | tf_op jit(solution)/shard_map/pallas_call | solution.py:445
  11.6 1.5 %collective-permute-start.4 = (bf16[16,1664]{1,0:T(8,128)(2,1)S(1)}, bf16[16,1664]{1,0:T(8,128)(2,1)S(1)}, u32[]{:S(2)}, u32[]{:S(2)}) collective-permute-start(bf16[16,1664]{1,0:T(8,128)(2,1)S(1)} %collective-permute-done.2.refs_1_), channel_id=1, source_target_pairs={{0,5},{1,4},{2,7},{3,6},{4,1},{5,0},{6,3},{7,2},{8,13},{9,12},{10,... | collective-permute-start | bytes 159752 | tf_op jit(solution)/shard_map/ppermute | solution.py:401
  13.5 1.0 %collective-permute-done.7.refs_7_ = bf16[16,1536]{1,0:T(8,128)(2,1)S(1)} collective-permute-done((bf16[16,1536]{1,0:T(8,128)(2,1)S(1)}, bf16[16,1536]{1,0:T(8,128)(2,1)S(1)}, u32[]{:S(2)}, u32[]{:S(2)}) %collective-permute-start.7) | collective-permute-done | bytes 49184 | tf_op jit(solution)/shard_map/ppermute | solution.py:401
  14.7 0.5 %collective-permute-done.4.refs_3_ = bf16[16,1664]{1,0:T(8,128)(2,1)S(1)} collective-permute-done((bf16[16,1664]{1,0:T(8,128)(2,1)S(1)}, bf16[16,1664]{1,0:T(8,128)(2,1)S(1)}, u32[]{:S(2)}, u32[]{:S(2)}) %collective-permute-start.4) | collective-permute-done | bytes 53280 | tf_op jit(solution)/shard_map/ppermute | solution.py:401
  15.2 0.5 %collective-permute-done.9 = bf16[4,16,1536]{2,1,0:T(8,128)(2,1)S(1)} collective-permute-done((bf16[4,16,1536]{2,1,0:T(8,128)(2,1)S(1)}, bf16[4,16,1536]{2,1,0:T(8,128)(2,1)S(1)}, u32[]{:S(2)}, u32[]{:S(2)}) %collective-permute-start.9) | collective-permute-done | bytes 196640 | tf_op jit(solution)/shard_map/ppermute | solution.py:401
  15.9 1.3 %shard_map.66 = (bf16[12,64,256]{2,1,0:T(8,128)(2,1)S(1)}, bf16[64,128]{1,0:T(8,128)(2,1)S(1)}) custom-call(bf16[16,1664]{1,0:T(8,128)(2,1)S(1)} %pad_maximum_fusion.refs_0_, bf16[16,1664]{1,0:T(8,128)(2,1)S(1)} %collective-permute-done.2.refs_1_, bf16[16,1664]{1,0:T(8,128)(2,1)S(1)} %collective-permute-done.3.refs_2_, ...), custom_call_target="tpu_custom_call" | custom-call | tf_op jit(solution)/shard_map/pallas_call | solution.py:473
  17.2 0.4 %shard_map.67 = (bf16[16,1664]{1,0:T(8,128)(2,1)S(1)}, bf16[16,1664]{1,0:T(8,128)(2,1)S(1)}, bf16[16,1664]{1,0:T(8,128)(2,1)S(1)}, bf16[16,1664]{1,0:T(8,128)(2,1)S(1)}) custom-call(bf16[12,64,256]{2,1,0:T(8,128)(2,1)S(1)} %get-tuple-element.32.refs_0_, bf16[64,128]{1,0:T(8,128)(2,1)S(1)} %get-tuple-element.33.refs_1_, bf16[4,2,16,3072]{3,2,1,0:T(8,128)(2,1)S(1)} %bitcast.9, ...), custom_call_target="tpu_custom_call" | custom-call | tf_op jit(solution)/shard_map/pallas_call | solution.py:483
  17.6 1.6 %collective-permute-start.12 = (bf16[16,1664]{1,0:T(8,128)(2,1)S(1)}, bf16[16,1664]{1,0:T(8,128)(2,1)S(1)}, u32[]{:S(2)}, u32[]{:S(2)}) collective-permute-start(bf16[16,1664]{1,0:T(8,128)(2,1)S(1)} %get-tuple-element.39), channel_id=1, source_target_pairs={{0,5},{1,4},{2,7},{3,6},{4,1},{5,0},{6,3},{7,2},{8,13},{9,12},{10,... | collective-permute-start | bytes 159752 | tf_op jit(solution)/shard_map/ppermute | solution.py:401
  19.2 0.2 collective-permute-start.11
  19.5 1.3 %collective-permute-start.13 = (bf16[8,1664]{1,0:T(8,128)(2,1)S(1)}, bf16[8,1664]{1,0:T(8,128)(2,1)S(1)}, u32[]{:S(2)}, u32[]{:S(2)}) collective-permute-start(bf16[8,1664]{1,0:T(8,128)(2,1)S(1)} %slice.20), channel_id=1, source_target_pairs={{0,3},{1,2},{2,1},{3,0},{4,7},{5,6},{6,5},{7,4},{8,11},{9,10},{10,... | collective-permute-start | bytes 79880 | tf_op jit(solution)/shard_map/ppermute | solution.py:401
  20.7 0.7 %collective-permute-done.12 = bf16[16,1664]{1,0:T(8,128)(2,1)S(1)} collective-permute-done((bf16[16,1664]{1,0:T(8,128)(2,1)S(1)}, bf16[16,1664]{1,0:T(8,128)(2,1)S(1)}, u32[]{:S(2)}, u32[]{:S(2)}) %collective-permute-start.12) | collective-permute-done | bytes 53280 | tf_op jit(solution)/shard_map/ppermute | solution.py:401
  21.4 1.1 %collective-permute-done.11 = bf16[8,1664]{1,0:T(8,128)(2,1)S(1)} collective-permute-done((bf16[8,1664]{1,0:T(8,128)(2,1)S(1)}, bf16[8,1664]{1,0:T(8,128)(2,1)S(1)}, u32[]{:S(2)}, u32[]{:S(2)}) %collective-permute-start.11) | collective-permute-done | bytes 26656 | tf_op jit(solution)/shard_map/ppermute | solution.py:401
  22.5 0.2 collective-permute-done.13
  22.7 3.0 %collective-permute-start.14 = (bf16[8,1664]{1,0:T(8,128)(2,1)S(1)}, bf16[8,1664]{1,0:T(8,128)(2,1)S(1)}, u32[]{:S(2)}, u32[]{:S(2)}) collective-permute-start(bf16[8,1664]{1,0:T(8,128)(2,1)S(1)} %get-tuple-element.44), channel_id=1, source_target_pairs={{0,9},{1,8},{2,11},{3,10},{4,13},{5,12},{6,15},{7,14},{8,1},{9,0},... | collective-permute-start | bytes 79880 | tf_op jit(solution)/shard_map/ppermute | solution.py:401
  25.8 2.6 %collective-permute-start.15 = (bf16[8,1664]{1,0:T(8,128)(2,1)S(1)}, bf16[8,1664]{1,0:T(8,128)(2,1)S(1)}, u32[]{:S(2)}, u32[]{:S(2)}) collective-permute-start(bf16[8,1664]{1,0:T(8,128)(2,1)S(1)} %get-tuple-element.41), channel_id=1, source_target_pairs={{0,6},{1,7},{2,4},{3,5},{4,2},{5,3},{6,0},{7,1},{8,14},{9,15},{10,... | collective-permute-start | bytes 79880 | tf_op jit(solution)/shard_map/ppermute | solution.py:401
  28.4 2.2 %collective-permute-done.15 = bf16[8,1664]{1,0:T(8,128)(2,1)S(1)} collective-permute-done((bf16[8,1664]{1,0:T(8,128)(2,1)S(1)}, bf16[8,1664]{1,0:T(8,128)(2,1)S(1)}, u32[]{:S(2)}, u32[]{:S(2)}) %collective-permute-start.15) | collective-permute-done | bytes 26656 | tf_op jit(solution)/shard_map/ppermute | solution.py:401
  30.5 3.7 %collective-permute-done.16 = bf16[8,1664]{1,0:T(8,128)(2,1)S(1)} collective-permute-done((bf16[8,1664]{1,0:T(8,128)(2,1)S(1)}, bf16[8,1664]{1,0:T(8,128)(2,1)S(1)}, u32[]{:S(2)}, u32[]{:S(2)}) %collective-permute-start.16) | collective-permute-done | bytes 26656 | tf_op jit(solution)/shard_map/ppermute | solution.py:401
  34.2 0.9 %shard_map.68 = bf16[16,1536]{1,0:T(8,128)(2,1)} custom-call(bf16[8,1664]{1,0:T(8,128)(2,1)S(1)} %add_add_fusion.1.mine_ref, bf16[8,1664]{1,0:T(8,128)(2,1)S(1)} %add_add_fusion.came_ref, bf16[16,4608]{1,0:T(8,128)(2,1)S(1)} %copy-done.2), custom_call_target="tpu_custom_call" | custom-call | tf_op jit(solution)/shard_map/pallas_call | solution.py:506
  (36 shorter events, 1.2 us)
Async XLA Ops:
  0.0 3.8 %copy-start.4 = (s32[1,16]{1,0:T(1,128)S(1)}, s32[1,16]{1,0:T(1,128)}, u32[]{:S(2)}) copy-start(s32[1,16]{1,0:T(1,128)} %parents_hbm_ref.1) | copy-start | bytes 196
  0.0 4.6 %copy-start = (bf16[16,8,3072]{2,1,0:T(8,128)(2,1)S(1)}, bf16[16,8,3072]{2,1,0:T(8,128)(2,1)}, u32[]{:S(2)}) copy-start(bf16[16,8,3072]{2,1,0:T(8,128)(2,1)} %param.6) | copy-start | bytes 2359300
  0.0 11.0 %copy-start.1 = (bf16[1,256,3072]{2,1,0:T(8,128)(2,1)S(1)}, bf16[1,256,3072]{2,1,0:T(8,128)(2,1)}, u32[]{:S(2)}) copy-start(bf16[1,256,3072]{2,1,0:T(8,128)(2,1)} %param.9) | copy-start | bytes 4718596
  0.0 11.0 %copy-start.3 = (bf16[16,1536]{1,0:T(8,128)(2,1)S(1)}, bf16[16,1536]{1,0:T(8,128)(2,1)}, u32[]{:S(2)}) copy-start(bf16[16,1536]{1,0:T(8,128)(2,1)} %query_ref) | copy-start | bytes 147460
  1.3 5.0 %collective-permute-start.1 = (bf16[8,1664]{1,0:T(8,128)(2,1)S(1)}, bf16[8,1664]{1,0:T(8,128)(2,1)S(1)}, u32[]{:S(2)}, u32[]{:S(2)}) collective-permute-start(bf16[8,1664]{1,0:T(8,128)(2,1)S(1)} %get-tuple-element.24), channel_id=1, source_target_pairs={{0,3},{1,2},{2,1},{3,0},{4,7},{5,6},{6,5},{7,4},{8,11},{9,10},{10,... | collective-permute-start | bytes 79880 | tf_op jit(solution)/shard_map/ppermute | solution.py:401
  3.8 2.4 %collective-permute-start = (s32[1,16]{1,0:T(1,128)S(1)}, s32[1,16]{1,0:T(1,128)S(1)}, u32[]{:S(2)}, u32[]{:S(2)}) collective-permute-start(s32[1,16]{1,0:T(1,128)S(1)} %copy-done.4), channel_id=1, source_target_pairs={{0,1},{1,0},{2,3},{3,2},{4,5},{5,4},{6,7},{7,6},{8,9},{9,8},{10,11... | collective-permute-start | bytes 200 | tf_op jit(solution)/shard_map/ppermute | solution.py:401
  4.5 10.0 %collective-permute-start.6 = (bf16[4,16,1536]{2,1,0:T(8,128)(2,1)S(1)}, bf16[4,16,1536]{2,1,0:T(8,128)(2,1)S(1)}, u32[]{:S(2)}, u32[]{:S(2)}) collective-permute-start(bf16[4,16,1536]{2,1,0:T(8,128)(2,1)S(1)} %get-tuple-element.29), channel_id=1, source_target_pairs={{0,3},{1,2},{2,1},{3,0},{4,7},{5,6},{6,5},{7,4},{8,11},{9,10},{10,... | collective-permute-start | bytes 589832 | tf_op jit(solution)/shard_map/ppermute | solution.py:401
  4.6 11.3 %collective-permute-start.5 = (bf16[4,2,16,3072]{3,2,1,0:T(8,128)(2,1)S(1)}, bf16[4,2,16,3072]{3,2,1,0:T(8,128)(2,1)S(1)}, u32[]{:S(2)}, u32[]{:S(2)}) collective-permute-start(bf16[4,2,16,3072]{3,2,1,0:T(8,128)(2,1)S(1)} %bitcast.7), channel_id=1, source_target_pairs={{0,1},{1,0},{2,3},{3,2},{4,5},{5,4},{6,7},{7,6},{8,9},{9,8},{10,11... | collective-permute-start | bytes 2359304 | tf_op jit(solution)/shard_map/ppermute | solution.py:401
  4.6 11.1 %collective-permute-start.9 = (bf16[4,16,1536]{2,1,0:T(8,128)(2,1)S(1)}, bf16[4,16,1536]{2,1,0:T(8,128)(2,1)S(1)}, u32[]{:S(2)}, u32[]{:S(2)}) collective-permute-start(bf16[4,16,1536]{2,1,0:T(8,128)(2,1)S(1)} %get-tuple-element.34), channel_id=1, source_target_pairs={{0,3},{1,2},{2,1},{3,0},{4,7},{5,6},{6,5},{7,4},{8,11},{9,10},{10,... | collective-permute-start | bytes 589832 | tf_op jit(solution)/shard_map/ppermute | solution.py:401
  6.4 5.2 %collective-permute-start.2 = (bf16[16,1664]{1,0:T(8,128)(2,1)S(1)}, bf16[16,1664]{1,0:T(8,128)(2,1)S(1)}, u32[]{:S(2)}, u32[]{:S(2)}) collective-permute-start(bf16[16,1664]{1,0:T(8,128)(2,1)S(1)} %pad_maximum_fusion.refs_0_), channel_id=1, source_target_pairs={{0,9},{1,8},{2,11},{3,10},{4,13},{5,12},{6,15},{7,14},{8,1},{9,0},... | collective-permute-start | bytes 159752 | tf_op jit(solution)/shard_map/ppermute | solution.py:401
  9.1 4.1 %collective-permute-start.3 = (bf16[16,1664]{1,0:T(8,128)(2,1)S(1)}, bf16[16,1664]{1,0:T(8,128)(2,1)S(1)}, u32[]{:S(2)}, u32[]{:S(2)}) collective-permute-start(bf16[16,1664]{1,0:T(8,128)(2,1)S(1)} %pad_maximum_fusion.refs_0_), channel_id=1, source_target_pairs={{0,5},{1,4},{2,7},{3,6},{4,1},{5,0},{6,3},{7,2},{8,13},{9,12},{10,... | collective-permute-start | bytes 159752 | tf_op jit(solution)/shard_map/ppermute | solution.py:401
  11.6 3.6 %collective-permute-start.4 = (bf16[16,1664]{1,0:T(8,128)(2,1)S(1)}, bf16[16,1664]{1,0:T(8,128)(2,1)S(1)}, u32[]{:S(2)}, u32[]{:S(2)}) collective-permute-start(bf16[16,1664]{1,0:T(8,128)(2,1)S(1)} %collective-permute-done.2.refs_1_), channel_id=1, source_target_pairs={{0,5},{1,4},{2,7},{3,6},{4,1},{5,0},{6,3},{7,2},{8,13},{9,12},{10,... | collective-permute-start | bytes 159752 | tf_op jit(solution)/shard_map/ppermute | solution.py:401
  13.2 1.2 %collective-permute-start.7 = (bf16[16,1536]{1,0:T(8,128)(2,1)S(1)}, bf16[16,1536]{1,0:T(8,128)(2,1)S(1)}, u32[]{:S(2)}, u32[]{:S(2)}) collective-permute-start(bf16[16,1536]{1,0:T(8,128)(2,1)S(1)} %shard_map.65.refs_6_), channel_id=1, source_target_pairs={{0,1},{1,0},{2,3},{3,2},{4,5},{5,4},{6,7},{7,6},{8,9},{9,8},{10,11... | collective-permute-start | bytes 147464 | tf_op jit(solution)/shard_map/ppermute | solution.py:401
  14.5 1.4 %collective-permute-start.8 = (bf16[64,1536]{1,0:T(8,128)(2,1)S(1)}, bf16[64,1536]{1,0:T(8,128)(2,1)S(1)}, u32[]{:S(2)}, u32[]{:S(2)}) collective-permute-start(bf16[64,1536]{1,0:T(8,128)(2,1)S(1)} %bitcast.13), channel_id=1, source_target_pairs={{0,1},{1,0},{2,3},{3,2},{4,5},{5,4},{6,7},{7,6},{8,9},{9,8},{10,11... | collective-permute-start | bytes 589832 | tf_op jit(solution)/shard_map/ppermute | solution.py:401
  15.7 1.5 %collective-permute-start.10 = (bf16[64,1536]{1,0:T(8,128)(2,1)S(1)}, bf16[64,1536]{1,0:T(8,128)(2,1)S(1)}, u32[]{:S(2)}, u32[]{:S(2)}) collective-permute-start(bf16[64,1536]{1,0:T(8,128)(2,1)S(1)} %bitcast.11), channel_id=1, source_target_pairs={{0,1},{1,0},{2,3},{3,2},{4,5},{5,4},{6,7},{7,6},{8,9},{9,8},{10,11... | collective-permute-start | bytes 589832 | tf_op jit(solution)/shard_map/ppermute | solution.py:401
  17.2 17.0 %copy-start.2 = (bf16[16,4608]{1,0:T(8,128)(2,1)S(1)}, bf16[16,4608]{1,0:T(8,128)(2,1)}, u32[]{:S(2)}) copy-start(bf16[16,4608]{1,0:T(8,128)(2,1)} %value_ref.1) | copy-start | bytes 442372
  17.6 3.8 %collective-permute-start.12 = (bf16[16,1664]{1,0:T(8,128)(2,1)S(1)}, bf16[16,1664]{1,0:T(8,128)(2,1)S(1)}, u32[]{:S(2)}, u32[]{:S(2)}) collective-permute-start(bf16[16,1664]{1,0:T(8,128)(2,1)S(1)} %get-tuple-element.39), channel_id=1, source_target_pairs={{0,5},{1,4},{2,7},{3,6},{4,1},{5,0},{6,3},{7,2},{8,13},{9,12},{10,... | collective-permute-start | bytes 159752 | tf_op jit(solution)/shard_map/ppermute | solution.py:401
  19.2 3.3 %collective-permute-start.11 = (bf16[8,1664]{1,0:T(8,128)(2,1)S(1)}, bf16[8,1664]{1,0:T(8,128)(2,1)S(1)}, u32[]{:S(2)}, u32[]{:S(2)}) collective-permute-start(bf16[8,1664]{1,0:T(8,128)(2,1)S(1)} %get-tuple-element.42), channel_id=1, source_target_pairs={{0,5},{1,4},{2,7},{3,6},{4,1},{5,0},{6,3},{7,2},{8,13},{9,12},{10,... | collective-permute-start | bytes 79880 | tf_op jit(solution)/shard_map/ppermute | solution.py:401
  19.5 3.3 %collective-permute-start.13 = (bf16[8,1664]{1,0:T(8,128)(2,1)S(1)}, bf16[8,1664]{1,0:T(8,128)(2,1)S(1)}, u32[]{:S(2)}, u32[]{:S(2)}) collective-permute-start(bf16[8,1664]{1,0:T(8,128)(2,1)S(1)} %slice.20), channel_id=1, source_target_pairs={{0,3},{1,2},{2,1},{3,0},{4,7},{5,6},{6,5},{7,4},{8,11},{9,10},{10,... | collective-permute-start | bytes 79880 | tf_op jit(solution)/shard_map/ppermute | solution.py:401
  22.7 5.6 %collective-permute-start.14 = (bf16[8,1664]{1,0:T(8,128)(2,1)S(1)}, bf16[8,1664]{1,0:T(8,128)(2,1)S(1)}, u32[]{:S(2)}, u32[]{:S(2)}) collective-permute-start(bf16[8,1664]{1,0:T(8,128)(2,1)S(1)} %get-tuple-element.44), channel_id=1, source_target_pairs={{0,9},{1,8},{2,11},{3,10},{4,13},{5,12},{6,15},{7,14},{8,1},{9,0},... | collective-permute-start | bytes 79880 | tf_op jit(solution)/shard_map/ppermute | solution.py:401
  25.8 4.7 %collective-permute-start.15 = (bf16[8,1664]{1,0:T(8,128)(2,1)S(1)}, bf16[8,1664]{1,0:T(8,128)(2,1)S(1)}, u32[]{:S(2)}, u32[]{:S(2)}) collective-permute-start(bf16[8,1664]{1,0:T(8,128)(2,1)S(1)} %get-tuple-element.41), channel_id=1, source_target_pairs={{0,6},{1,7},{2,4},{3,5},{4,2},{5,3},{6,0},{7,1},{8,14},{9,15},{10,... | collective-permute-start | bytes 79880 | tf_op jit(solution)/shard_map/ppermute | solution.py:401
  28.3 5.8 %collective-permute-start.16 = (bf16[8,1664]{1,0:T(8,128)(2,1)S(1)}, bf16[8,1664]{1,0:T(8,128)(2,1)S(1)}, u32[]{:S(2)}, u32[]{:S(2)}) collective-permute-start(bf16[8,1664]{1,0:T(8,128)(2,1)S(1)} %get-tuple-element.43), channel_id=1, source_target_pairs={{0,10},{1,11},{2,8},{3,9},{4,14},{5,15},{6,12},{7,13},{8,2},{9,3},... | collective-permute-start | bytes 79880 | tf_op jit(solution)/shard_map/ppermute | solution.py:401
